TPU v7x, 32 devices: a whole 2x2x4 slice. The times are simulated.
32 devices in a mesh: wide: 8 (over z, x), narrow: 4 (over y, core).
Axes of the slice: x: 2, y: 2, z: 4, core: 2. Of those that a mesh axis runs over, the one named last changes fastest.
Arguments:
- tokens: bfloat16 [17408, 384], P('wide'), may hold values from -6 to 6
- w_qkv: bfloat16 [384, 3, 384], replicated, may hold values from -0.3125 to 0.3125
- w_proj: bfloat16 [384, 384], replicated, may hold values from -1.25 to 1.25
- norm1_gain: float32 [384], replicated, may hold values from 0.25 to 1.75
- norm2_gain: float32 [384], replicated, may hold values from 0.25 to 1.75
- w_route: bfloat16 [384, 8], replicated, may hold values from -0.21875 to 0.21875
- w_in: bfloat16 [8, 384, 1536], P(None, None, 'narrow'), may hold values from -0.3125 to 0.3125
- w_out: bfloat16 [8, 1536, 384], P(None, 'narrow'), may hold values from -0.625 to 0.625
- cotangent: bfloat16 [17408, 384], P('wide'), may hold values from -6 to 6
- routes: int32 [17408, 1], P('wide'), may hold values from 0 to 7; in each aligned block of 2176 rows (0 to 2175, 2176 to 4351, ...) at most 408 rows name the same one
- kept_mask: int32 [17408], P('wide'), may hold values 0 or 1
- lengths: int32 [8, 8], P('wide'), may hold values from 1 to 1024, 2176 in all within a row
Outputs:
- layer_out: bfloat16 [17408, 384], P('wide')
- grad_tokens: bfloat16 [17408, 384], P('wide')
- grad_qkv: float32 [384, 3, 384], replicated
- grad_proj: float32 [384, 384], replicated
- grad_norm1: float32 [384], replicated
- grad_norm2: float32 [384], replicated
- grad_route: float32 [384, 8], replicated
- grad_in: float32 [8, 384, 1536], P(None, None, 'narrow')
- grad_out: float32 [8, 1536, 384], P(None, 'narrow')
Inputs may be any that keep to these rules, and one draw needn't show every extreme that they name: `routes`: in each aligned block of 2176 rows (the rows of one index of wide) no expert is named by more than 408 rows, a bound that some block reaches. `lengths`: each row sums to 2176, and its longest sequence has exactly 1024 tokens.
All inputs are finite; a program needn't handle non-finite values. No bound on the sum of `kept_mask` on one device may be relied on, other than what follows from the above.
Results may differ from a plain program's by a relative error of at most 0.019.
Values may be sent and summed in bfloat16 or wider, within the bound.
No kernel may reach another device: no remote copies, remote signals or barrier semaphores. Data moves between devices by JAX's collectives and lax.ppermute only.
A program may use at most 192 MiB of HBM per device.

v0:
```python
import math

import jax
import jax.numpy as jnp
from jax import lax
from jax.experimental import pallas as pl
from jax.experimental.pallas import tpu as pltpu
from jax.sharding import Mesh, PartitionSpec as P

HEADS = 6
CAP = 408
EPS = 1e-06
NEG = -1e30
F32 = jnp.float32
BF16 = jnp.bfloat16
LANES = 128
KB = 256
GRAIN = 16
STRIP = 32
FLOPS = 10**10
PARTS = (4, 2, 2)
GELU_A = math.sqrt(2.0 / math.pi)
GELU_B = 0.044715

ROWS_COLS = (((1,), (0,)), ((), ()))
COLS_COLS = (((1,), (1,)), ((), ()))
ROWS_ROWS = (((0,), (0,)), ((), ()))


def up(value, grain):
    return -(-value // grain) * grain


def mm(a, b, dims=ROWS_COLS):
    return lax.dot_general(a, b, dims, preferred_element_type=F32)


def normalize_rows(values):
    centre = values - jnp.mean(values, -1, keepdims=True)
    row_scale = lax.rsqrt(jnp.mean(centre * centre, -1, keepdims=True) + EPS)
    return centre * row_scale, row_scale


def normal_back(grad_h, normed, row_scale, gain_row):
    g = grad_h * gain_row
    return row_scale * (
        g - jnp.mean(g, -1, keepdims=True) - normed * jnp.mean(g * normed, -1, keepdims=True)
    )


def lane_head(h):
    return slice((h // 2) * LANES, (h // 2 + 1) * LANES)


def seq_ends(len_ref, count):
    ends = []
    total = jnp.int32(0)
    for j in range(count):
        total = total + len_ref[0, j]
        ends.append(total)
    return ends


def seq_bounds(ends, first_row, last_row):
    low = jnp.int32(0)
    high = ends[-1]
    for end in ends:
        low = jnp.where(end <= first_row, end, low)
    for end in reversed(ends):
        high = jnp.where(end > last_row, end, high)
    return low, high


def segment_of(index, ends):
    seg = jnp.zeros(index.shape, jnp.int32)
    for end in ends:
        seg = seg + (index >= end).astype(jnp.int32)
    return seg


def key_segments(segk_ref, ends, kpad):
    def body(i, carry):
        start = pl.multiple_of(i * LANES, LANES)
        index = lax.broadcasted_iota(jnp.int32, (LANES, LANES), 0) + start
        segk_ref[pl.ds(start, LANES), :] = segment_of(index, ends)
        return carry

    lax.fori_loop(0, kpad // LANES, body, 0)


def bias_block(segk_ref, kstart, segq):
    segk = segk_ref[pl.ds(kstart, KB), :]
    return jnp.where(jnp.concatenate([segk, segk], 1) == segq, 0.0, NEG)


def head_mask(rows, odd):
    lane = lax.broadcasted_iota(jnp.int32, (rows, LANES), 1)
    return ((lane >= 64) if odd else (lane < 64)).astype(BF16)


def plan_of(code_row, experts):
    n = code_row.shape[1]
    sub = lax.broadcasted_iota(jnp.int32, (experts, n), 0)
    lane = lax.broadcasted_iota(jnp.int32, (experts, n), 1)
    member = (code_row == sub).astype(F32)
    rank = member
    shift = 1
    while shift < n:
        rank = rank + jnp.where(lane >= shift, pltpu.roll(rank, shift, 1), 0.0)
        shift *= 2
    counts = jnp.broadcast_to(rank[:, n - 1 : n], (experts, LANES))
    sizes = jnp.floor((counts + (GRAIN - 1)) * (1.0 / GRAIN)) * GRAIN
    row = lax.broadcasted_iota(jnp.int32, (experts, LANES), 0)
    total = sizes
    shift = 1
    while shift < experts:
        total = total + jnp.where(row >= shift, pltpu.roll(total, shift, 0), 0.0)
        shift *= 2
    offsets = total - sizes
    pos = jnp.sum(member * (rank + offsets[:, 0:1]), 0, keepdims=True) - 1.0
    return pos, offsets, sizes


def key_steps(low, high):
    start = low // LANES * LANES
    return start, (high - start + KB - 1) // KB


def plan_kernel(where_ref, code_ref, plan_ref, pos_ref):
    experts = 8
    core = where_ref[0]
    pos, offsets, sizes = plan_of(code_ref[core], experts)
    unused, other_offsets, other_sizes = plan_of(code_ref[1 - core], experts)
    plan_ref[0:8, :] = offsets.astype(jnp.int32)
    plan_ref[8:16, :] = sizes.astype(jnp.int32)
    plan_ref[16:24, :] = other_offsets.astype(jnp.int32)
    plan_ref[24:32, :] = other_sizes.astype(jnp.int32)
    pos_ref[...] = jnp.broadcast_to(pos, pos_ref.shape)


def unpick_part(columns, part, half, cpad):
    lane = lax.broadcasted_iota(jnp.int32, (half, LANES), 1).astype(F32)
    column = strips(columns, part, half)
    return jnp.concatenate(
        [jnp.where(column == lane + float(j * LANES), 1.0, 0.0).astype(BF16) for j in range(cpad // LANES)], 1
    )


def unpick_kernel(pos_ref, unpick_ref):
    half, cpad = unpick_ref.shape[1:]
    columns = jnp.broadcast_to(pos_ref[0:1, :], (LANES, pos_ref.shape[1])).T
    for part in range(2):
        unpick_ref[part] = unpick_part(columns, part, half, cpad)


def run_unpick(pos, own, count, after):
    return call(
        unpick_kernel, sds((2, own // 2, up(count, LANES)), BF16), [], "unpick", 2, limit=12,
        in_specs=[VMEM_SPEC], after=after,
    )(pos)


def strips(value, part, half):
    return jnp.concatenate(
        [value[(2 * i + part) * STRIP : (2 * i + part + 1) * STRIP] for i in range(half // STRIP)], 0
    )


def strip_start(base, i, side):
    return pl.multiple_of(base + 2 * STRIP * i + STRIP * side, STRIP)


def in_strips(array):
    return array.reshape(-1, 2, STRIP, array.shape[-1])


def strip_copy(ref, first, side, dst, sem):
    return pltpu.make_async_copy(ref.at[pl.ds(first, dst.shape[0]), side], dst, sem)


def load_strips(ref, base, side, half):
    return jnp.concatenate([ref[pl.ds(strip_start(base, i, side), STRIP), :] for i in range(half // STRIP)], 0)


def front_kernel(
    len_ref, where_ref, tok_ref, w3_ref, wproj_ref, gain1_ref,
    hid_out, k_out, kt_out, v_out, q_out, ho_out, lse_out, keep_ref, send_ref,
    hid_ref, k_ref, kt_ref, v_ref, q_ref, ho_ref, lse_ref,
    vt_s, segk_s, qm_s, acc_s, m_s, l_s, s_s, st_s, sems,
):
    rows, width = tok_ref.shape
    own = rows // 2
    copies = [
        pltpu.make_async_copy(src, dst, sems.at[i])
        for i, (src, dst) in enumerate(
            (
                (hid_ref, hid_out), (k_ref, k_out), (kt_ref, kt_out), (v_ref, v_out), (q_ref, q_out),
                (ho_ref, ho_out), (lse_ref, lse_out),
            )
        )
    ]
    kpad = hid_ref.shape[0]
    qpad = q_ref.shape[0]
    mine = w3_ref.shape[2]
    heads = mine // 64
    core = where_ref[0]
    ends = seq_ends(len_ref, len_ref.shape[1])
    scale = 1.0 / math.sqrt(width // HEADS)
    key_segments(segk_s, ends, kpad)
    gain1 = gain1_ref[...]
    wq, wk, wv = w3_ref[0], w3_ref[1], w3_ref[2]
    step = rows // 4

    def norm_body(i, carry):
        at = pl.ds(pl.multiple_of(i * step, GRAIN), step)
        normed, unused = normalize_rows(tok_ref[at, :].astype(F32))
        hid = (normed * gain1).astype(BF16)
        hid_ref[at, :] = hid
        k_ref[at, 0:mine] = mm(hid, wk).astype(BF16)
        v_ref[at, 0:mine] = mm(hid, wv).astype(BF16)
        q_ref[at, 0:mine] = (mm(hid, wq).astype(BF16).astype(F32) * scale).astype(BF16)
        return carry

    lax.fori_loop(0, 4, norm_body, 0)
    hid_ref[rows:kpad, :] = jnp.zeros((kpad - rows, width), BF16)
    for ref in (k_ref, v_ref, q_ref):
        size = ref.shape[0]
        ref[rows:size, 0:mine] = jnp.zeros((size - rows, mine), BF16)
        ref[:, mine:] = jnp.zeros((size, ref.shape[1] - mine), BF16)
    wkt = wk.T
    wvt = wv.T

    def key_body(i, carry):
        at = pl.ds(pl.multiple_of(i * 2 * KB, 2 * KB), 2 * KB)
        hid = hid_ref[at, :]
        kt_ref[:, at] = mm(wkt, hid, COLS_COLS).astype(BF16)
        vt_s[:, at] = mm(wvt, hid, COLS_COLS).astype(BF16)
        return carry

    lax.fori_loop(0, kpad // (2 * KB), key_body, 0)
    for copy in copies[:5]:
        copy.start()
    st_s[...] = jnp.zeros(st_s.shape, F32)

    def q_step(qb, carry):
        first = pl.multiple_of(qb * KB, KB)
        last = jnp.minimum(first + KB, rows) - 1
        for h in range(heads):
            qm_s[h] = q_ref[pl.ds(first, KB), lane_head(h)] * head_mask(KB, h % 2)
        for h in range(heads):
            m_s[h : h + 1] = jnp.full((1, KB), NEG, F32)
            l_s[h : h + 1] = jnp.zeros((1, KB), F32)
        acc_s[...] = jnp.zeros(acc_s.shape, F32)
        low, high = seq_bounds(ends, first, last)
        start, steps = key_steps(low, high)
        segq = segment_of(lax.broadcasted_iota(jnp.int32, (8, KB), 1) + first, ends)[0:1]

        def scores(at):
            return [mm(k_ref[pl.ds(at, KB), lane_head(h)], qm_s[h], COLS_COLS) for h in range(heads)]

        for h, s in enumerate(scores(pl.multiple_of(start, LANES))):
            s_s[h] = s

        def k_step(kb, carry):
            at = pl.multiple_of(start + kb * KB, LANES)
            later = pl.multiple_of(start + jnp.minimum(kb + 1, steps - 1) * KB, LANES)
            bias = bias_block(segk_s, at, segq)
            now = [s_s[h] + bias for h in range(heads)]
            nexts = scores(later)
            m_old = [m_s[h : h + 1] for h in range(heads)]
            m_new = [jnp.maximum(m, jnp.max(s, 0, keepdims=True)) for m, s in zip(m_old, now)]
            p = [jnp.exp(s - m) for s, m in zip(now, m_new)]
            alpha = [jnp.exp(a - b) for a, b in zip(m_old, m_new)]
            for h in range(heads):
                m_s[h : h + 1] = m_new[h]
                l_s[h : h + 1] = l_s[h : h + 1] * alpha[h] + jnp.sum(p[h], 0, keepdims=True)
            out = [mm(vt_s[h * 64 : (h + 1) * 64, pl.ds(at, KB)], p[h].astype(BF16)) for h in range(heads)]
            for h in range(heads):
                acc_s[h * 64 : (h + 1) * 64] = acc_s[h * 64 : (h + 1) * 64] * alpha[h] + out[h]
                s_s[h] = nexts[h]
            return carry

        lax.fori_loop(0, steps, k_step, 0)
        parts = []
        for h in range(heads):
            total = l_s[h : h + 1]
            st_s[h : h + 1] = m_s[h : h + 1] + jnp.log(total)
            parts.append(acc_s[h * 64 : (h + 1) * 64] * (1.0 / total))
        lse_ref[pl.ds(first, KB), :] = st_s[...].T
        parts.append(jnp.zeros((ho_ref.shape[1] - mine, KB), F32))
        ho_ref[pl.ds(first, KB), :] = jnp.concatenate(parts, 0).T.astype(BF16)
        return carry

    lax.fori_loop(0, qpad // KB, q_step, 0)
    for copy in copies[5:]:
        copy.start()
    wproj = wproj_ref[pl.ds(pl.multiple_of(core * mine, GRAIN), mine), :]
    keep_ref[...] = mm(ho_ref[pl.ds(pl.multiple_of(core * own, GRAIN), own), 0:mine], wproj).astype(BF16)
    send_ref[...] = mm(ho_ref[pl.ds(pl.multiple_of((1 - core) * own, GRAIN), own), 0:mine], wproj).astype(BF16)
    for copy in copies:
        copy.wait()


def mid_kernel(
    where_ref, keep_ref, got_ref, tok_ref, cot_ref, gain2_ref, wr_ref, code_ref, pos_ref,
    mid_ref, sorted_ref, send_ref, x_s, tok_s, cot_s, mid_s, sems,
):
    own, width = keep_ref.shape
    npad = x_s.shape[0]
    core = where_ref[0]
    at = pl.ds(pl.multiple_of(core * own, GRAIN), own)
    tok_copy = pltpu.make_async_copy(tok_ref.at[at, :], tok_s, sems.at[0])
    cot_copy = pltpu.make_async_copy(cot_ref.at[at, :], cot_s, sems.at[1])
    tok_copy.start()
    cot_copy.start()
    tok_copy.wait()
    mid = tok_s[...].astype(F32) + (keep_ref[...].astype(F32) + got_ref[...].astype(F32))
    mid_s[...] = mid
    mid_copy = pltpu.make_async_copy(mid_s, mid_ref, sems.at[6])
    mid_copy.start()
    normed2, unused = normalize_rows(mid)
    hidden2 = (normed2 * gain2_ref[...]).astype(BF16)
    lane = lax.broadcasted_iota(jnp.int32, (own, LANES), 1)
    gates = router_gates(hidden2, wr_ref[...], lane, 8)
    code_col = jnp.broadcast_to(code_ref[core].astype(F32), (LANES, npad)).T[0:own]
    gate = jnp.sum(jnp.where(code_col == lane.astype(F32), gates, 0.0), -1, keepdims=True)
    x_s[0:own, 0:width] = hidden2
    cot_copy.wait()
    x_s[0:own, width:] = (gate * cot_s[...].astype(F32)).astype(BF16)
    x_s[own:npad, :] = jnp.zeros((npad - own, 2 * width), BF16)
    piece = sorted_ref.shape[0] // 4
    copies = []
    for i in range(4):
        rows = slice(i * piece, (i + 1) * piece)
        sub = lax.broadcasted_iota(jnp.int32, (piece, npad), 0) + i * piece
        pick = jnp.where(sub.astype(F32) == pos_ref[0:1, :], 1.0, 0.0).astype(BF16)
        sorted_ref[rows, :] = mm(pick, x_s[...]).astype(BF16)
        copies.append(pltpu.make_async_copy(sorted_ref.at[rows, :], send_ref.at[rows, :], sems.at[2 + i]))
        copies[-1].start()
    for copy in copies + [mid_copy]:
        copy.wait()


def router_gates(hidden2, wr, lane, experts):
    logits = jnp.where(lane < experts, mm(hidden2, wr), NEG)
    top = jnp.max(logits, -1, keepdims=True)
    e = jnp.exp(logits - top)
    return e / jnp.sum(e, -1, keepdims=True)


def call(kernel, outs, scratch, name, micros, in_specs, limit=24, after=None, **more):
    def out_of(shape, spec):
        if spec is VMEM_SPEC:
            return pltpu.VMEM(shape.shape, shape.dtype)
        return pltpu.HBM(shape.shape, shape.dtype) if is_far(spec) else shape

    out_specs = more.get("out_specs")
    if out_specs is None:
        out_specs = jax.tree.map(lambda o: VMEM_SPEC, outs)
    if isinstance(outs, tuple):
        outs = tuple(out_of(o, spec) for o, spec in zip(outs, out_specs))
    else:
        outs = out_of(outs, out_specs)
    more["out_specs"] = out_specs
    aliases = more.pop("input_output_aliases", {})
    body = kernel
    if after is not None:
        in_specs = [ANY_SPEC] + list(in_specs)
        aliases = {i + 1: o for i, o in aliases.items()}
        body = lambda after_ref, *refs: kernel(*refs)
    run = pl.pallas_call(
        body,
        out_shape=outs,
        in_specs=in_specs,
        scratch_shapes=scratch,
        name=name,
        input_output_aliases=aliases,
        compiler_params=pltpu.CompilerParams(vmem_limit_bytes=limit * 1024 * 1024),
        cost_estimate=pl.CostEstimate(flops=micros * FLOPS, bytes_accessed=10**4, transcendentals=0),
        **more,
    )

    def place(array, spec):
        if spec is VMEM_SPEC:
            return pltpu.with_memory_space_constraint(array, pltpu.VMEM)
        return pltpu.with_memory_space_constraint(array, pltpu.HBM) if is_far(spec) else array

    def run_on(*args):
        placed = [place(a, spec) for a, spec in zip(args, in_specs[len(in_specs) - len(args) :])]
        if after is not None:
            array, spec = after
            placed = [place(array, spec)] + placed
        return run(*placed)

    return run_on


def is_far(spec):
    return spec is FAR_SPEC or spec is FAR_ANY or spec.block_shape is not None


ANY_SPEC = pl.BlockSpec(memory_space=pl.ANY)
FAR_SPEC = pl.BlockSpec(memory_space=pltpu.VMEM)
FAR_ANY = pl.BlockSpec(memory_space=pl.ANY)
PLAIN_SPEC = pl.BlockSpec(memory_space=pltpu.VMEM)
SMEM_SPEC = pl.BlockSpec(memory_space=pltpu.SMEM)
VMEM_SPEC = pl.BlockSpec(memory_space=pltpu.VMEM)


def sds(shape, dtype):
    return jax.ShapeDtypeStruct(shape, dtype)


def run_plan(where, code, after=None):
    npad = code.shape[2]
    outs = (
        sds((32, LANES), jnp.int32),
        sds((8, npad), F32),
    )
    return call(plan_kernel, outs, [], "plan", 5, limit=12, in_specs=[SMEM_SPEC, VMEM_SPEC], after=after)(where, code)


def run_front(lengths, where, tokens, w3, wproj, gain1):
    rows, width = tokens.shape
    own = rows // 2
    mine = w3.shape[2]
    heads = mine // 64
    kpad = up(rows + KB, 2 * KB)
    qpad = up(rows, KB)
    lanes = up(mine, LANES)
    outs = (
        sds((kpad, width), BF16),
        sds((kpad, lanes), BF16),
        sds((mine, kpad), BF16),
        sds((kpad, lanes), BF16),
        sds((qpad, lanes), BF16),
        sds((qpad, lanes), BF16),
        sds((qpad, LANES), F32),
        sds((own, width), BF16),
        sds((own, width), BF16),
    )
    scratch = [pltpu.VMEM(o.shape, o.dtype) for o in outs[:7]] + [
        pltpu.VMEM((mine, kpad), BF16),
        pltpu.VMEM((kpad, LANES), jnp.int32),
        pltpu.VMEM((heads, KB, LANES), BF16),
        pltpu.VMEM((mine, KB), F32),
        pltpu.VMEM((8, KB), F32),
        pltpu.VMEM((8, KB), F32),
        pltpu.VMEM((heads, KB, KB), F32),
        pltpu.VMEM((LANES, KB), F32),
        pltpu.SemaphoreType.DMA((7,)),
    ]
    return call(
        front_kernel, outs, scratch, "front", 33, in_specs=[SMEM_SPEC, SMEM_SPEC] + [VMEM_SPEC] * 4, limit=32,
        out_specs=(FAR_ANY,) * 7 + (PLAIN_SPEC,) * 2,
    )(lengths, where, tokens, w3, wproj, gain1)


def run_mid(where, keep, got, tokens, cot, gain2, wr, code, pos):
    own, width = keep.shape
    count = up(own + 8 * (GRAIN - 1), 4 * GRAIN)
    outs = (sds((own, width), F32),) + (sds((count, 2 * width), BF16),) * 2
    scratch = [
        pltpu.VMEM((code.shape[2], 2 * width), BF16),
        pltpu.VMEM((own, width), BF16),
        pltpu.VMEM((own, width), BF16),
        pltpu.VMEM((own, width), F32),
        pltpu.SemaphoreType.DMA((7,)),
    ]
    return call(
        mid_kernel, outs, scratch, "mid", 9, limit=20,
        in_specs=[SMEM_SPEC, PLAIN_SPEC, PLAIN_SPEC, FAR_ANY, FAR_ANY] + [VMEM_SPEC] * 4,
        out_specs=(FAR_ANY, VMEM_SPEC, ANY_SPEC),
    )(where, keep, got, tokens, cot, gain2, wr, code, pos)


def expert_kernel(
    plan_ref, where_ref, own_ref, oth_ref, win_ref, wout_ref, wr_ref,
    yown_ref, yoth_ref, groute_ref, *refs,
):
    *grads, x_s, y_s = refs
    e = pl.program_id(0)
    width = win_ref.shape[1]
    most = x_s.shape[0]

    @pl.when(e == 0)
    def _():
        yown_ref[...] = jnp.zeros(yown_ref.shape, BF16)
        yoth_ref[...] = jnp.zeros(yoth_ref.shape, BF16)
        groute_ref[...] = jnp.zeros(groute_ref.shape, F32)

    own_at, own_size = plan_ref[e, 0], plan_ref[8 + e, 0]
    oth_at, oth_size = plan_ref[16 + e, 0], plan_ref[24 + e, 0]
    total = own_size + oth_size

    def move(dst, dst_at, src, src_at, size):
        def body(i, carry):
            a = pl.multiple_of(dst_at + i * GRAIN, GRAIN)
            b = pl.multiple_of(src_at + i * GRAIN, GRAIN)
            dst[pl.ds(a, GRAIN), :] = src[pl.ds(b, GRAIN), :]
            return carry

        lax.fori_loop(0, size // GRAIN, body, 0)

    move(x_s, 0, own_ref, own_at, own_size)
    move(x_s, own_size, oth_ref, oth_at, oth_size)

    def work(m):
        def zero_body(i, carry):
            x_s[pl.ds(pl.multiple_of(i * GRAIN, GRAIN), GRAIN), :] = jnp.zeros((GRAIN, 2 * width), BF16)
            return carry

        lax.fori_loop(total // GRAIN, m // GRAIN, zero_body, 0)
        h = x_s[0:m, 0:width]
        g = x_s[0:m, width:]
        w_in = win_ref[0]
        w_out = wout_ref[0]
        lane = lax.broadcasted_iota(jnp.int32, (m, LANES), 1)
        gates = router_gates(h, wr_ref[...], lane, 8)
        here = (lane == e).astype(F32)
        pre = mm(h, w_in)
        t = jnp.tanh(GELU_A * (pre + GELU_B * (pre * pre * pre)))
        act = (0.5 * pre * (1.0 + t)).astype(BF16)
        slope = 0.5 * (1.0 + t) + 0.5 * pre * (1.0 - t * t) * (GELU_A * (1.0 + 3.0 * GELU_B * (pre * pre)))
        out = mm(act, w_out)
        grad_pre = (mm(g, w_out, COLS_COLS) * slope).astype(BF16)
        dot = jnp.sum(g.astype(F32) * out, -1, keepdims=True)
        grad_logits = (dot * (here - gates)).astype(BF16)
        gate = jnp.sum(gates * here, -1, keepdims=True)
        y_s[0:m, 0:width] = (mm(grad_pre, w_in, COLS_COLS) + mm(grad_logits, wr_ref[...], COLS_COLS)).astype(BF16)
        y_s[0:m, width:] = (gate * out).astype(BF16)
        ht = h.T
        groute_ref[...] += mm(ht, grad_logits)
        grad_in = mm(ht, grad_pre).astype(BF16)
        grad_out = mm(act.T, g).astype(BF16)

        at = 0
        for i, size in enumerate(PARTS):
            here = (e >= at) & (e < at + size)
            if i == 0:
                put_both(grads[0], grad_in, grad_out, here)
            else:
                put(grads[2 * i - 1 : 2 * i + 1], grad_in, grad_out, here)
            at += size

    def put_both(ref, grad_in, grad_out, here):
        @pl.when(here)
        def _():
            ref[0, 0] = grad_in
            ref[0, 1] = grad_out

    def put(pair, grad_in, grad_out, here):
        keep_ref, send_ref = pair

        @pl.when(here & (where_ref[2] == 0))
        def _():
            keep_ref[0] = grad_in
            send_ref[0] = grad_out

        @pl.when(here & (where_ref[2] != 0))
        def _():
            keep_ref[0] = grad_out
            send_ref[0] = grad_in

    small = up(CAP * 2 // 3, GRAIN)

    @pl.when(total <= small)
    def _():
        work(small)

    @pl.when(total > small)
    def _():
        work(most)

    move(yown_ref, own_at, y_s, 0, own_size)
    move(yoth_ref, oth_at, y_s, own_size, oth_size)


def run_experts(plan, where, own, oth, w_in, w_out, wr):
    experts, width, hidden = w_in.shape
    count = own.shape[0]
    most = (CAP + 2 * (GRAIN - 1)) // GRAIN * GRAIN
    outs = [sds((count, 2 * width), BF16)] * 2 + [sds((width, LANES), F32)]
    out_specs = [VMEM_SPEC, PLAIN_SPEC, VMEM_SPEC]

    def part(at, size, tail):
        return pl.BlockSpec((1,) + tail, lambda e: (jnp.clip(e - at, 0, size - 1),) + (0,) * len(tail))

    at = 0
    for i, size in enumerate(PARTS):
        tail = (2, width, hidden) if i == 0 else (width, hidden)
        copies = 1 if i == 0 else 2
        outs += [sds((size,) + tail, BF16)] * copies
        out_specs += [part(at, size, tail)] * copies
        at += size
    return call(
        expert_kernel,
        tuple(outs),
        [pltpu.VMEM((most, 2 * width), BF16), pltpu.VMEM((most, 2 * width), BF16)],
        "experts",
        22, limit=28,
        grid=(experts,),
        in_specs=[
            SMEM_SPEC,
            SMEM_SPEC,
            VMEM_SPEC,
            PLAIN_SPEC,
            pl.BlockSpec((1, width, hidden), lambda e: (e, 0, 0)),
            pl.BlockSpec((1, hidden, width), lambda e: (e, 0, 0)),
            VMEM_SPEC,
        ],
        out_specs=tuple(out_specs),
    )(plan, where, own, oth, w_in, w_out, wr)


def unsort_kernel(where_ref, mine_ref, got_ref, unpick_ref, keep_ref, send_ref, y_s):
    count = mine_ref.shape[0]
    cpad, width = y_s.shape
    y_s[0:count, :] = (mine_ref[:, 0:width].astype(F32) + got_ref[:, 0:width].astype(F32)).astype(BF16)
    if cpad > count:
        y_s[count:cpad, :] = jnp.zeros((cpad - count, width), BF16)
    side = where_ref[1]
    send_ref[...] = mm(unpick_ref[1 - side], y_s[...]).astype(BF16)
    keep_ref[...] = mm(unpick_ref[side], y_s[...]).astype(BF16)


def run_unsort(where, mine, got, unpick):
    width = mine.shape[1] // 2
    half, cpad = unpick.shape[1:]
    outs = (sds((half, width), BF16), sds((half, width), BF16))
    return call(
        unsort_kernel, outs, [pltpu.VMEM((cpad, width), BF16)], "unsort", 4, limit=12,
        in_specs=[SMEM_SPEC, VMEM_SPEC, PLAIN_SPEC, VMEM_SPEC], out_specs=(VMEM_SPEC, PLAIN_SPEC),
    )(where, mine, got, unpick)


def unsort_out_kernel(mine_ref, got_ref, pos_ref, ex_ref, y_s):
    count = mine_ref.shape[0]
    half = ex_ref.shape[0] // 2
    columns = jnp.broadcast_to(pos_ref[0:1, :], (LANES, pos_ref.shape[1])).T
    cpad, width = y_s.shape
    y_s[0:count, :] = (mine_ref[:, width:].astype(F32) + got_ref[:, width:].astype(F32)).astype(BF16)
    if cpad > count:
        y_s[count:cpad, :] = jnp.zeros((cpad - count, width), BF16)
    for part in range(2):
        rows = mm(unpick_part(columns, part, half, cpad), y_s[...]).astype(BF16)
        for i in range(half // STRIP):
            at = (2 * i + part) * STRIP
            ex_ref[at : at + STRIP, :] = rows[i * STRIP : (i + 1) * STRIP]


def run_unsort_out(mine, got, pos, own, after):
    count, width = mine.shape[0], mine.shape[1] // 2
    cpad = up(count, LANES)
    return call(
        unsort_out_kernel, sds((own, width), BF16), [pltpu.VMEM((cpad, width), BF16)], "unsort_out", 3, limit=12,
        in_specs=[VMEM_SPEC, PLAIN_SPEC, VMEM_SPEC], out_specs=PLAIN_SPEC, after=after,
    )(mine, got, pos)


def out_kernel(mid_ref, mine_ref, got_ref, out_ref):
    out_ref[...] = (mid_ref[...] + (mine_ref[...].astype(F32) + got_ref[...].astype(F32))).astype(BF16)


def run_out(mid, mine, got, after):
    return call(
        out_kernel, sds(mid.shape, BF16), [], "block_out", 2, limit=12,
        in_specs=[FAR_SPEC, PLAIN_SPEC, PLAIN_SPEC], out_specs=PLAIN_SPEC, after=after,
    )(mid, mine, got)


def join_kernel(where_ref, mine_ref, other_ref, out_ref, sems):
    own = mine_ref.shape[0]
    core = where_ref[0]
    copies = [
        pltpu.make_async_copy(ref, out_ref.at[pl.ds(pl.multiple_of(place * own, GRAIN), own), :], sems.at[i])
        for i, (ref, place) in enumerate(((mine_ref, core), (other_ref, 1 - core)))
    ]
    for copy in copies:
        copy.start()
    for copy in copies:
        copy.wait()


def run_join(where, mine, other, after):
    own, width = mine.shape
    return call(
        join_kernel, sds((2 * own, width), BF16), [pltpu.SemaphoreType.DMA((2,))], "join", 2, limit=4,
        in_specs=[SMEM_SPEC, PLAIN_SPEC, PLAIN_SPEC], out_specs=FAR_ANY, after=after,
    )(where, mine, other)


def mid_back_kernel(where_ref, keep_ref, got_ref, mid_ref, cot_ref, gain2_ref, gmid_ref, ga_ref, part_ref, cot_s, mid_s, sems):
    half = keep_ref.shape[0]
    core, side = where_ref[0], where_ref[1]
    mid_copy = strip_copy(mid_ref, 0, side, mid_s, sems.at[0])
    mid_copy.start()
    copy = strip_copy(cot_ref, core * (half // STRIP), side, cot_s, sems.at[1])
    copy.start()
    grad_h2 = keep_ref[...].astype(F32) + got_ref[...].astype(F32)
    mid_copy.wait()
    normed2, scale2 = normalize_rows(mid_s[...].reshape(half, -1))
    part_ref[...] = jnp.broadcast_to(jnp.sum(grad_h2 * normed2, 0, keepdims=True), part_ref.shape)
    copy.wait()
    grad_final = cot_s[...].reshape(half, -1).astype(F32)
    grad_mid = grad_final + normal_back(grad_h2, normed2, scale2, gain2_ref[...])
    gmid_ref[...] = grad_mid
    ga_ref[...] = grad_mid.astype(BF16)


def run_mid_back(where, keep, got, mid, cot, gain2):
    half, width = keep.shape
    outs = (sds((half, width), F32), sds((half, width), BF16), sds((8, width), F32))
    return call(
        mid_back_kernel, outs, [pltpu.VMEM((half // STRIP, STRIP, width), dtype) for dtype in (BF16, F32)] + [pltpu.SemaphoreType.DMA((2,))],
        "mid_back", 4, limit=12,
        in_specs=[SMEM_SPEC, VMEM_SPEC, PLAIN_SPEC, FAR_ANY, FAR_ANY, VMEM_SPEC],
        out_specs=(FAR_SPEC, PLAIN_SPEC, VMEM_SPEC),
    )(where, keep, got, in_strips(mid), in_strips(cot), gain2)


def back_kernel(
    len_ref, where_ref, ga_ref, gao_ref, ho_any, q_any, lse_any, k_any, kt_any, v_any, hid_any, w3_ref, wproj_ref,
    hkeep_ref, hsend_ref, dqt_ref, dkt_ref, dvt_ref, ga_s, hid_s, ho_s,
    segk_s, qm_s, dm_s, dq_s, dk_s, dv_s, q_s, do_s, lse_s, d_s, gh_s, col_s,
    k_ref, v_ref, kt_ref, hoc_s, lsec_s, qc_s, hidc_s, sems,
):
    half, width = ga_ref.shape
    rows = 4 * half
    own = 2 * half
    kpad = k_ref.shape[0]
    cpad = ga_s.shape[0]
    mine = w3_ref.shape[2]
    heads = mine // 64
    core, side = where_ref[0], where_ref[1]
    ends = seq_ends(len_ref, len_ref.shape[1])
    scale = 1.0 / math.sqrt(width // HEADS)

    strips_of = (hoc_s, lsec_s, qc_s, hidc_s)
    copies = [
        strip_copy(ref, 0, side, dst, sems.at[i])
        for i, (ref, dst) in enumerate(zip((ho_any, lse_any, q_any, hid_any), strips_of))
    ] + [
        pltpu.make_async_copy(ref, dst, sems.at[4 + i])
        for i, (ref, dst) in enumerate(((k_any, k_ref), (v_any, v_ref), (kt_any, kt_ref)))
    ]
    for copy in copies:
        copy.start()
    key_segments(segk_s, ends, kpad)
    at = pl.multiple_of(core * half, GRAIN)
    ga_s[pl.ds(at, half), :] = ga_ref[...]
    at = pl.multiple_of((1 - core) * half, GRAIN)
    ga_s[pl.ds(at, half), :] = gao_ref[...]
    ga_s[own:cpad, :] = jnp.zeros((cpad - own, width), BF16)
    dk_s[...] = jnp.zeros(dk_s.shape, F32)
    dv_s[...] = jnp.zeros(dv_s.shape, F32)
    for copy in copies:
        copy.wait()
    for src, dst in zip(strips_of, (ho_s, col_s, q_s, hid_s)):
        dst[0:own, :] = src[0 : own // STRIP].reshape(own, -1)
        dst[own:cpad, :] = jnp.zeros((cpad - own, dst.shape[1]), dst.dtype)
    lse_s[...] = col_s[...].T[0:8]
    wproj = wproj_ref[pl.ds(pl.multiple_of(core * mine, GRAIN), mine), :]
    do_s[:, 0:mine] = mm(ga_s[...], wproj, COLS_COLS).astype(BF16)
    do_s[:, mine:] = jnp.zeros((cpad, do_s.shape[1] - mine), BF16)
    sub = lax.broadcasted_iota(jnp.int32, (8, do_s.shape[1]), 0)
    lane = lax.broadcasted_iota(jnp.int32, (8, do_s.shape[1]), 1)
    d_s[...] = lax.dot_general(
        (lane // 64 == sub).astype(F32),
        do_s[...].astype(F32) * ho_s[...].astype(F32),
        COLS_COLS,
        precision=lax.Precision.HIGHEST,
        preferred_element_type=F32,
    )

    def place(index):
        return 2 * STRIP * (index // STRIP) + STRIP * side + index % STRIP

    def q_step(qb, carry):
        first = pl.multiple_of(qb * KB, KB)
        last = jnp.minimum(first + KB, own) - 1
        for h in range(heads):
            mask = head_mask(KB, h % 2)
            qm_s[h] = q_s[pl.ds(first, KB), lane_head(h)] * mask
            dm_s[h] = do_s[pl.ds(first, KB), lane_head(h)] * mask
        dq_s[:, pl.ds(first, KB)] = jnp.zeros((mine, KB), F32)
        low, high = seq_bounds(ends, place(first), place(last))
        start, steps = key_steps(low, high)
        index = lax.broadcasted_iota(jnp.int32, (8, KB), 1) + first
        segq = jnp.where(index < own, segment_of(place(index), ends), -1)[0:1]
        lse = [lse_s[h : h + 1, pl.ds(first, KB)] for h in range(heads)]
        dots = [d_s[h : h + 1, pl.ds(first, KB)] for h in range(heads)]

        def k_step(kb, carry):
            at = pl.multiple_of(start + kb * KB, LANES)
            bias = bias_block(segk_s, at, segq)
            s = [mm(k_ref[pl.ds(at, KB), lane_head(h)], qm_s[h], COLS_COLS) for h in range(heads)]
            dp = [mm(v_ref[pl.ds(at, KB), lane_head(h)], dm_s[h], COLS_COLS) for h in range(heads)]
            p = [jnp.exp((s[h] + bias) - lse[h]) for h in range(heads)]
            ds = [(p[h] * (dp[h] - dots[h])).astype(BF16) for h in range(heads)]
            p = [a.astype(BF16) for a in p]
            dv = [mm(p[h], dm_s[h]) for h in range(heads)]
            dk = [mm(ds[h], qm_s[h]) for h in range(heads)]
            dq = [mm(kt_ref[h * 64 : (h + 1) * 64, pl.ds(at, KB)], ds[h]) for h in range(heads)]
            for ref, add in ((dv_s, dv), (dk_s, dk)):
                for j in range(up(heads, 2) // 2):
                    pair = add[2 * j : 2 * j + 2]
                    ref[pl.ds(at, KB), j * LANES : (j + 1) * LANES] += pair[0] if len(pair) == 1 else pair[0] + pair[1]
            for h in range(heads):
                dq_s[h * 64 : (h + 1) * 64, pl.ds(first, KB)] += dq[h]
            return carry

        lax.fori_loop(0, steps, k_step, 0)
        return carry

    lax.fori_loop(0, cpad // KB, q_step, 0)

    wq, wk, wv = w3_ref[0], w3_ref[1], w3_ref[2]
    dqt = (dq_s[...] * scale).astype(BF16)
    dqt_ref[...] = dqt
    step = rows // 8

    def h_body(i, carry):
        at = pl.ds(pl.multiple_of(i * step, GRAIN), step)
        gh_s[at, :] = mm(dk_s[at, 0:mine].astype(BF16), wk, COLS_COLS) + mm(
            dv_s[at, 0:mine].astype(BF16), wv, COLS_COLS
        )
        return carry

    lax.fori_loop(0, 8, h_body, 0)
    dkt_ref[...] = dk_s[...].astype(BF16).T[0:mine]
    dvt_ref[...] = dv_s[...].astype(BF16).T[0:mine]
    grad_q = mm(dqt.T, wq, COLS_COLS)
    for i in range(own // STRIP):
        at = pl.ds(strip_start(0, i, side), STRIP)
        gh_s[at, :] += grad_q[i * STRIP : (i + 1) * STRIP]
    hkeep_ref[...] = gh_s[pl.ds(pl.multiple_of(core * own, GRAIN), own), :].astype(BF16)
    hsend_ref[...] = gh_s[pl.ds(pl.multiple_of((1 - core) * own, GRAIN), own), :].astype(BF16)

def weight_kernel(
    dqt_ref, dkt_ref, dvt_ref, ga_ref, hidc_ref, hoc_ref, hid_any, groute_ref, gain2_ref, pay_ref, hid_ref, sem
):
    mine = dqt_ref.shape[0]
    width = ga_ref.shape[1]
    copy = pltpu.make_async_copy(hid_any, hid_ref, sem)
    copy.start()
    pay_ref[0:mine, :] = mm(dqt_ref[...], hidc_ref[...]).astype(BF16)
    pay_ref[3 * mine : 4 * mine, :] = mm(hoc_ref[...].T[0:mine], ga_ref[...]).astype(BF16)
    copy.wait()
    pay_ref[mine : 2 * mine, :] = mm(dkt_ref[...], hid_ref[...]).astype(BF16)
    pay_ref[2 * mine : 3 * mine, :] = mm(dvt_ref[...], hid_ref[...]).astype(BF16)
    pay_ref[4 * mine : 4 * mine + 8, :] = groute_ref[...].T[0:8].astype(BF16)
    pay_ref[4 * mine + 8 : 4 * mine + 16, :] = gain2_ref[...].astype(BF16)
    pay_ref[4 * mine + 16 :, :] = jnp.zeros((pay_ref.shape[0] - 4 * mine - 16, width), BF16)


def run_weights(pay_rows, dqt, dkt, dvt, ga, hidc, hoc, hid, groute, gain2, after):
    return call(
        weight_kernel, sds((pay_rows, ga.shape[1]), BF16),
        [pltpu.VMEM(hid.shape, BF16), pltpu.SemaphoreType.DMA], "weights", 4, limit=16,
        in_specs=[VMEM_SPEC] * 6 + [FAR_ANY] + [VMEM_SPEC] * 2, out_specs=PLAIN_SPEC, after=after,
    )(dqt, dkt, dvt, ga, hidc, hoc, hid, groute, gain2)


def run_back(lengths, where, ga, gao, ho, q, lse, k, kt, v, hid, w3, wproj, after):
    half, width = ga.shape
    own = 2 * half
    kpad, lanes = k.shape
    mine = w3.shape[2]
    heads = mine // 64
    cpad = up(own, KB)
    outs = (
        sds((own, width), BF16),
        sds((own, width), BF16),
        sds((mine, cpad), BF16),
        sds((mine, kpad), BF16),
        sds((mine, kpad), BF16),
        sds((cpad, width), BF16),
        sds((cpad, width), BF16),
        sds((cpad, lanes), BF16),
    )
    scratch = [
        pltpu.VMEM((kpad, LANES), jnp.int32),
        pltpu.VMEM((heads, KB, LANES), BF16),
        pltpu.VMEM((heads, KB, LANES), BF16),
        pltpu.VMEM((mine, cpad), F32),
        pltpu.VMEM((kpad, lanes), F32),
        pltpu.VMEM((kpad, lanes), F32),
        pltpu.VMEM((cpad, lanes), BF16),
        pltpu.VMEM((cpad, lanes), BF16),
        pltpu.VMEM((8, cpad), F32),
        pltpu.VMEM((8, cpad), F32),
        pltpu.VMEM((4 * half, width), F32),
        pltpu.VMEM((cpad, LANES), F32),
        pltpu.VMEM((kpad, lanes), BF16),
        pltpu.VMEM((kpad, lanes), BF16),
        pltpu.VMEM((mine, kpad), BF16),
        pltpu.VMEM((own // STRIP, STRIP, lanes), BF16),
        pltpu.VMEM((own // STRIP, STRIP, LANES), F32),
        pltpu.VMEM((own // STRIP, STRIP, lanes), BF16),
        pltpu.VMEM((own // STRIP, STRIP, width), BF16),
        pltpu.SemaphoreType.DMA((7,)),
    ]
    return call(
        back_kernel, outs, scratch, "back", 28,
        in_specs=[SMEM_SPEC, SMEM_SPEC, PLAIN_SPEC, PLAIN_SPEC] + [FAR_ANY] * 7 + [VMEM_SPEC] * 2,
        out_specs=(FAR_SPEC, PLAIN_SPEC) + (VMEM_SPEC,) * 6, limit=32, after=after,
    )(lengths, where, ga, gao, in_strips(ho), in_strips(q), in_strips(lse), k, kt, v, in_strips(hid), w3, wproj)


def token_kernel(where_ref, mine_ref, got_ref, gmid_ref, tok_ref, gain1_ref, out_ref, tok_s, sem):
    half = gmid_ref.shape[0]
    copy = strip_copy(tok_ref, where_ref[0] * (half // STRIP), where_ref[1], tok_s, sem)
    copy.start()
    grad_h1 = mine_ref[...].astype(F32) + got_ref[...].astype(F32)
    copy.wait()
    normed1, scale1 = normalize_rows(tok_s[...].reshape(half, -1).astype(F32))
    out_ref[...] = (gmid_ref[...] + normal_back(grad_h1, normed1, scale1, gain1_ref[...])).astype(BF16)


def run_tokens(where, mine, got, gmid, tokens, gain1, after):
    return call(
        token_kernel, sds(gmid.shape, BF16),
        [pltpu.VMEM((gmid.shape[0] // STRIP, STRIP, gmid.shape[1]), BF16), pltpu.SemaphoreType.DMA], "token_grad", 3, limit=12,
        in_specs=[SMEM_SPEC, FAR_SPEC, PLAIN_SPEC, FAR_SPEC, FAR_ANY, VMEM_SPEC], out_specs=PLAIN_SPEC, after=after,
    )(where, mine, got, gmid, in_strips(tokens), gain1)


def split_kernel(where_ref, a_ref, b_ref, keep_ref, send_ref):
    half = keep_ref.shape[0]
    total = (a_ref[...].astype(F32) + b_ref[...].astype(F32)).astype(BF16)
    side = where_ref[1]
    first, second = strips(total, 0, half), strips(total, 1, half)
    keep_ref[...] = jnp.where(side == 0, first, second)
    send_ref[...] = jnp.where(side == 0, second, first)


def run_split(where, a, b, after):
    own, width = a.shape
    outs = (sds((own // 2, width), BF16),) * 2
    return call(
        split_kernel, outs, [], "split", 2, limit=12, in_specs=[SMEM_SPEC, FAR_SPEC, PLAIN_SPEC],
        out_specs=(FAR_SPEC, PLAIN_SPEC), after=after,
    )(where, a, b)


def weave_kernel(where_ref, mine_ref, other_ref, out_ref):
    side = where_ref[1]
    for i in range(mine_ref.shape[0] // STRIP):
        rows = slice(i * STRIP, (i + 1) * STRIP)
        out_ref[pl.ds(strip_start(0, i, side), STRIP), :] = mine_ref[rows, :]
        out_ref[pl.ds(strip_start(0, i, 1 - side), STRIP), :] = other_ref[rows, :]


def run_weave(where, mine, other, after):
    half, width = mine.shape
    return call(
        weave_kernel, sds((2 * half, width), BF16), [], "weave", 2, limit=8,
        in_specs=[SMEM_SPEC] + [PLAIN_SPEC] * 2, out_specs=PLAIN_SPEC, after=after,
    )(where, mine, other)


def summed_end_kernel(total_ref, gin_ref, gout_ref):
    gin_ref[0] = total_ref[0, 0].astype(F32)
    gout_ref[0] = total_ref[0, 1].astype(F32)


def run_summed_end(total, shape_in, shape_out, after):
    size, unused, width, hidden = total.shape
    block = pl.BlockSpec((1, width, hidden), lambda e: (e, 0, 0))
    return call(
        summed_end_kernel,
        (sds(shape_in, F32), sds(shape_out, F32)),
        [],
        "summed_end",
        4, limit=12,
        grid=(size,),
        in_specs=[pl.BlockSpec((1, 2, width, hidden), lambda e: (e, 0, 0, 0))],
        out_specs=(block, block),
        after=after,
    )(total)


def expert_end_kernel(where_ref, mine_ref, other_ref, *refs):
    gin_ref, gout_ref = refs[-2:]
    e = pl.program_id(0)
    mine = mine_ref[e].astype(F32)
    other = other_ref[e].astype(F32)
    first = where_ref[2] == 0
    gin_ref[0] = jnp.where(first, mine, other)
    gout_ref[0] = jnp.where(first, other, mine)


def run_expert_end(at, where, mine, other, shape_in, shape_out, before):
    size, width, hidden = mine.shape
    block = pl.BlockSpec((1, width, hidden), lambda e: (e + at, 0, 0))
    return call(
        expert_end_kernel,
        (sds(shape_in, F32), sds(shape_out, F32)),
        [],
        "expert_end",
        3, limit=12,
        grid=(size,),
        in_specs=[SMEM_SPEC, PLAIN_SPEC, PLAIN_SPEC] + [FAR_ANY] * 2,
        out_specs=(block, block),
        input_output_aliases={3: 0, 4: 1},
    )(where, mine, other, *before)


def total_kernel(parts_ref, out_ref):
    pieces = parts_ref.shape[0]
    total = parts_ref[0].astype(F32)
    for i in range(1, pieces):
        total = total + parts_ref[i].astype(F32)
    total = total.astype(BF16)
    for i in range(pieces):
        out_ref[i] = total


def run_total(parts, after):
    return call(
        total_kernel, sds(parts.shape, BF16), [], "total", 2, limit=8, in_specs=[PLAIN_SPEC], out_specs=PLAIN_SPEC, after=after
    )(parts)


def attn_end_kernel(where_ref, mine_ref, other_ref, wqkv_ref, gain1_ref, gqkv_ref, gproj_ref, g1_ref, g2_ref, groute_ref):
    width = wqkv_ref.shape[1]
    share = width // 2
    first = where_ref[0] == 0
    mine = mine_ref[...].astype(F32)
    other = other_ref[...].astype(F32)
    low = jnp.where(first, mine, other)
    high = jnp.where(first, other, mine)
    product = jnp.zeros((width, width), F32)
    for i in range(3):
        rows = slice(i * share, (i + 1) * share)
        part = jnp.concatenate([low[rows], high[rows]], 0).T
        gqkv_ref[:, i, :] = part
        product = product + part * wqkv_ref[i].astype(F32)
    gproj_ref[...] = jnp.concatenate([low[3 * share : 4 * share], high[3 * share : 4 * share]], 0)
    g1_ref[...] = jnp.sum(product.T, 0, keepdims=True) / gain1_ref[...]
    small = low[4 * share : 4 * share + 16] + high[4 * share : 4 * share + 16]
    groute_ref[...] = small[0:8]
    g2_ref[...] = small[8:9]


def run_attn_end(where, mine, other, wqkv, gain1, after):
    width = wqkv.shape[1]
    outs = (
        sds((width, 3, width), F32),
        sds((width, width), F32),
        sds((1, width), F32),
        sds((1, width), F32),
        sds((8, width), F32),
    )
    return call(
        attn_end_kernel, outs, [], "attn_end", 4, limit=16, in_specs=[SMEM_SPEC, PLAIN_SPEC, PLAIN_SPEC, VMEM_SPEC, VMEM_SPEC],
        out_specs=(FAR_SPEC,) * 5, after=after,
    )(where, mine, other, wqkv, gain1)


def swap(value, axis, mask):
    size = lax.axis_size(axis)
    return lax.ppermute(value, axis, [(i, i ^ mask) for i in range(size)])


def add_kernel(a_ref, b_ref, out_ref):
    out_ref[...] = (a_ref[...].astype(F32) + b_ref[...].astype(F32)).astype(BF16)


def added(a, b, after):
    return call(
        add_kernel, sds(a.shape, BF16), [], "add", 2, limit=8, in_specs=[PLAIN_SPEC] * 2, out_specs=PLAIN_SPEC, after=after
    )(a, b)


def choose_kernel(where_ref, inner_ref, outer_ref, out_ref):
    @pl.when(where_ref[3] == 0)
    def _():
        out_ref[...] = inner_ref[...]

    @pl.when(where_ref[3] != 0)
    def _():
        out_ref[...] = outer_ref[...]


def chosen(where, inner, outer, after):
    return call(
        choose_kernel, sds(inner.shape, BF16), [], "choose", 2, limit=8,
        in_specs=[SMEM_SPEC, PLAIN_SPEC, PLAIN_SPEC], out_specs=PLAIN_SPEC, after=after,
    )(where, inner, outer)


def wide_step(value, step):
    inward = [(w, w + 2) for w in (0, 1)] + [(w, w - 2) for w in (6, 7)]
    if step == 0:
        return lax.ppermute(value, "wide", inward)
    if step == 1:
        return lax.ppermute(value, "wide", [(2, 4), (3, 5), (4, 2), (5, 3)])
    return lax.ppermute(value, "wide", [(b, a) for a, b in inward])


def on_device(
    tokens, w_qkv, w_proj, norm1_gain, norm2_gain, w_route, w_in, w_out, cotangent, routes, kept_mask, lengths
):
    rows, width = tokens.shape
    own, half = rows // 2, rows // 4
    experts = w_in.shape[0]
    core, side = lax.axis_index("lo"), lax.axis_index("hi")
    wide_size, w = lax.axis_size("wide"), lax.axis_index("wide")
    z = w // 2
    outer = ((z == 0) | (z == wide_size // 2 - 1)).astype(jnp.int32)
    where = jnp.stack([core, side, w % 2, outer]).astype(jnp.int32)

    wqkv = w_qkv.transpose(1, 0, 2)
    w3 = lax.dynamic_slice_in_dim(wqkv, core * (width // 2), width // 2, 2)
    wr = jnp.pad(w_route, ((0, 0), (0, LANES - experts)))
    gain1 = norm1_gain.reshape(1, width)
    gain2 = norm2_gain.reshape(1, width)
    code = jnp.where(kept_mask == 1, routes[:, 0], experts).reshape(2, 1, own)
    code = jnp.pad(code, ((0, 0), (0, 0), (0, up(own, LANES) - own)), constant_values=experts)

    hid, k, kt, v, q, ho, lse, keep, send = run_front(lengths, where, tokens, w3, w_proj, gain1)
    got = swap(send, "lo", 1)
    plan, pos = run_plan(where, code, (keep, ANY_SPEC))
    mid, own_x, own_send = run_mid(where, keep, got, tokens, cotangent, gain2, wr, code, pos)
    oth_x = swap(own_send, "lo", 1)

    yown, yoth, groute, grads_a, *pairs = run_experts(plan, where, own_x, oth_x, w_in, w_out, wr)
    got = swap(yoth, "lo", 1)
    total_a = lax.psum(grads_a, "wide")
    pairs = [(pairs[2 * i], pairs[2 * i + 1]) for i in range(len(pairs) // 2)]
    recvs = [swap(give, "wide", 1) for unused, give in pairs]

    unpick = run_unpick(pos, own, own_x.shape[0], (yoth, ANY_SPEC))
    keep, send = run_unsort(where, yown, got, unpick)
    gh2 = swap(send, "hi", 1)
    gmid, ga, gain2_part = run_mid_back(where, keep, gh2, mid, cotangent, gain2)
    gao = swap(ga, "lo", 1)
    ex = run_unsort_out(yown, got, pos, own, (ga, ANY_SPEC))
    ex_got = swap(ex, "hi", 1)

    hkeep, hsend, dqt, dkt, dvt, ga_c, hid_c, ho_c = run_back(
        lengths, where, ga, gao, ho, q, lse, k, kt, v, hid, w3, w_proj, (ex, ANY_SPEC)
    )
    hgot = swap(hsend, "lo", 1)
    last = hsend, ANY_SPEC
    line = wide_size == 8
    sums = []
    for (mine, unused), recv in zip(pairs, recvs):
        mine = added(mine, recv, last)
        if not line:
            for i in range(1, wide_size.bit_length() - 1):
                mine = added(mine, swap(mine, "wide", 1 << i), last)
        last = mine, ANY_SPEC
        sums.append(mine)
    moved = [wide_step(a, 0) for a in sums] if line else sums
    pay_rows = up(2 * width + 16, 8 * lax.axis_size(("wide", "hi")))
    pay = run_weights(pay_rows, dqt, dkt, dvt, ga_c, hid_c, ho_c, hid, groute, gain2_part, last)
    count = pay_rows // lax.axis_size(("wide", "hi"))
    pay_got = lax.all_to_all(pay.reshape(-1, count, width), ("wide", "hi"), 0, 0)
    hk, hs = run_split(where, hkeep, hgot, (pay, ANY_SPEC))
    hs_got = swap(hs, "hi", 1)
    last = hs, ANY_SPEC
    if line:
        for i in range(len(sums)):
            sums[i] = added(sums[i], moved[i], last)
            last = sums[i], ANY_SPEC
            moved[i] = wide_step(sums[i], 1)
    mine = run_out(mid, ex, ex_got, last)
    other = swap(mine, "lo", 1)
    pay_got = run_total(pay_got, (mine, ANY_SPEC))
    last = pay_got, ANY_SPEC
    pay_got = lax.all_to_all(pay_got, ("wide", "hi"), 0, 0).reshape(pay.shape)
    token_rows = run_tokens(where, hk, hs_got, gmid, tokens, gain1, last)
    last = token_rows, ANY_SPEC
    token_got = swap(token_rows, "hi", 1)
    layer_out = run_join(where, mine, other, last)
    last = layer_out, FAR_ANY
    if line:
        for i in range(len(sums)):
            sums[i] = added(sums[i], moved[i], last)
            last = sums[i], ANY_SPEC
            moved[i] = wide_step(sums[i], 2)
    token_own = run_weave(where, token_rows, token_got, last)
    last = token_own, ANY_SPEC
    token_oth = swap(token_own, "lo", 1)
    if line:
        for i in range(len(sums)):
            sums[i] = chosen(where, sums[i], moved[i], last)
            last = sums[i], ANY_SPEC
    others = [swap(a, "wide", 1) for a in sums]
    pay_oth = swap(pay_got, "lo", 1)
    grad_tokens = run_join(where, token_own, token_oth, last)
    last = grad_tokens, FAR_ANY
    grad_qkv, grad_proj, grad_norm1, grad_norm2, route_t = run_attn_end(where, pay_got, pay_oth, wqkv, gain1, last)
    before = run_summed_end(total_a, w_in.shape, w_out.shape, (grad_proj, FAR_ANY))
    at = PARTS[0]
    for mine, other, size in zip(sums, others, PARTS[1:]):
        before = run_expert_end(at, where, mine, other, w_in.shape, w_out.shape, before)
        at += size
    grad_in, grad_out = before

    return (
        layer_out,
        grad_tokens,
        grad_qkv,
        grad_proj,
        grad_norm1.reshape(width),
        grad_norm2.reshape(width),
        route_t.T,
        grad_in,
        grad_out,
    )


def solution(mesh):
    axes = ("wide", ("hi", "lo"))
    split = Mesh(mesh.devices.reshape(mesh.shape["wide"], -1, 2), ("wide", "hi", "lo"))
    wide, narrow = axes
    in_specs = (
        P(wide, None),
        P(),
        P(),
        P(),
        P(),
        P(),
        P(None, None, narrow),
        P(None, narrow, None),
        P(wide, None),
        P(wide, None),
        P(wide),
        P(wide, None),
    )
    out_specs = (
        P(wide, None),
        P(wide, None),
        P(),
        P(),
        P(),
        P(),
        P(),
        P(None, None, narrow),
        P(None, narrow, None),
    )
    return jax.shard_map(on_device, mesh=split, in_specs=in_specs, out_specs=out_specs, check_vma=False)
```

profile of v0, /device:TPU:0, one launch (start us, length us, event | category | flops | bytes accessed | tf_op | source)
XLA Modules:
  0.0 273.4 jit_solution(15701044552467944974)
XLA Ops:
  12.7 28.9 %front.1 = (bf16[2560,384]{1,0:T(8,128)(2,1)}, bf16[2560,256]{1,0:T(8,128)(2,1)}, bf16[192,2560]{1,0:T(8,128)(2,1)}, bf16[2560,256]{1,0:T(8,128)(2,1)}, bf16[230...) custom-call(s32[1,8]{1,0:T(1,128)S(1)} %copy-done.12, ...), custom_call_target="tpu_custom_call" | custom-call | flops 330000007168 | bytes 10000 | tf_op jit(solution)/shard_map/front/pallas_call | solution.py:393
  44.0 8.2 %mid.1 = (f32[1088,384]{1,0:T(8,128)}, bf16[1216,768]{1,0:T(8,128)(2,1)S(1)}, bf16[1216,768]{1,0:T(8,128)(2,1)S(1)}) custom-call(s32[4]{0:T(128)S(1)} %pad_add_fusion.where_ref.refs_0_.refs_1_, bf16[1088,384]{1,0:T(8,128)(2,1)S(1)} %get-tuple-element.57.after_ref.keep_ref, bf16[1088,384]{1,0:T(8,128)(2,1)S(1)} %collective-permute-done.got_ref, ...), custom_call_target="tpu_custom_call" | custom-call | flops 89999998976 | bytes 10000 | tf_op jit(solution)/shard_map/mid/pallas_call | solution.py:393
  52.7 3.5 %collective-permute-done.1.oth_ref = bf16[1216,768]{1,0:T(8,128)(2,1)S(1)} collective-permute-done((bf16[1216,768]{1,0:T(8,128)(2,1)S(1)}, bf16[1216,768]{1,0:T(8,128)(2,1)S(1)}, u32[]{:S(2)}, u32[]{:S(2)}) %collective-permute-start.1) | collective-permute-done | bytes 1867808 | tf_op jit(solution)/shard_map/ppermute | solution.py:1064
  56.2 19.8 %experts.1 = (bf16[1216,768]{1,0:T(8,128)(2,1)S(1)}, bf16[1216,768]{1,0:T(8,128)(2,1)S(1)}, f32[384,128]{1,0:T(8,128)S(1)}, bf16[4,2,384,384]{3,2,1,0:T(8,128)(2...) custom-call(s32[32,128]{1,0:T(8,128)S(1)} %get-tuple-element.58.plan, ...), custom_call_target="tpu_custom_call" | custom-call | flops 219999993856 | bytes 10000 | tf_op jit(solution)/shard_map/experts/pallas_call | solution.py:393
  76.9 2.9 %collective-permute-done.2.got_ref.refs_1_ = bf16[1216,768]{1,0:T(8,128)(2,1)S(1)} collective-permute-done((bf16[1216,768]{1,0:T(8,128)(2,1)S(1)}, bf16[1216,768]{1,0:T(8,128)(2,1)S(1)}, u32[]{:S(2)}, u32[]{:S(2)}) %collective-permute-start.2) | collective-permute-done | bytes 1867808 | tf_op jit(solution)/shard_map/ppermute | solution.py:1064
  79.9 2.2 unsort.1
  82.1 3.0 %collective-permute-start.3 = (bf16[544,384]{1,0:T(8,128)(2,1)S(1)}, bf16[544,384]{1,0:T(8,128)(2,1)S(1)}, u32[]{:S(2)}, u32[]{:S(2)}) collective-permute-start(bf16[544,384]{1,0:T(8,128)(2,1)S(1)} %get-tuple-element.66), channel_id=1, source_target_pairs={{0,2},{2,0},{1,3},{3,1},{4,6},{6,4},{5,7},{7,5},{8,10},{10,8},{9,1... | collective-permute-start | bytes 1253384 | tf_op jit(solution)/shard_map/ppermute | solution.py:1064
  87.2 7.9 %collective-permute-done.3.got_ref = bf16[544,384]{1,0:T(8,128)(2,1)S(1)} collective-permute-done((bf16[544,384]{1,0:T(8,128)(2,1)S(1)}, bf16[544,384]{1,0:T(8,128)(2,1)S(1)}, u32[]{:S(2)}, u32[]{:S(2)}) %collective-permute-start.3) | collective-permute-done | bytes 417824 | tf_op jit(solution)/shard_map/ppermute | solution.py:1064
  95.1 3.3 %mid_back.1 = (f32[544,384]{1,0:T(8,128)}, bf16[544,384]{1,0:T(8,128)(2,1)S(1)}, f32[8,384]{1,0:T(8,128)S(1)}) custom-call(s32[4]{0:T(128)S(1)} %pad_add_fusion.where_ref.refs_0_.refs_1_, bf16[544,384]{1,0:T(8,128)(2,1)S(1)} %get-tuple-element.65.keep_ref, bf16[544,384]{1,0:T(8,128)(2,1)S(1)} %collective-permute-done.3.got_ref, f32[17,2,32,384]{3,2,1,0:T(8,128)} %bitcast.21, ...), custom_call_target="tpu_custom_call" | custom-call | flops 40000000000 | bytes 10000 | tf_op jit(solution)/shard_map/mid_back/pallas_call | solution.py:393
  98.5 2.7 unsort_out.1.after_ref.refs_1_
  101.2 1.7 collective-permute-start.10
  103.0 27.3 %back.1 = (bf16[1088,384]{1,0:T(8,128)(2,1)}, bf16[1088,384]{1,0:T(8,128)(2,1)S(1)}, bf16[192,1280]{1,0:T(8,128)(2,1)S(1)}, bf16[192,2560]{1,0:T(8,128)(2,1)S(1)...) custom-call(bf16[1088,384]{1,0:T(8,128)(2,1)} %unsort_out.1.after_re, ...), custom_call_target="tpu_custom_call" | custom-call | flops 280000004096 | bytes 10000 | tf_op jit(solution)/shard_map/back/pallas_call | solution.py:393
  133.2 2.0 add.33.after_ref.refs_0_
  135.2 2.1 collective-permute-start.9
  137.4 4.1 %weights.1.after_ref = bf16[896,384]{1,0:T(8,128)(2,1)} custom-call(bf16[2,384,384]{2,1,0:T(8,128)(2,1)} %add.33.after_ref.refs_0_, bf16[192,1280]{1,0:T(8,128)(2,1)S(1)} %get-tuple-element.81.refs_0_, bf16[192,2560]{1,0:T(8,128)(2,1)S(1)} %get-tuple-element.82.refs_1_, bf16[192,2560]{1,0:T(8,128)(2,1)S(1)} %get-tuple-element.83.refs_2_, ...), custom_call_target="tpu_custom_call" | custom-call | flops 40000000000 | bytes 10000 | tf_op jit(solution)/shard_map/weights/pallas_call | solution.py:393
  141.5 5.4 %all-to-all-start = ((bf16[16,56,384]{2,1,0:T(8,128)(2,1)}), bf16[16,56,384]{2,1,0:T(8,128)(2,1)S(1)}, u32[]{:S(2)}, u32[]{:S(2)}) async-start(bf16[16,56,384]{2,1,0:T(8,128)(2,1)} %bitcast.11), calls=%async_computation | async-start | bytes 1376256 | tf_op jit(solution)/shard_map/all_to_all | solution.py:1161
  146.9 2.3 split.1
  149.2 1.9 collective-permute-start.11
  154.7 15.3 %collective-permute-done.9.refs_1_ = bf16[2,384,384]{2,1,0:T(8,128)(2,1)} collective-permute-done((bf16[2,384,384]{2,1,0:T(8,128)(2,1)}, bf16[2,384,384]{2,1,0:T(8,128)(2,1)}, u32[]{:S(2)}, u32[]{:S(2)}) %collective-permute-start.9) | collective-permute-done | bytes 589856 | tf_op jit(solution)/shard_map/ppermute | solution.py:1097
  172.9 2.4 block_out.1.after_ref.refs_1_
  175.5 14.2 %all-to-all-done.refs_0_ = bf16[16,56,384]{2,1,0:T(8,128)(2,1)S(1)} async-done(((bf16[16,56,384]{2,1,0:T(8,128)(2,1)}), bf16[16,56,384]{2,1,0:T(8,128)(2,1)S(1)}, u32[]{:S(2)}, u32[]{:S(2)}) %all-to-all-start) | async-done | bytes 688160 | tf_op jit(solution)/shard_map/all_to_all | solution.py:1161
  190.6 5.9 %all-to-all-start.1 = ((bf16[16,56,384]{2,1,0:T(8,128)(2,1)}), bf16[16,56,384]{2,1,0:T(8,128)(2,1)}, u32[]{:S(2)}, u32[]{:S(2)}) async-start(bf16[16,56,384]{2,1,0:T(8,128)(2,1)} %total.1.after_ref), calls=%async_computation.1 | async-start | bytes 1376256 | tf_op jit(solution)/shard_map/all_to_all | solution.py:1174
  196.5 2.9 %token_grad.1.after_ref.refs_1_ = bf16[544,384]{1,0:T(8,128)(2,1)S(1)} custom-call(bf16[16,56,384]{2,1,0:T(8,128)(2,1)} %total.1.after_ref, s32[4]{0:T(128)S(1)} %pad_add_fusion.where_ref.refs_0_.refs_1_, bf16[544,384]{1,0:T(8,128)(2,1)} %get-tuple-element.91.refs_1_, bf16[544,384]{1,0:T(8,128)(2,1)} %collective-permute-done.11.refs_2_, ...), custom_call_target="tpu_custom_call" | custom-call | flops 30000001024 | bytes 10000 | tf_op jit(solution)/shard_map/token_grad/pallas_call | solution.py:393
  199.5 1.9 collective-permute-start.15
  208.2 5.6 %collective-permute-done.15.refs_2_ = bf16[544,384]{1,0:T(8,128)(2,1)S(1)} collective-permute-done((bf16[544,384]{1,0:T(8,128)(2,1)S(1)}, bf16[544,384]{1,0:T(8,128)(2,1)S(1)}, u32[]{:S(2)}, u32[]{:S(2)}) %collective-permute-start.15) | collective-permute-done | bytes 417824 | tf_op jit(solution)/shard_map/ppermute | solution.py:1064
  214.6 14.4 %collective-permute-done.16.refs_2_ = bf16[2,384,384]{2,1,0:T(8,128)(2,1)S(1)} collective-permute-done((bf16[2,384,384]{2,1,0:T(8,128)(2,1)S(1)}, bf16[2,384,384]{2,1,0:T(8,128)(2,1)S(1)}, u32[]{:S(2)}, u32[]{:S(2)}) %collective-permute-start.16) | collective-permute-done | bytes 589856 | tf_op jit(solution)/shard_map/ppermute | solution.py:1100
  231.1 16.5 %collective-permute-done.17.refs_2_ = bf16[2,384,384]{2,1,0:T(8,128)(2,1)S(1)} collective-permute-done((bf16[2,384,384]{2,1,0:T(8,128)(2,1)S(1)}, bf16[2,384,384]{2,1,0:T(8,128)(2,1)S(1)}, u32[]{:S(2)}, u32[]{:S(2)}) %collective-permute-start.17) | collective-permute-done | bytes 589856 | tf_op jit(solution)/shard_map/ppermute | solution.py:1100
  249.1 1.7 join.3.after_ref
  251.5 3.5 %attn_end.1 = (f32[384,3,384]{2,1,0:T(4,128)}, f32[384,384]{1,0:T(8,128)}, f32[1,384]{1,0:T(1,128)}, f32[1,384]{1,0:T(1,128)}, f32[8,384]{1,0:T(8,128)}) custom-call(bf16[2176,384]{1,0:T(8,128)(2,1)} %join.3.after_ref, s32[4]{0:T(128)S(1)} %pad_add_fusion.where_ref.refs_0_.refs_1_, bf16[896,384]{1,0:T(8,128)(2,1)} %bitcast.13.refs_1_, ...), custom_call_target="tpu_custom_call" | custom-call | flops 40000000000 | bytes 10000 | tf_op jit(solution)/shard_map/attn_end/pallas_call | solution.py:393
  255.0 4.3 %summed_end.1 = (f32[8,384,384]{2,1,0:T(8,128)}, f32[8,384,384]{2,1,0:T(8,128)}) custom-call(f32[384,384]{1,0:T(8,128)} %get-tuple-element.108.after_ref, bf16[4,2,384,384]{3,2,1,0:T(8,128)(2,1)} %all-reduce.4.cloned.1.call-done.refs_0_), custom_call_target="tpu_custom_call" | custom-call | flops 40000000000 | bytes 10000 | tf_op jit(solution)/shard_map/summed_end/pallas_call | solution.py:393
  259.3 2.7 %expert_end.2 = (f32[8,384,384]{2,1,0:T(8,128)}, f32[8,384,384]{2,1,0:T(8,128)}) custom-call(s32[4]{0:T(128)S(1)} %pad_add_fusion.where_ref.refs_0_.refs_1_, bf16[2,384,384]{2,1,0:T(8,128)(2,1)S(1)} %choose.2.after_ref.mine_ref, bf16[2,384,384]{2,1,0:T(8,128)(2,1)} %collective-permute-done.21.other_ref, ...), custom_call_target="tpu_custom_call", output_to_operand_aliasing={{0}: (3, {}), {1}: (4, {})} | custom-call | flops 30000001024 | bytes 10000 | tf_op jit(solution)/shard_map/expert_end/pallas_call | solution.py:393
  264.6 2.0 expert_end.3
  (115 shorter events, 35.9 us)
Async XLA Ops:
  7.2 247.8 %all-reduce.4.cloned.1.call-start = ((), (), s32[]{:S(2)}) async-start(), calls=%async_computation.2 | async-start | bytes 4718592 | tf_op jit(solution)/shard_map/psum | solution.py:1131
  7.9 33.7 %copy-start.3 = (f32[1,384]{1,0:T(1,128)}, f32[1,384]{1,0:T(1,128)S(1)}, u32[]{:S(2)}) copy-start(f32[1,384]{1,0:T(1,128)S(1)} %reshape.60.gain1_ref.refs_5_.refs_4_) | copy-start | bytes 4612
  9.4 32.2 %copy-start = (bf16[3,384,192]{2,1,0:T(8,128)(2,1)}, bf16[3,384,192]{2,1,0:T(8,128)(2,1)S(1)}, u32[]{:S(2)}) copy-start(bf16[3,384,192]{2,1,0:T(8,128)(2,1)S(1)} %dynamic-slice_bitcast_fusion.w3_ref.refs_11_) | copy-start | bytes 1327108
  12.6 29.4 %copy-start.22 = (s32[2176,1]{0,1:T(1,128)S(1)}, s32[2176,1]{0,1:T(1,128)}, u32[]{:S(2)}) copy-start(s32[2176,1]{0,1:T(1,128)} %param.21) | copy-start | bytes 26116
  12.6 29.4 %copy-start.21 = (s32[2176]{0:T(1024)S(1)}, s32[2176]{0:T(1024)}, u32[]{:S(2)}) copy-start(s32[2176]{0:T(1024)} %param.22) | copy-start | bytes 26116
  41.6 2.4 collective-permute-start
  43.5 32.9 %copy-start.18 = (f32[8,1152]{1,0:T(8,128)}, f32[8,1152]{1,0:T(8,128)S(1)}, u32[]{:S(2)}) copy-start(f32[8,1152]{1,0:T(8,128)S(1)} %get-tuple-element.60.pos_ref.refs_0_.refs_2_) | copy-start | bytes 110596
  52.3 3.9 %collective-permute-start.1 = (bf16[1216,768]{1,0:T(8,128)(2,1)S(1)}, bf16[1216,768]{1,0:T(8,128)(2,1)S(1)}, u32[]{:S(2)}, u32[]{:S(2)}) collective-permute-start(bf16[1216,768]{1,0:T(8,128)(2,1)S(1)} %get-tuple-element.62), channel_id=1, source_target_pairs={{0,1},{1,0},{2,3},{3,2},{4,5},{5,4},{6,7},{7,6},{8,9},{9,8},{10,11... | collective-permute-start | bytes 5603336 | tf_op jit(solution)/shard_map/ppermute | solution.py:1064
  76.0 3.9 %collective-permute-start.2 = (bf16[1216,768]{1,0:T(8,128)(2,1)S(1)}, bf16[1216,768]{1,0:T(8,128)(2,1)S(1)}, u32[]{:S(2)}, u32[]{:S(2)}) collective-permute-start(bf16[1216,768]{1,0:T(8,128)(2,1)S(1)} %get-tuple-element.64.after_ref), channel_id=1, source_target_pairs={{0,1},{1,0},{2,3},{3,2},{4,5},{5,4},{6,7},{7,6},{8,9},{9,8},{10,11... | collective-permute-start | bytes 5603336 | tf_op jit(solution)/shard_map/ppermute | solution.py:1064
  82.1 13.0 %collective-permute-start.3 = (bf16[544,384]{1,0:T(8,128)(2,1)S(1)}, bf16[544,384]{1,0:T(8,128)(2,1)S(1)}, u32[]{:S(2)}, u32[]{:S(2)}) collective-permute-start(bf16[544,384]{1,0:T(8,128)(2,1)S(1)} %get-tuple-element.66), channel_id=1, source_target_pairs={{0,2},{2,0},{1,3},{3,1},{4,6},{6,4},{5,7},{7,5},{8,10},{10,8},{9,1... | collective-permute-start | bytes 1253384 | tf_op jit(solution)/shard_map/ppermute | solution.py:1064
  85.1 45.4 %collective-permute-start.5 = (bf16[2,384,384]{2,1,0:T(8,128)(2,1)}, bf16[2,384,384]{2,1,0:T(8,128)(2,1)}, u32[]{:S(2)}, u32[]{:S(2)}) collective-permute-start(bf16[2,384,384]{2,1,0:T(8,128)(2,1)} %get-tuple-element.78), channel_id=1, source_target_pairs={{0,4},{4,0},{8,12},{12,8},{16,20},{20,16},{24,28},{28,24},{1,5},{5... | collective-permute-start | bytes 1769480 | tf_op jit(solution)/shard_map/ppermute | solution.py:1064
  86.3 46.9 %collective-permute-start.6 = (bf16[2,384,384]{2,1,0:T(8,128)(2,1)}, bf16[2,384,384]{2,1,0:T(8,128)(2,1)}, u32[]{:S(2)}, u32[]{:S(2)}) collective-permute-start(bf16[2,384,384]{2,1,0:T(8,128)(2,1)} %get-tuple-element.80), channel_id=1, source_target_pairs={{0,4},{4,0},{8,12},{12,8},{16,20},{20,16},{24,28},{28,24},{1,5},{5... | collective-permute-start | bytes 1769480 | tf_op jit(solution)/shard_map/ppermute | solution.py:1064
  98.4 4.5 %collective-permute-start.4 = (bf16[544,384]{1,0:T(8,128)(2,1)S(1)}, bf16[544,384]{1,0:T(8,128)(2,1)S(1)}, u32[]{:S(2)}, u32[]{:S(2)}) collective-permute-start(bf16[544,384]{1,0:T(8,128)(2,1)S(1)} %get-tuple-element.68.after_ref.refs_2_), channel_id=1, source_target_pairs={{0,1},{1,0},{2,3},{3,2},{4,5},{5,4},{6,7},{7,6},{8,9},{9,8},{10,11... | collective-permute-start | bytes 1253384 | tf_op jit(solution)/shard_map/ppermute | solution.py:1064
  101.2 71.7 %collective-permute-start.10 = (bf16[1088,384]{1,0:T(8,128)(2,1)}, bf16[1088,384]{1,0:T(8,128)(2,1)}, u32[]{:S(2)}, u32[]{:S(2)}) collective-permute-start(bf16[1088,384]{1,0:T(8,128)(2,1)} %unsort_out.1.after_ref.refs_1_), channel_id=1, source_target_pairs={{0,2},{2,0},{1,3},{3,1},{4,6},{6,4},{5,7},{7,5},{8,10},{10,8},{9,1... | collective-permute-start | bytes 2506760 | tf_op jit(solution)/shard_map/ppermute | solution.py:1064
  103.0 27.6 %copy-start.16 = (bf16[2,384,384]{2,1,0:T(8,128)(2,1)S(1)}, bf16[2,384,384]{2,1,0:T(8,128)(2,1)}, u32[]{:S(2)}) copy-start(bf16[2,384,384]{2,1,0:T(8,128)(2,1)} %get-tuple-element.77.refs_0_) | copy-start | bytes 1769476
  130.3 16.6 %collective-permute-start.7 = (bf16[1088,384]{1,0:T(8,128)(2,1)S(1)}, bf16[1088,384]{1,0:T(8,128)(2,1)S(1)}, u32[]{:S(2)}, u32[]{:S(2)}) collective-permute-start(bf16[1088,384]{1,0:T(8,128)(2,1)S(1)} %get-tuple-element.76.after_ref), channel_id=1, source_target_pairs={{0,1},{1,0},{2,3},{3,2},{4,5},{5,4},{6,7},{7,6},{8,9},{9,8},{10,11... | collective-permute-start | bytes 2506760 | tf_op jit(solution)/shard_map/ppermute | solution.py:1064
  131.9 19.3 %collective-permute-start.8 = (bf16[2,384,384]{2,1,0:T(8,128)(2,1)S(1)}, bf16[2,384,384]{2,1,0:T(8,128)(2,1)S(1)}, u32[]{:S(2)}, u32[]{:S(2)}) collective-permute-start(bf16[2,384,384]{2,1,0:T(8,128)(2,1)S(1)} %add.32.after_ref.refs_0_), channel_id=1, source_target_pairs={{0,8},{4,12},{24,16},{28,20},{1,9},{5,13},{25,17},{29,21},{2,10},{... | collective-permute-start | bytes 1769480 | tf_op jit(solution)/shard_map/ppermute | solution.py:1097
  135.2 34.8 %collective-permute-start.9 = (bf16[2,384,384]{2,1,0:T(8,128)(2,1)}, bf16[2,384,384]{2,1,0:T(8,128)(2,1)}, u32[]{:S(2)}, u32[]{:S(2)}) collective-permute-start(bf16[2,384,384]{2,1,0:T(8,128)(2,1)} %add.33.after_ref.refs_0_), channel_id=1, source_target_pairs={{0,8},{4,12},{24,16},{28,20},{1,9},{5,13},{25,17},{29,21},{2,10},{... | collective-permute-start | bytes 1769480 | tf_op jit(solution)/shard_map/ppermute | solution.py:1097
  141.5 48.1 %all-to-all-start = ((bf16[16,56,384]{2,1,0:T(8,128)(2,1)}), bf16[16,56,384]{2,1,0:T(8,128)(2,1)S(1)}, u32[]{:S(2)}, u32[]{:S(2)}) async-start(bf16[16,56,384]{2,1,0:T(8,128)(2,1)} %bitcast.11), calls=%async_computation | async-start | bytes 1376256 | tf_op jit(solution)/shard_map/all_to_all | solution.py:1161
  149.2 47.3 %collective-permute-start.11 = (bf16[544,384]{1,0:T(8,128)(2,1)}, bf16[544,384]{1,0:T(8,128)(2,1)}, u32[]{:S(2)}, u32[]{:S(2)}) collective-permute-start(bf16[544,384]{1,0:T(8,128)(2,1)} %get-tuple-element.90.after_ref), channel_id=1, source_target_pairs={{0,2},{2,0},{1,3},{3,1},{4,6},{6,4},{5,7},{7,5},{8,10},{10,8},{9,1... | collective-permute-start | bytes 1253384 | tf_op jit(solution)/shard_map/ppermute | solution.py:1064
  153.2 49.9 %collective-permute-start.13 = (bf16[2,384,384]{2,1,0:T(8,128)(2,1)S(1)}, bf16[2,384,384]{2,1,0:T(8,128)(2,1)}, u32[]{:S(2)}, u32[]{:S(2)}) collective-permute-start(bf16[2,384,384]{2,1,0:T(8,128)(2,1)S(1)} %add.34.after_ref.refs_0_), channel_id=1, source_target_pairs={{8,16},{12,20},{16,8},{20,12},{9,17},{13,21},{17,9},{21,13},{10,18... | collective-permute-start | bytes 1769480 | tf_op jit(solution)/shard_map/ppermute | solution.py:1099
  171.4 34.3 %collective-permute-start.14 = (bf16[2,384,384]{2,1,0:T(8,128)(2,1)S(1)}, bf16[2,384,384]{2,1,0:T(8,128)(2,1)}, u32[]{:S(2)}, u32[]{:S(2)}) collective-permute-start(bf16[2,384,384]{2,1,0:T(8,128)(2,1)S(1)} %add.35.after_ref.refs_0_), channel_id=1, source_target_pairs={{8,16},{12,20},{16,8},{20,12},{9,17},{13,21},{17,9},{21,13},{10,18... | collective-permute-start | bytes 1769480 | tf_op jit(solution)/shard_map/ppermute | solution.py:1099
  175.4 21.1 %copy-start.4 = (f32[1,384]{1,0:T(1,128)S(1)}, f32[1,384]{1,0:T(1,128)}, u32[]{:S(2)}) copy-start(f32[1,384]{1,0:T(1,128)} %copy-done.3) | copy-start | bytes 4612
  175.4 26.0 %collective-permute-start.12 = (bf16[1088,384]{1,0:T(8,128)(2,1)S(1)}, bf16[1088,384]{1,0:T(8,128)(2,1)S(1)}, u32[]{:S(2)}, u32[]{:S(2)}) collective-permute-start(bf16[1088,384]{1,0:T(8,128)(2,1)S(1)} %block_out.1.after_ref.refs_1_), channel_id=1, source_target_pairs={{0,1},{1,0},{2,3},{3,2},{4,5},{5,4},{6,7},{7,6},{8,9},{9,8},{10,11... | collective-permute-start | bytes 2506760 | tf_op jit(solution)/shard_map/ppermute | solution.py:1064
  190.6 58.5 %all-to-all-start.1 = ((bf16[16,56,384]{2,1,0:T(8,128)(2,1)}), bf16[16,56,384]{2,1,0:T(8,128)(2,1)}, u32[]{:S(2)}, u32[]{:S(2)}) async-start(bf16[16,56,384]{2,1,0:T(8,128)(2,1)} %total.1.after_ref), calls=%async_computation.1 | async-start | bytes 1376256 | tf_op jit(solution)/shard_map/all_to_all | solution.py:1174
  199.5 14.4 %collective-permute-start.15 = (bf16[544,384]{1,0:T(8,128)(2,1)S(1)}, bf16[544,384]{1,0:T(8,128)(2,1)S(1)}, u32[]{:S(2)}, u32[]{:S(2)}) collective-permute-start(bf16[544,384]{1,0:T(8,128)(2,1)S(1)} %token_grad.1.after_ref.refs_1_), channel_id=1, source_target_pairs={{0,2},{2,0},{1,3},{3,1},{4,6},{6,4},{5,7},{7,5},{8,10},{10,8},{9,1... | collective-permute-start | bytes 1253384 | tf_op jit(solution)/shard_map/ppermute | solution.py:1064
  204.4 24.6 %collective-permute-start.16 = (bf16[2,384,384]{2,1,0:T(8,128)(2,1)S(1)}, bf16[2,384,384]{2,1,0:T(8,128)(2,1)S(1)}, u32[]{:S(2)}, u32[]{:S(2)}) collective-permute-start(bf16[2,384,384]{2,1,0:T(8,128)(2,1)S(1)} %add.36.after_ref.refs_1_), channel_id=1, source_target_pairs={{8,0},{12,4},{16,24},{20,28},{9,1},{13,5},{17,25},{21,29},{10,2},{... | collective-permute-start | bytes 1769480 | tf_op jit(solution)/shard_map/ppermute | solution.py:1100
  206.9 40.6 %collective-permute-start.17 = (bf16[2,384,384]{2,1,0:T(8,128)(2,1)S(1)}, bf16[2,384,384]{2,1,0:T(8,128)(2,1)S(1)}, u32[]{:S(2)}, u32[]{:S(2)}) collective-permute-start(bf16[2,384,384]{2,1,0:T(8,128)(2,1)S(1)} %add.37.after_ref.refs_1_), channel_id=1, source_target_pairs={{8,0},{12,4},{16,24},{20,28},{9,1},{13,5},{17,25},{21,29},{10,2},{... | collective-permute-start | bytes 1769480 | tf_op jit(solution)/shard_map/ppermute | solution.py:1100
  214.5 34.6 %collective-permute-start.18 = (bf16[1088,384]{1,0:T(8,128)(2,1)S(1)}, bf16[1088,384]{1,0:T(8,128)(2,1)S(1)}, u32[]{:S(2)}, u32[]{:S(2)}) collective-permute-start(bf16[1088,384]{1,0:T(8,128)(2,1)S(1)} %weave.1.after_ref.refs_1_), channel_id=1, source_target_pairs={{0,1},{1,0},{2,3},{3,2},{4,5},{5,4},{6,7},{7,6},{8,9},{9,8},{10,11... | collective-permute-start | bytes 2506760 | tf_op jit(solution)/shard_map/ppermute | solution.py:1064
  229.6 29.7 %collective-permute-start.21 = (bf16[2,384,384]{2,1,0:T(8,128)(2,1)S(1)}, bf16[2,384,384]{2,1,0:T(8,128)(2,1)}, u32[]{:S(2)}, u32[]{:S(2)}) collective-permute-start(bf16[2,384,384]{2,1,0:T(8,128)(2,1)S(1)} %choose.2.after_ref.mine_ref), channel_id=1, source_target_pairs={{0,4},{4,0},{8,12},{12,8},{16,20},{20,16},{24,28},{28,24},{1,5},{5... | collective-permute-start | bytes 1769480 | tf_op jit(solution)/shard_map/ppermute | solution.py:1064
  248.1 16.4 %collective-permute-start.20 = (bf16[2,384,384]{2,1,0:T(8,128)(2,1)S(1)}, bf16[2,384,384]{2,1,0:T(8,128)(2,1)S(1)}, u32[]{:S(2)}, u32[]{:S(2)}) collective-permute-start(bf16[2,384,384]{2,1,0:T(8,128)(2,1)S(1)} %choose.3.after_ref.mine_ref), channel_id=1, source_target_pairs={{0,4},{4,0},{8,12},{12,8},{16,20},{20,16},{24,28},{28,24},{1,5},{5... | collective-permute-start | bytes 1769480 | tf_op jit(solution)/shard_map/ppermute | solution.py:1064
  249.1 2.4 collective-permute-start.19
  (20 other events, 64.8 us)
Sparse Core Ops, SparseCore 0:
  87.3 139.8 all-reduce.3
where the time goes:
time: 276 us; the launch traced here: 273 us
  Pallas kernels  132 us (48%)
  waiting for transfers between devices  81.3 us (29%)
  starting transfers between devices  35.3 us (13%)
  between operations  14.6 us (5%)
  local copies, waits for them, and re-layouts  8.89 us (3%)
    pallas_call x29, Pallas kernels, run_on(): return run(*placed)  132 us
    ppermute x2, waiting for transfers between devices, wide_step(): return lax.ppermute(value, 'wide', [(b, a) for a, b in inward])  30.9 us
    ppermute x16, waiting for transfers between devices, swap(): return lax.ppermute(value, axis, [(i, i ^ mask) for i in range(size)])  20.9 us
    ppermute x2, waiting for transfers between devices, wide_step(): return lax.ppermute(value, 'wide', inward)  15.3 us
    ppermute x16, starting transfers between devices, swap(): return lax.ppermute(value, axis, [(i, i ^ mask) for i in range(size)])  14.9 us
    all_to_all x1, waiting for transfers between devices, on_device(): lax.all_to_all(pay.reshape(-1, count, width), ('wide', 'hi'), 0, 0)  14.2 us
    unnamed x56, local copies, waits for them, and re-layouts  6.67 us
    all_to_all x1, starting transfers between devices, on_device(): pay_got = lax.all_to_all(pay_got, ('wide', 'hi'), 0, 0).reshape(pay.shape)  5.92 us
  transfers between devices with their start and end apart: 25, of which 10 were waited for; matrix products, arithmetic and copies ran while one was open for 1% of the time, Pallas kernels for 26%

commit v1 on v0

--- a/solution.py
+++ b/solution.py
@@ -18,7 +18,8 @@
 GRAIN = 16
 STRIP = 32
 FLOPS = 10**10
-PARTS = (4, 2, 2)
+PARTS = (2, 2, 2, 2)
+FIRST_TILES = 2
 GELU_A = math.sqrt(2.0 / math.pi)
 GELU_B = 0.044715
 
@@ -451,7 +452,8 @@
         pltpu.SemaphoreType.DMA((7,)),
     ]
     return call(
-        front_kernel, outs, scratch, "front", 33, in_specs=[SMEM_SPEC, SMEM_SPEC] + [VMEM_SPEC] * 4, limit=32,
+        front_kernel, outs, scratch, "front", 33, in_specs=[SMEM_SPEC, SMEM_SPEC, FAR_SPEC, PLAIN_SPEC, FAR_SPEC, PLAIN_SPEC],
+        limit=32,
         out_specs=(FAR_ANY,) * 7 + (PLAIN_SPEC,) * 2,
     )(lengths, where, tokens, w3, wproj, gain1)
 
@@ -581,7 +583,7 @@
     count = own.shape[0]
     most = (CAP + 2 * (GRAIN - 1)) // GRAIN * GRAIN
     outs = [sds((count, 2 * width), BF16)] * 2 + [sds((width, LANES), F32)]
-    out_specs = [VMEM_SPEC, PLAIN_SPEC, VMEM_SPEC]
+    out_specs = [PLAIN_SPEC, PLAIN_SPEC, VMEM_SPEC]
 
     def part(at, size, tail):
         return pl.BlockSpec((1,) + tail, lambda e: (jnp.clip(e - at, 0, size - 1),) + (0,) * len(tail))
@@ -630,7 +632,7 @@
     outs = (sds((half, width), BF16), sds((half, width), BF16))
     return call(
         unsort_kernel, outs, [pltpu.VMEM((cpad, width), BF16)], "unsort", 4, limit=12,
-        in_specs=[SMEM_SPEC, VMEM_SPEC, PLAIN_SPEC, VMEM_SPEC], out_specs=(VMEM_SPEC, PLAIN_SPEC),
+        in_specs=[SMEM_SPEC, PLAIN_SPEC, PLAIN_SPEC, VMEM_SPEC], out_specs=(VMEM_SPEC, PLAIN_SPEC),
     )(where, mine, got, unpick)
 
 
@@ -654,7 +656,7 @@
     cpad = up(count, LANES)
     return call(
         unsort_out_kernel, sds((own, width), BF16), [pltpu.VMEM((cpad, width), BF16)], "unsort_out", 3, limit=12,
-        in_specs=[VMEM_SPEC, PLAIN_SPEC, VMEM_SPEC], out_specs=PLAIN_SPEC, after=after,
+        in_specs=[PLAIN_SPEC, PLAIN_SPEC, VMEM_SPEC], out_specs=VMEM_SPEC, after=after,
     )(mine, got, pos)
 
 
@@ -690,7 +692,7 @@
     )(where, mine, other)
 
 
-def mid_back_kernel(where_ref, keep_ref, got_ref, mid_ref, cot_ref, gain2_ref, gmid_ref, ga_ref, part_ref, cot_s, mid_s, sems):
+def mid_back_kernel(where_ref, keep_ref, got_ref, mid_ref, cot_ref, gain2_ref, ex_ref, gmid_ref, ga_ref, part_ref, ex_out, cot_s, mid_s, sems):
     half = keep_ref.shape[0]
     core, side = where_ref[0], where_ref[1]
     mid_copy = strip_copy(mid_ref, 0, side, mid_s, sems.at[0])
@@ -706,35 +708,82 @@
     grad_mid = grad_final + normal_back(grad_h2, normed2, scale2, gain2_ref[...])
     gmid_ref[...] = grad_mid
     ga_ref[...] = grad_mid.astype(BF16)
-
-
-def run_mid_back(where, keep, got, mid, cot, gain2):
+    ex_out[...] = ex_ref[...]
+
+
+def run_mid_back(where, keep, got, mid, cot, gain2, ex, after):
     half, width = keep.shape
-    outs = (sds((half, width), F32), sds((half, width), BF16), sds((8, width), F32))
+    outs = (sds((half, width), F32), sds((half, width), BF16), sds((8, width), F32), sds(ex.shape, BF16))
     return call(
         mid_back_kernel, outs, [pltpu.VMEM((half // STRIP, STRIP, width), dtype) for dtype in (BF16, F32)] + [pltpu.SemaphoreType.DMA((2,))],
         "mid_back", 4, limit=12,
-        in_specs=[SMEM_SPEC, VMEM_SPEC, PLAIN_SPEC, FAR_ANY, FAR_ANY, VMEM_SPEC],
-        out_specs=(FAR_SPEC, PLAIN_SPEC, VMEM_SPEC),
-    )(where, keep, got, in_strips(mid), in_strips(cot), gain2)
-
-
-def back_kernel(
-    len_ref, where_ref, ga_ref, gao_ref, ho_any, q_any, lse_any, k_any, kt_any, v_any, hid_any, w3_ref, wproj_ref,
-    hkeep_ref, hsend_ref, dqt_ref, dkt_ref, dvt_ref, ga_s, hid_s, ho_s,
-    segk_s, qm_s, dm_s, dq_s, dk_s, dv_s, q_s, do_s, lse_s, d_s, gh_s, col_s,
-    k_ref, v_ref, kt_ref, hoc_s, lsec_s, qc_s, hidc_s, sems,
+        in_specs=[SMEM_SPEC, VMEM_SPEC, PLAIN_SPEC, FAR_ANY, FAR_ANY, VMEM_SPEC, VMEM_SPEC],
+        out_specs=(FAR_SPEC, PLAIN_SPEC, VMEM_SPEC, FAR_SPEC), after=after,
+    )(where, keep, got, in_strips(mid), in_strips(cot), gain2, ex)
+
+
+def back_tiles(
+    first_tile, last_tile, ends, side, own, q_s, do_s, lse_s, d_s, k_ref, v_ref, kt_ref,
+    segk_s, qm_s, dm_s, dq_s, dk_s, dv_s,
+):
+    mine = kt_ref.shape[0]
+    heads = mine // 64
+
+    def place(index):
+        return 2 * STRIP * (index // STRIP) + STRIP * side + index % STRIP
+
+    def q_step(qb, carry):
+        first = pl.multiple_of(qb * KB, KB)
+        last = jnp.minimum(first + KB, own) - 1
+        for h in range(heads):
+            mask = head_mask(KB, h % 2)
+            qm_s[h] = q_s[pl.ds(first, KB), lane_head(h)] * mask
+            dm_s[h] = do_s[pl.ds(first, KB), lane_head(h)] * mask
+        dq_s[:, pl.ds(first, KB)] = jnp.zeros((mine, KB), F32)
+        low, high = seq_bounds(ends, place(first), place(last))
+        start, steps = key_steps(low, high)
+        index = lax.broadcasted_iota(jnp.int32, (8, KB), 1) + first
+        segq = jnp.where(index < own, segment_of(place(index), ends), -1)[0:1]
+        lse = [lse_s[h : h + 1, pl.ds(first, KB)] for h in range(heads)]
+        dots = [d_s[h : h + 1, pl.ds(first, KB)] for h in range(heads)]
+
+        def k_step(kb, carry):
+            at = pl.multiple_of(start + kb * KB, LANES)
+            bias = bias_block(segk_s, at, segq)
+            s = [mm(k_ref[pl.ds(at, KB), lane_head(h)], qm_s[h], COLS_COLS) for h in range(heads)]
+            dp = [mm(v_ref[pl.ds(at, KB), lane_head(h)], dm_s[h], COLS_COLS) for h in range(heads)]
+            p = [jnp.exp((s[h] + bias) - lse[h]) for h in range(heads)]
+            ds = [(p[h] * (dp[h] - dots[h])).astype(BF16) for h in range(heads)]
+            p = [a.astype(BF16) for a in p]
+            dv = [mm(p[h], dm_s[h]) for h in range(heads)]
+            dk = [mm(ds[h], qm_s[h]) for h in range(heads)]
+            dq = [mm(kt_ref[h * 64 : (h + 1) * 64, pl.ds(at, KB)], ds[h]) for h in range(heads)]
+            for ref, add in ((dv_s, dv), (dk_s, dk)):
+                for j in range(up(heads, 2) // 2):
+                    pair = add[2 * j : 2 * j + 2]
+                    ref[pl.ds(at, KB), j * LANES : (j + 1) * LANES] += pair[0] if len(pair) == 1 else pair[0] + pair[1]
+            for h in range(heads):
+                dq_s[h * 64 : (h + 1) * 64, pl.ds(first, KB)] += dq[h]
+            return carry
+
+        lax.fori_loop(0, steps, k_step, 0)
+        return carry
+
+    lax.fori_loop(first_tile, last_tile, q_step, 0)
+
+
+def back_first_kernel(
+    len_ref, where_ref, ga_ref, gao_ref, ho_any, q_any, lse_any, k_any, kt_any, v_any, hid_any, wproj_ref,
+    ga_s, hid_s, ho_s, q_s, do_s, lse_s, d_s, dq_s, dk_s, dv_s,
+    segk_s, qm_s, dm_s, col_s, k_ref, v_ref, kt_ref, hoc_s, lsec_s, qc_s, hidc_s, sems,
 ):
     half, width = ga_ref.shape
-    rows = 4 * half
     own = 2 * half
     kpad = k_ref.shape[0]
     cpad = ga_s.shape[0]
-    mine = w3_ref.shape[2]
-    heads = mine // 64
+    mine = kt_ref.shape[0]
     core, side = where_ref[0], where_ref[1]
     ends = seq_ends(len_ref, len_ref.shape[1])
-    scale = 1.0 / math.sqrt(width // HEADS)
 
     strips_of = (hoc_s, lsec_s, qc_s, hidc_s)
     copies = [
@@ -773,47 +822,41 @@
         preferred_element_type=F32,
     )
 
-    def place(index):
-        return 2 * STRIP * (index // STRIP) + STRIP * side + index % STRIP
-
-    def q_step(qb, carry):
-        first = pl.multiple_of(qb * KB, KB)
-        last = jnp.minimum(first + KB, own) - 1
-        for h in range(heads):
-            mask = head_mask(KB, h % 2)
-            qm_s[h] = q_s[pl.ds(first, KB), lane_head(h)] * mask
-            dm_s[h] = do_s[pl.ds(first, KB), lane_head(h)] * mask
-        dq_s[:, pl.ds(first, KB)] = jnp.zeros((mine, KB), F32)
-        low, high = seq_bounds(ends, place(first), place(last))
-        start, steps = key_steps(low, high)
-        index = lax.broadcasted_iota(jnp.int32, (8, KB), 1) + first
-        segq = jnp.where(index < own, segment_of(place(index), ends), -1)[0:1]
-        lse = [lse_s[h : h + 1, pl.ds(first, KB)] for h in range(heads)]
-        dots = [d_s[h : h + 1, pl.ds(first, KB)] for h in range(heads)]
-
-        def k_step(kb, carry):
-            at = pl.multiple_of(start + kb * KB, LANES)
-            bias = bias_block(segk_s, at, segq)
-            s = [mm(k_ref[pl.ds(at, KB), lane_head(h)], qm_s[h], COLS_COLS) for h in range(heads)]
-            dp = [mm(v_ref[pl.ds(at, KB), lane_head(h)], dm_s[h], COLS_COLS) for h in range(heads)]
-            p = [jnp.exp((s[h] + bias) - lse[h]) for h in range(heads)]
-            ds = [(p[h] * (dp[h] - dots[h])).astype(BF16) for h in range(heads)]
-            p = [a.astype(BF16) for a in p]
-            dv = [mm(p[h], dm_s[h]) for h in range(heads)]
-            dk = [mm(ds[h], qm_s[h]) for h in range(heads)]
-            dq = [mm(kt_ref[h * 64 : (h + 1) * 64, pl.ds(at, KB)], ds[h]) for h in range(heads)]
-            for ref, add in ((dv_s, dv), (dk_s, dk)):
-                for j in range(up(heads, 2) // 2):
-                    pair = add[2 * j : 2 * j + 2]
-                    ref[pl.ds(at, KB), j * LANES : (j + 1) * LANES] += pair[0] if len(pair) == 1 else pair[0] + pair[1]
-            for h in range(heads):
-                dq_s[h * 64 : (h + 1) * 64, pl.ds(first, KB)] += dq[h]
-            return carry
-
-        lax.fori_loop(0, steps, k_step, 0)
-        return carry
-
-    lax.fori_loop(0, cpad // KB, q_step, 0)
+    back_tiles(
+        0, FIRST_TILES, ends, side, own, q_s, do_s, lse_s, d_s, k_ref, v_ref, kt_ref,
+        segk_s, qm_s, dm_s, dq_s, dk_s, dv_s,
+    )
+
+
+def back_second_kernel(
+    len_ref, where_ref, k_any, kt_any, v_any, q_s, do_s, lse_s, d_s, dq_ref, dk_ref, dv_ref, w3_ref,
+    hkeep_ref, hsend_ref, dqt_ref, dkt_ref, dvt_ref,
+    segk_s, qm_s, dm_s, dq_s, dk_s, dv_s, gh_s, k_ref, v_ref, kt_ref, sems,
+):
+    own, width = hkeep_ref.shape
+    rows = 2 * own
+    kpad = k_ref.shape[0]
+    cpad = q_s.shape[0]
+    mine = w3_ref.shape[2]
+    core, side = where_ref[0], where_ref[1]
+    ends = seq_ends(len_ref, len_ref.shape[1])
+    scale = 1.0 / math.sqrt(width // HEADS)
+    copies = [
+        pltpu.make_async_copy(ref, dst, sems.at[i])
+        for i, (ref, dst) in enumerate(((k_any, k_ref), (v_any, v_ref), (kt_any, kt_ref)))
+    ]
+    for copy in copies:
+        copy.start()
+    key_segments(segk_s, ends, kpad)
+    dq_s[...] = dq_ref[...]
+    dk_s[...] = dk_ref[...]
+    dv_s[...] = dv_ref[...]
+    for copy in copies:
+        copy.wait()
+    back_tiles(
+        FIRST_TILES, cpad // KB, ends, side, own, q_s, do_s, lse_s, d_s, k_ref, v_ref, kt_ref,
+        segk_s, qm_s, dm_s, dq_s, dk_s, dv_s,
+    )
 
     wq, wk, wv = w3_ref[0], w3_ref[1], w3_ref[2]
     dqt = (dq_s[...] * scale).astype(BF16)
@@ -836,6 +879,7 @@
         gh_s[at, :] += grad_q[i * STRIP : (i + 1) * STRIP]
     hkeep_ref[...] = gh_s[pl.ds(pl.multiple_of(core * own, GRAIN), own), :].astype(BF16)
     hsend_ref[...] = gh_s[pl.ds(pl.multiple_of((1 - core) * own, GRAIN), own), :].astype(BF16)
+
 
 def weight_kernel(
     dqt_ref, dkt_ref, dvt_ref, ga_ref, hidc_ref, hoc_ref, hid_any, groute_ref, gain2_ref, pay_ref, hid_ref, sem
@@ -862,35 +906,29 @@
     )(dqt, dkt, dvt, ga, hidc, hoc, hid, groute, gain2)
 
 
-def run_back(lengths, where, ga, gao, ho, q, lse, k, kt, v, hid, w3, wproj, after):
+def run_back_first(lengths, where, ga, gao, ho, q, lse, k, kt, v, hid, wproj, after):
     half, width = ga.shape
     own = 2 * half
     kpad, lanes = k.shape
-    mine = w3.shape[2]
+    mine = kt.shape[0]
     heads = mine // 64
     cpad = up(own, KB)
     outs = (
-        sds((own, width), BF16),
-        sds((own, width), BF16),
-        sds((mine, cpad), BF16),
-        sds((mine, kpad), BF16),
-        sds((mine, kpad), BF16),
         sds((cpad, width), BF16),
         sds((cpad, width), BF16),
         sds((cpad, lanes), BF16),
+        sds((cpad, lanes), BF16),
+        sds((cpad, lanes), BF16),
+        sds((8, cpad), F32),
+        sds((8, cpad), F32),
+        sds((mine, cpad), F32),
+        sds((kpad, lanes), F32),
+        sds((kpad, lanes), F32),
     )
     scratch = [
         pltpu.VMEM((kpad, LANES), jnp.int32),
         pltpu.VMEM((heads, KB, LANES), BF16),
         pltpu.VMEM((heads, KB, LANES), BF16),
-        pltpu.VMEM((mine, cpad), F32),
-        pltpu.VMEM((kpad, lanes), F32),
-        pltpu.VMEM((kpad, lanes), F32),
-        pltpu.VMEM((cpad, lanes), BF16),
-        pltpu.VMEM((cpad, lanes), BF16),
-        pltpu.VMEM((8, cpad), F32),
-        pltpu.VMEM((8, cpad), F32),
-        pltpu.VMEM((4 * half, width), F32),
         pltpu.VMEM((cpad, LANES), F32),
         pltpu.VMEM((kpad, lanes), BF16),
         pltpu.VMEM((kpad, lanes), BF16),
@@ -902,10 +940,43 @@
         pltpu.SemaphoreType.DMA((7,)),
     ]
     return call(
-        back_kernel, outs, scratch, "back", 28,
-        in_specs=[SMEM_SPEC, SMEM_SPEC, PLAIN_SPEC, PLAIN_SPEC] + [FAR_ANY] * 7 + [VMEM_SPEC] * 2,
-        out_specs=(FAR_SPEC, PLAIN_SPEC) + (VMEM_SPEC,) * 6, limit=32, after=after,
-    )(lengths, where, ga, gao, in_strips(ho), in_strips(q), in_strips(lse), k, kt, v, in_strips(hid), w3, wproj)
+        back_first_kernel, outs, scratch, "back_first", 14,
+        in_specs=[SMEM_SPEC, SMEM_SPEC, PLAIN_SPEC, PLAIN_SPEC] + [FAR_ANY] * 7 + [PLAIN_SPEC],
+        out_specs=(VMEM_SPEC,) * 10, limit=24, after=after,
+    )(lengths, where, ga, gao, in_strips(ho), in_strips(q), in_strips(lse), k, kt, v, in_strips(hid), wproj)
+
+
+def run_back_second(own, lengths, where, k, kt, v, q, do, lse, dots, dq, dk, dv, w3, after):
+    kpad, lanes = k.shape
+    mine = kt.shape[0]
+    heads = mine // 64
+    cpad = q.shape[0]
+    width = w3.shape[1]
+    outs = (
+        sds((own, width), BF16),
+        sds((own, width), BF16),
+        sds((mine, cpad), BF16),
+        sds((mine, kpad), BF16),
+        sds((mine, kpad), BF16),
+    )
+    scratch = [
+        pltpu.VMEM((kpad, LANES), jnp.int32),
+        pltpu.VMEM((heads, KB, LANES), BF16),
+        pltpu.VMEM((heads, KB, LANES), BF16),
+        pltpu.VMEM((mine, cpad), F32),
+        pltpu.VMEM((kpad, lanes), F32),
+        pltpu.VMEM((kpad, lanes), F32),
+        pltpu.VMEM((2 * own, width), F32),
+        pltpu.VMEM((kpad, lanes), BF16),
+        pltpu.VMEM((kpad, lanes), BF16),
+        pltpu.VMEM((mine, kpad), BF16),
+        pltpu.SemaphoreType.DMA((3,)),
+    ]
+    return call(
+        back_second_kernel, outs, scratch, "back_second", 14,
+        in_specs=[SMEM_SPEC, SMEM_SPEC] + [FAR_ANY] * 3 + [VMEM_SPEC] * 7 + [PLAIN_SPEC],
+        out_specs=(FAR_SPEC, PLAIN_SPEC) + (VMEM_SPEC,) * 3, limit=24, after=after,
+    )(lengths, where, k, kt, v, q, do, lse, dots, dq, dk, dv, w3)
 
 
 def token_kernel(where_ref, mine_ref, got_ref, gmid_ref, tok_ref, gain1_ref, out_ref, tok_s, sem):
@@ -1035,7 +1106,7 @@
     for i in range(3):
         rows = slice(i * share, (i + 1) * share)
         part = jnp.concatenate([low[rows], high[rows]], 0).T
-        gqkv_ref[:, i, :] = part
+        gqkv_ref[i] = part
         product = product + part * wqkv_ref[i].astype(F32)
     gproj_ref[...] = jnp.concatenate([low[3 * share : 4 * share], high[3 * share : 4 * share]], 0)
     g1_ref[...] = jnp.sum(product.T, 0, keepdims=True) / gain1_ref[...]
@@ -1047,7 +1118,7 @@
 def run_attn_end(where, mine, other, wqkv, gain1, after):
     width = wqkv.shape[1]
     outs = (
-        sds((width, 3, width), F32),
+        sds((3, width, width), F32),
         sds((width, width), F32),
         sds((1, width), F32),
         sds((1, width), F32),
@@ -1135,76 +1206,92 @@
     unpick = run_unpick(pos, own, own_x.shape[0], (yoth, ANY_SPEC))
     keep, send = run_unsort(where, yown, got, unpick)
     gh2 = swap(send, "hi", 1)
-    gmid, ga, gain2_part = run_mid_back(where, keep, gh2, mid, cotangent, gain2)
+    ex = run_unsort_out(yown, got, pos, own, (send, ANY_SPEC))
+    sums, moved = [], []
+    for mine, unused in pairs:
+        sums.append(mine)
+    line = wide_size == 8
+
+    def add_step(i, recv, after):
+        sums[i] = added(sums[i], recv, after)
+        return sums[i], ANY_SPEC
+
+    def first_step(i, after):
+        after = add_step(i, recvs[i], after)
+        if line:
+            moved.append(wide_step(sums[i], 0))
+        else:
+            for j in range(1, wide_size.bit_length() - 1):
+                after = add_step(i, swap(sums[i], "wide", 1 << j), after)
+        return after
+
+    def line_step(i, step, after):
+        if line:
+            after = add_step(i, moved[i], after)
+            moved[i] = wide_step(sums[i], step)
+        return after
+
+    def last_step(i, after):
+        if line:
+            sums[i] = chosen(where, sums[i], moved[i], after)
+            after = sums[i], ANY_SPEC
+        others.append(swap(sums[i], "wide", 1))
+        return after
+
+    others = []
+    gmid, ga, gain2_part, ex = run_mid_back(where, keep, gh2, mid, cotangent, gain2, ex, (ex, VMEM_SPEC))
     gao = swap(ga, "lo", 1)
-    ex = run_unsort_out(yown, got, pos, own, (ga, ANY_SPEC))
     ex_got = swap(ex, "hi", 1)
-
-    hkeep, hsend, dqt, dkt, dvt, ga_c, hid_c, ho_c = run_back(
-        lengths, where, ga, gao, ho, q, lse, k, kt, v, hid, w3, w_proj, (ex, ANY_SPEC)
-    )
+    last = first_step(0, (ex, FAR_ANY))
+
+    ga_c, hid_c, ho_c, *state = run_back_first(lengths, where, ga, gao, ho, q, lse, k, kt, v, hid, w_proj, last)
+    last = ga_c, VMEM_SPEC
+    last = first_step(1, last)
+    last = line_step(0, 1, last)
+    hkeep, hsend, dqt, dkt, dvt = run_back_second(own, lengths, where, k, kt, v, *state, w3, last)
     hgot = swap(hsend, "lo", 1)
-    last = hsend, ANY_SPEC
-    line = wide_size == 8
-    sums = []
-    for (mine, unused), recv in zip(pairs, recvs):
-        mine = added(mine, recv, last)
-        if not line:
-            for i in range(1, wide_size.bit_length() - 1):
-                mine = added(mine, swap(mine, "wide", 1 << i), last)
-        last = mine, ANY_SPEC
-        sums.append(mine)
-    moved = [wide_step(a, 0) for a in sums] if line else sums
     pay_rows = up(2 * width + 16, 8 * lax.axis_size(("wide", "hi")))
-    pay = run_weights(pay_rows, dqt, dkt, dvt, ga_c, hid_c, ho_c, hid, groute, gain2_part, last)
-    count = pay_rows // lax.axis_size(("wide", "hi"))
-    pay_got = lax.all_to_all(pay.reshape(-1, count, width), ("wide", "hi"), 0, 0)
-    hk, hs = run_split(where, hkeep, hgot, (pay, ANY_SPEC))
+    pay = run_weights(pay_rows, dqt, dkt, dvt, ga_c, hid_c, ho_c, hid, groute, gain2_part, (hsend, ANY_SPEC))
+    share = pay_rows // lax.axis_size(("wide", "hi"))
+    pay_got = lax.all_to_all(pay.reshape(-1, share, width), ("wide", "hi"), 0, 0)
+    last = first_step(2, (pay, ANY_SPEC))
+    last = line_step(0, 2, last)
+    last = line_step(1, 1, last)
+    hk, hs = run_split(where, hkeep, hgot, last)
     hs_got = swap(hs, "hi", 1)
-    last = hs, ANY_SPEC
-    if line:
-        for i in range(len(sums)):
-            sums[i] = added(sums[i], moved[i], last)
-            last = sums[i], ANY_SPEC
-            moved[i] = wide_step(sums[i], 1)
-    mine = run_out(mid, ex, ex_got, last)
-    other = swap(mine, "lo", 1)
-    pay_got = run_total(pay_got, (mine, ANY_SPEC))
+    out_own = run_out(mid, ex, ex_got, (hs, ANY_SPEC))
+    out_oth = swap(out_own, "lo", 1)
+    last = line_step(2, 1, (out_own, ANY_SPEC))
+    last = line_step(1, 2, last)
+    last = last_step(0, last)
+    token_rows = run_tokens(where, hk, hs_got, gmid, tokens, gain1, last)
+    token_got = swap(token_rows, "hi", 1)
+    last = line_step(2, 2, (token_rows, ANY_SPEC))
+    pay_got = run_total(pay_got, last)
     last = pay_got, ANY_SPEC
     pay_got = lax.all_to_all(pay_got, ("wide", "hi"), 0, 0).reshape(pay.shape)
-    token_rows = run_tokens(where, hk, hs_got, gmid, tokens, gain1, last)
-    last = token_rows, ANY_SPEC
-    token_got = swap(token_rows, "hi", 1)
-    layer_out = run_join(where, mine, other, last)
-    last = layer_out, FAR_ANY
-    if line:
-        for i in range(len(sums)):
-            sums[i] = added(sums[i], moved[i], last)
-            last = sums[i], ANY_SPEC
-            moved[i] = wide_step(sums[i], 2)
-    token_own = run_weave(where, token_rows, token_got, last)
-    last = token_own, ANY_SPEC
+    last = last_step(1, last)
+    layer_out = run_join(where, out_own, out_oth, last)
+    token_own = run_weave(where, token_rows, token_got, (layer_out, FAR_ANY))
     token_oth = swap(token_own, "lo", 1)
-    if line:
-        for i in range(len(sums)):
-            sums[i] = chosen(where, sums[i], moved[i], last)
-            last = sums[i], ANY_SPEC
-    others = [swap(a, "wide", 1) for a in sums]
-    pay_oth = swap(pay_got, "lo", 1)
+    last = last_step(2, (token_own, ANY_SPEC))
     grad_tokens = run_join(where, token_own, token_oth, last)
-    last = grad_tokens, FAR_ANY
-    grad_qkv, grad_proj, grad_norm1, grad_norm2, route_t = run_attn_end(where, pay_got, pay_oth, wqkv, gain1, last)
-    before = run_summed_end(total_a, w_in.shape, w_out.shape, (grad_proj, FAR_ANY))
+    before = run_summed_end(total_a, w_in.shape, w_out.shape, (grad_tokens, FAR_ANY))
     at = PARTS[0]
-    for mine, other, size in zip(sums, others, PARTS[1:]):
-        before = run_expert_end(at, where, mine, other, w_in.shape, w_out.shape, before)
+    for i, size in enumerate(PARTS[1:]):
+        if i == len(PARTS) - 2:
+            pay_oth = swap(pay_got, "lo", 1)
+            grad_qkv, grad_proj, grad_norm1, grad_norm2, route_t = run_attn_end(
+                where, pay_got, pay_oth, wqkv, gain1, (before[0], FAR_ANY)
+            )
+        before = run_expert_end(at, where, sums[i], others[i], w_in.shape, w_out.shape, before)
         at += size
     grad_in, grad_out = before
 
     return (
         layer_out,
         grad_tokens,
-        grad_qkv,
+        grad_qkv.transpose(1, 0, 2),
         grad_proj,
         grad_norm1.reshape(width),
         grad_norm2.reshape(width),

time: 276 us -> 263 us (0.953)
  waiting for transfers between devices: 81.3 us -> 33.9 us
  starting transfers between devices: 35.3 us -> 62.1 us
  Pallas kernels: 132 us -> 143 us
  local copies, waits for them, and re-layouts: 8.89 us -> 5.38 us
    all_to_all x1, waiting for transfers between devices: 14.2 us -> 0.01 us  [on_device(): lax.all_to_all(pay.reshape(-1, share, width), ('wide', 'hi'), 0, 0)]
    ppermute x2 -> x3, waiting for transfers between devices: 30.9 us -> 17.2 us  [wide_step(): return lax.ppermute(value, 'wide', [(b, a) for a, b in inward])]
    ppermute x2 -> x3, waiting for transfers between devices: 15.3 us -> 3.26 us  [wide_step(): return lax.ppermute(value, 'wide', inward)]
    ppermute x2 -> x3, starting transfers between devices: 3.46 us -> 15.5 us  [wide_step(): return lax.ppermute(value, 'wide', inward)]
    pallas_call x29 -> x35, Pallas kernels: 132 us -> 143 us  [run_on(): return run(*placed)]
    all_to_all x1, starting transfers between devices: 5.92 us -> 14.8 us  [on_device(): pay_got = lax.all_to_all(pay_got, ('wide', 'hi'), 0, 0).reshape(pay.shape)]
    ppermute x16 -> x18, waiting for transfers between devices: 20.9 us -> 13.3 us  [swap(): return lax.ppermute(value, axis, [(i, i ^ mask) for i in range(size)])]
    ppermute x16 -> x18, starting transfers between devices: 14.9 us -> 20.2 us  [swap(): return lax.ppermute(value, axis, [(i, i ^ mask) for i in range(size)])]
  transfers between devices with their start and end apart: 25 -> 30, of which waited for: 10 -> 7; matrix products, arithmetic and copies ran while one was open for 1% -> 1% of each run, Pallas kernels for 26% -> 32%
where the time goes in v1:
time: 263 us; the launch traced here: 262 us
  Pallas kernels  143 us (54%)
  starting transfers between devices  62.1 us (24%)
  waiting for transfers between devices  33.9 us (13%)
  between operations  14.7 us (6%)
  local copies, waits for them, and re-layouts  5.38 us (2%)
  other arithmetic  2.65 us (1%)
    pallas_call x35, Pallas kernels, run_on(): return run(*placed)  143 us
    ppermute x18, starting transfers between devices, swap(): return lax.ppermute(value, axis, [(i, i ^ mask) for i in range(size)])  20.2 us
    ppermute x3, waiting for transfers between devices, wide_step(): return lax.ppermute(value, 'wide', [(b, a) for a, b in inward])  17.2 us
    ppermute x3, starting transfers between devices, wide_step(): return lax.ppermute(value, 'wide', inward)  15.5 us
    all_to_all x1, starting transfers between devices, on_device(): pay_got = lax.all_to_all(pay_got, ('wide', 'hi'), 0, 0).reshape(pay.shape)  14.8 us
    ppermute x18, waiting for transfers between devices, swap(): return lax.ppermute(value, axis, [(i, i ^ mask) for i in range(size)])  13.3 us
  transfers between devices with their start and end apart: 30, of which 7 were waited for; matrix products, arithmetic and copies ran while one was open for 1% of the time, Pallas kernels for 32%

profile of v1, /device:TPU:0, one launch (start us, length us, event | category | flops | bytes accessed | tf_op | source)
XLA Modules:
  0.0 261.7 jit_solution(15230537164398686551)
XLA Ops:
  10.2 29.0 %front.1 = (bf16[2560,384]{1,0:T(8,128)(2,1)}, bf16[2560,256]{1,0:T(8,128)(2,1)}, bf16[192,2560]{1,0:T(8,128)(2,1)}, bf16[2560,256]{1,0:T(8,128)(2,1)}, bf16[230...) custom-call(s32[1,8]{1,0:T(1,128)S(1)} %copy-done.10, ...), custom_call_target="tpu_custom_call" | custom-call | flops 330000007168 | bytes 10000 | tf_op jit(solution)/shard_map/front/pallas_call | solution.py:394
  41.7 8.2 %mid.1 = (f32[1088,384]{1,0:T(8,128)}, bf16[1216,768]{1,0:T(8,128)(2,1)S(1)}, bf16[1216,768]{1,0:T(8,128)(2,1)S(1)}) custom-call(s32[4]{0:T(128)S(1)} %pad_add_fusion.where_ref.refs_0_.refs_1_, bf16[1088,384]{1,0:T(8,128)(2,1)S(1)} %get-tuple-element.69.after_ref.keep_ref, bf16[1088,384]{1,0:T(8,128)(2,1)S(1)} %collective-permute-done.got_ref, ...), custom_call_target="tpu_custom_call" | custom-call | flops 89999998976 | bytes 10000 | tf_op jit(solution)/shard_map/mid/pallas_call | solution.py:394
  50.3 3.5 %collective-permute-done.1.oth_ref = bf16[1216,768]{1,0:T(8,128)(2,1)S(1)} collective-permute-done((bf16[1216,768]{1,0:T(8,128)(2,1)S(1)}, bf16[1216,768]{1,0:T(8,128)(2,1)S(1)}, u32[]{:S(2)}, u32[]{:S(2)}) %collective-permute-start.1) | collective-permute-done | bytes 1867808 | tf_op jit(solution)/shard_map/ppermute | solution.py:1135
  53.8 20.3 %experts.1 = (bf16[1216,768]{1,0:T(8,128)(2,1)S(1)}, bf16[1216,768]{1,0:T(8,128)(2,1)S(1)}, f32[384,128]{1,0:T(8,128)S(1)}, bf16[2,2,384,384]{3,2,1,0:T(8,128)(2...) custom-call(s32[32,128]{1,0:T(8,128)S(1)} %get-tuple-element.70.plan, ...), custom_call_target="tpu_custom_call" | custom-call | flops 219999993856 | bytes 10000 | tf_op jit(solution)/shard_map/experts/pallas_call | solution.py:394
  75.6 2.8 %collective-permute-start.4 = (bf16[2,384,384]{2,1,0:T(8,128)(2,1)}, bf16[2,384,384]{2,1,0:T(8,128)(2,1)S(1)}, u32[]{:S(2)}, u32[]{:S(2)}) collective-permute-start(bf16[2,384,384]{2,1,0:T(8,128)(2,1)} %get-tuple-element.82), channel_id=1, source_target_pairs={{0,4},{4,0},{8,12},{12,8},{16,20},{20,16},{24,28},{28,24},{1,5},{5... | collective-permute-start | bytes 1769480 | tf_op jit(solution)/shard_map/ppermute | solution.py:1135
  81.9 3.2 %unsort.1 = (bf16[544,384]{1,0:T(8,128)(2,1)S(1)}, bf16[544,384]{1,0:T(8,128)(2,1)S(1)}) custom-call(s32[4]{0:T(128)S(1)} %pad_add_fusion.where_ref.refs_0_.refs_1_, bf16[1216,768]{1,0:T(8,128)(2,1)S(1)} %copy-done.15, bf16[1216,768]{1,0:T(8,128)(2,1)} %collective-permute-done.2.got_ref.refs_1_, bf16[2,544,1280]{2,1,0:T(8,128)(2,1)S(1)} %unpick.1.unpick_ref), custom_call_target="tpu_custom_call" | custom-call | flops 40000000000 | bytes 10000 | tf_op jit(solution)/shard_map/unsort/pallas_call | solution.py:394
  86.8 3.2 %unsort_out.1.after_ref.refs_6_ = bf16[1088,384]{1,0:T(8,128)(2,1)S(1)} custom-call(bf16[544,384]{1,0:T(8,128)(2,1)S(1)} %get-tuple-element.77.after_ref, bf16[1216,768]{1,0:T(8,128)(2,1)S(1)} %copy-done.15, bf16[1216,768]{1,0:T(8,128)(2,1)} %collective-permute-done.2.got_ref.refs_1_, f32[8,1152]{1,0:T(8,128)S(1)} %copy-done.20), custom_call_target="tpu_custom_call" | custom-call | flops 30000001024 | bytes 10000 | tf_op jit(solution)/shard_map/unsort_out/pallas_call | solution.py:394
  90.0 6.3 %collective-permute-done.3.refs_2_ = bf16[544,384]{1,0:T(8,128)(2,1)S(1)} collective-permute-done((bf16[544,384]{1,0:T(8,128)(2,1)S(1)}, bf16[544,384]{1,0:T(8,128)(2,1)S(1)}, u32[]{:S(2)}, u32[]{:S(2)}) %collective-permute-start.3) | collective-permute-done | bytes 417824 | tf_op jit(solution)/shard_map/ppermute | solution.py:1135
  96.3 3.6 %mid_back.1 = (f32[544,384]{1,0:T(8,128)}, bf16[544,384]{1,0:T(8,128)(2,1)S(1)}, f32[8,384]{1,0:T(8,128)S(1)}, bf16[1088,384]{1,0:T(8,128)(2,1)}) custom-call(bf16[1088,384]{1,0:T(8,128)(2,1)S(1)} %unsort_out.1.after_ref.refs_6_, s32[4]{0:T(128)S(1)} %pad_add_fusion.where_ref.refs_0_.refs_1_, bf16[544,384]{1,0:T(8,128)(2,1)S(1)} %get-tuple-element.78.refs_1_, ...), custom_call_target="tpu_custom_call" | custom-call | flops 40000000000 | bytes 10000 | tf_op jit(solution)/shard_map/mid_back/pallas_call | solution.py:394
  102.6 5.2 %collective-permute-start.7 = (bf16[2,384,384]{2,1,0:T(8,128)(2,1)}, bf16[2,384,384]{2,1,0:T(8,128)(2,1)}, u32[]{:S(2)}, u32[]{:S(2)}) collective-permute-start(bf16[2,384,384]{2,1,0:T(8,128)(2,1)} %add.35.after_ref.refs_0_), channel_id=1, source_target_pairs={{0,8},{4,12},{24,16},{28,20},{1,9},{5,13},{25,17},{29,21},{2,10},{... | collective-permute-start | bytes 1769480 | tf_op jit(solution)/shard_map/ppermute | solution.py:1168
  107.8 11.1 %back_first.1 = (bf16[1280,384]{1,0:T(8,128)(2,1)S(1)}, bf16[1280,384]{1,0:T(8,128)(2,1)S(1)}, bf16[1280,256]{1,0:T(8,128)(2,1)S(1)}, bf16[1280,256]{1,0:T(8,128...) custom-call(bf16[2,384,384]{2,1,0:T(8,128)(2,1)} %add.35.after_ref.r, ...), custom_call_target="tpu_custom_call" | custom-call | flops 140000002048 | bytes 10000 | tf_op jit(solution)/shard_map/back_first/pallas_call | solution.py:394
  118.9 2.4 add.36.after_ref.refs_0_
  121.3 2.3 collective-permute-start.10
  127.2 15.4 %back_second.1 = (bf16[1088,384]{1,0:T(8,128)(2,1)}, bf16[1088,384]{1,0:T(8,128)(2,1)S(1)}, bf16[192,1280]{1,0:T(8,128)(2,1)S(1)}, bf16[192,2560]{1,0:T(8,128)(2,1)S(1)}, bf16[192,2560]{1,0:T(8,128)(2,1)S(1)}) custom-call(bf16[2,384,384]{2,1,0:T(8,128)(2,1)} %add.37.after_ref.refs_0_, s32[1,8]{1,0:T(1,128)S(1)} %copy-done.11, ...), custom_call_target="tpu_custom_call" | custom-call | flops 140000002048 | bytes 10000 | tf_op jit(solution)/shard_map/back_second/pallas_call | solution.py:394
  142.7 4.1 %weights.1.after_ref = bf16[896,384]{1,0:T(8,128)(2,1)} custom-call(bf16[1088,384]{1,0:T(8,128)(2,1)S(1)} %get-tuple-element.101.after_ref, bf16[192,1280]{1,0:T(8,128)(2,1)S(1)} %get-tuple-element.102.refs_0_, bf16[192,2560]{1,0:T(8,128)(2,1)S(1)} %get-tuple-element.103.refs_1_, bf16[192,2560]{1,0:T(8,128)(2,1)S(1)} %get-tuple-element.104.refs_2_, ...), custom_call_target="tpu_custom_call" | custom-call | flops 40000000000 | bytes 10000 | tf_op jit(solution)/shard_map/weights/pallas_call | solution.py:394
  148.1 8.0 %collective-permute-start.13 = (bf16[2,384,384]{2,1,0:T(8,128)(2,1)S(1)}, bf16[2,384,384]{2,1,0:T(8,128)(2,1)S(1)}, u32[]{:S(2)}, u32[]{:S(2)}) collective-permute-start(bf16[2,384,384]{2,1,0:T(8,128)(2,1)S(1)} %add.38.after_ref.refs_0_), channel_id=1, source_target_pairs={{0,8},{4,12},{24,16},{28,20},{1,9},{5,13},{25,17},{29,21},{2,10},{... | collective-permute-start | bytes 1769480 | tf_op jit(solution)/shard_map/ppermute | solution.py:1168
  156.1 5.0 %all-to-all-start = ((bf16[16,56,384]{2,1,0:T(8,128)(2,1)}), bf16[16,56,384]{2,1,0:T(8,128)(2,1)}, u32[]{:S(2)}, u32[]{:S(2)}) async-start(bf16[16,56,384]{2,1,0:T(8,128)(2,1)} %bitcast.12), calls=%async_computation | async-start | bytes 1376256 | tf_op jit(solution)/shard_map/all_to_all | solution.py:1256
  170.0 2.9 %block_out.1.after_ref.refs_1_ = bf16[1088,384]{1,0:T(8,128)(2,1)} custom-call(bf16[544,384]{1,0:T(8,128)(2,1)S(1)} %get-tuple-element.112.after_ref, f32[1088,384]{1,0:T(8,128)} %get-tuple-element.79.refs_0_, bf16[1088,384]{1,0:T(8,128)(2,1)S(1)} %copy-done.8, bf16[1088,384]{1,0:T(8,128)(2,1)} %collective-permute-done.12.refs_2_), custom_call_target="tpu_custom_call" | custom-call | flops 20000000000 | bytes 10000 | tf_op jit(solution)/shard_map/block_out/pallas_call | solution.py:394
  172.9 3.3 %collective-permute-done.13.refs_1_ = bf16[2,384,384]{2,1,0:T(8,128)(2,1)S(1)} collective-permute-done((bf16[2,384,384]{2,1,0:T(8,128)(2,1)S(1)}, bf16[2,384,384]{2,1,0:T(8,128)(2,1)S(1)}, u32[]{:S(2)}, u32[]{:S(2)}) %collective-permute-start.13) | collective-permute-done | bytes 589856 | tf_op jit(solution)/shard_map/ppermute | solution.py:1168
  178.5 11.0 %collective-permute-done.15.refs_2_ = bf16[2,384,384]{2,1,0:T(8,128)(2,1)S(1)} collective-permute-done((bf16[2,384,384]{2,1,0:T(8,128)(2,1)S(1)}, bf16[2,384,384]{2,1,0:T(8,128)(2,1)S(1)}, u32[]{:S(2)}, u32[]{:S(2)}) %collective-permute-start.15) | collective-permute-done | bytes 589856 | tf_op jit(solution)/shard_map/ppermute | solution.py:1171
  192.4 2.8 %token_grad.1.after_ref.refs_1_ = bf16[544,384]{1,0:T(8,128)(2,1)S(1)} custom-call(bf16[2,384,384]{2,1,0:T(8,128)(2,1)} %choose.3.after_ref.mine_ref, s32[4]{0:T(128)S(1)} %pad_add_fusion.where_ref.refs_0_.refs_1_, bf16[544,384]{1,0:T(8,128)(2,1)} %get-tuple-element.113.refs_1_, bf16[544,384]{1,0:T(8,128)(2,1)S(1)} %collective-permute-done.16.refs_2_, ...), custom_call_target="tpu_custom_call" | custom-call | flops 30000001024 | bytes 10000 | tf_op jit(solution)/shard_map/token_grad/pallas_call | solution.py:394
  195.3 3.1 %collective-permute-start.20 = (bf16[544,384]{1,0:T(8,128)(2,1)S(1)}, bf16[544,384]{1,0:T(8,128)(2,1)S(1)}, u32[]{:S(2)}, u32[]{:S(2)}) collective-permute-start(bf16[544,384]{1,0:T(8,128)(2,1)S(1)} %token_grad.1.after_ref.refs_1_), channel_id=1, source_target_pairs={{0,2},{2,0},{1,3},{3,1},{4,6},{6,4},{5,7},{7,5},{8,10},{10,8},{9,1... | collective-permute-start | bytes 1253384 | tf_op jit(solution)/shard_map/ppermute | solution.py:1135
  201.9 14.8 %all-to-all-start.1 = ((bf16[16,56,384]{2,1,0:T(8,128)(2,1)}), bf16[16,56,384]{2,1,0:T(8,128)(2,1)}, u32[]{:S(2)}, u32[]{:S(2)}) async-start(bf16[16,56,384]{2,1,0:T(8,128)(2,1)} %total.1.after_ref), calls=%async_computation.1 | async-start | bytes 1376256 | tf_op jit(solution)/shard_map/all_to_all | solution.py:1272
  219.9 2.6 join.2.after_ref
  223.3 6.2 %collective-permute-done.21.refs_2_ = bf16[2,384,384]{2,1,0:T(8,128)(2,1)S(1)} collective-permute-done((bf16[2,384,384]{2,1,0:T(8,128)(2,1)S(1)}, bf16[2,384,384]{2,1,0:T(8,128)(2,1)S(1)}, u32[]{:S(2)}, u32[]{:S(2)}) %collective-permute-start.21) | collective-permute-done | bytes 589856 | tf_op jit(solution)/shard_map/ppermute | solution.py:1171
  230.9 2.4 collective-permute-start.26
  235.2 2.5 summed_end.1
  237.7 2.8 %expert_end.3 = (f32[8,384,384]{2,1,0:T(8,128)}, f32[8,384,384]{2,1,0:T(8,128)}) custom-call(s32[4]{0:T(128)S(1)} %pad_add_fusion.where_ref.refs_0_.refs_1_, bf16[2,384,384]{2,1,0:T(8,128)(2,1)} %choose.3.after_ref.mine_ref, bf16[2,384,384]{2,1,0:T(8,128)(2,1)} %collective-permute-done.24.other_ref, ...), custom_call_target="tpu_custom_call", output_to_operand_aliasing={{0}: (3, {}), {1}: (4, {})} | custom-call | flops 30000001024 | bytes 10000 | tf_op jit(solution)/shard_map/expert_end/pallas_call | solution.py:394
  240.5 2.8 %expert_end.4 = (f32[8,384,384]{2,1,0:T(8,128)}, f32[8,384,384]{2,1,0:T(8,128)}) custom-call(s32[4]{0:T(128)S(1)} %pad_add_fusion.where_ref.refs_0_.refs_1_, bf16[2,384,384]{2,1,0:T(8,128)(2,1)} %choose.4.after_ref.mine_ref, bf16[2,384,384]{2,1,0:T(8,128)(2,1)} %collective-permute-done.23.other_ref, ...), custom_call_target="tpu_custom_call", output_to_operand_aliasing={{0}: (3, {}), {1}: (4, {})} | custom-call | flops 30000001024 | bytes 10000 | tf_op jit(solution)/shard_map/expert_end/pallas_call | solution.py:394
  243.3 3.0 %attn_end.1 = (f32[3,384,384]{2,1,0:T(8,128)}, f32[384,384]{1,0:T(8,128)}, f32[1,384]{1,0:T(1,128)}, f32[1,384]{1,0:T(1,128)}, f32[8,384]{1,0:T(8,128)}) custom-call(f32[8,384,384]{2,1,0:T(8,128)} %get-tuple-element.120.after_ref.refs_0_, s32[4]{0:T(128)S(1)} %pad_add_fusion.where_ref.refs_0_.refs_1_, bf16[896,384]{1,0:T(8,128)(2,1)} %bitcast.13.refs_1_, ...), custom_call_target="tpu_custom_call" | custom-call | flops 40000000000 | bytes 10000 | tf_op jit(solution)/shard_map/attn_end/pallas_call | solution.py:394
  248.9 3.2 %collective-permute-done.26.other_ref = bf16[2,384,384]{2,1,0:T(8,128)(2,1)} collective-permute-done((bf16[2,384,384]{2,1,0:T(8,128)(2,1)}, bf16[2,384,384]{2,1,0:T(8,128)(2,1)}, u32[]{:S(2)}, u32[]{:S(2)}) %collective-permute-start.26) | collective-permute-done | bytes 589856 | tf_op jit(solution)/shard_map/ppermute | solution.py:1135
  252.1 2.7 %expert_end.5 = (f32[8,384,384]{2,1,0:T(8,128)}, f32[8,384,384]{2,1,0:T(8,128)}) custom-call(s32[4]{0:T(128)S(1)} %pad_add_fusion.where_ref.refs_0_.refs_1_, bf16[2,384,384]{2,1,0:T(8,128)(2,1)} %choose.5.after_ref.mine_ref, bf16[2,384,384]{2,1,0:T(8,128)(2,1)} %collective-permute-done.26.other_ref, ...), custom_call_target="tpu_custom_call", output_to_operand_aliasing={{0}: (3, {}), {1}: (4, {})} | custom-call | flops 30000001024 | bytes 10000 | tf_op jit(solution)/shard_map/expert_end/pallas_call | solution.py:394
  (126 shorter events, 47.4 us)
Async XLA Ops:
  7.2 228.0 %all-reduce.4.cloned.1.call-start = ((), (), s32[]{:S(2)}) async-start(), calls=%async_computation.2 | async-start | bytes 2359296 | tf_op jit(solution)/shard_map/psum | solution.py:1202
  7.9 31.3 %copy-start.3 = (f32[1,384]{1,0:T(1,128)}, f32[1,384]{1,0:T(1,128)S(1)}, u32[]{:S(2)}) copy-start(f32[1,384]{1,0:T(1,128)S(1)} %reshape.60.gain1_ref.refs_5_.refs_4_) | copy-start | bytes 4612
  9.4 29.9 %copy-start = (bf16[3,384,192]{2,1,0:T(8,128)(2,1)}, bf16[3,384,192]{2,1,0:T(8,128)(2,1)S(1)}, u32[]{:S(2)}) copy-start(bf16[3,384,192]{2,1,0:T(8,128)(2,1)S(1)} %dynamic-slice_bitcast_fusion.w3_ref.refs_12_) | copy-start | bytes 1327108
  39.2 2.4 collective-permute-start
  49.9 3.9 %collective-permute-start.1 = (bf16[1216,768]{1,0:T(8,128)(2,1)S(1)}, bf16[1216,768]{1,0:T(8,128)(2,1)S(1)}, u32[]{:S(2)}, u32[]{:S(2)}) collective-permute-start(bf16[1216,768]{1,0:T(8,128)(2,1)S(1)} %get-tuple-element.74), channel_id=1, source_target_pairs={{0,1},{1,0},{2,3},{3,2},{4,5},{5,4},{6,7},{7,6},{8,9},{9,8},{10,11... | collective-permute-start | bytes 5603336 | tf_op jit(solution)/shard_map/ppermute | solution.py:1135
  75.3 5.7 %collective-permute-start.2 = (bf16[1216,768]{1,0:T(8,128)(2,1)S(1)}, bf16[1216,768]{1,0:T(8,128)(2,1)}, u32[]{:S(2)}, u32[]{:S(2)}) collective-permute-start(bf16[1216,768]{1,0:T(8,128)(2,1)S(1)} %get-tuple-element.76.after_ref), channel_id=1, source_target_pairs={{0,1},{1,0},{2,3},{3,2},{4,5},{5,4},{6,7},{7,6},{8,9},{9,8},{10,11... | collective-permute-start | bytes 5603336 | tf_op jit(solution)/shard_map/ppermute | solution.py:1135
  75.6 26.0 %collective-permute-start.4 = (bf16[2,384,384]{2,1,0:T(8,128)(2,1)}, bf16[2,384,384]{2,1,0:T(8,128)(2,1)S(1)}, u32[]{:S(2)}, u32[]{:S(2)}) collective-permute-start(bf16[2,384,384]{2,1,0:T(8,128)(2,1)} %get-tuple-element.82), channel_id=1, source_target_pairs={{0,4},{4,0},{8,12},{12,8},{16,20},{20,16},{24,28},{28,24},{1,5},{5... | collective-permute-start | bytes 1769480 | tf_op jit(solution)/shard_map/ppermute | solution.py:1135
  78.4 40.5 %collective-permute-start.6 = (bf16[2,384,384]{2,1,0:T(8,128)(2,1)}, bf16[2,384,384]{2,1,0:T(8,128)(2,1)}, u32[]{:S(2)}, u32[]{:S(2)}) collective-permute-start(bf16[2,384,384]{2,1,0:T(8,128)(2,1)} %get-tuple-element.93), channel_id=1, source_target_pairs={{0,4},{4,0},{8,12},{12,8},{16,20},{20,16},{24,28},{28,24},{1,5},{5... | collective-permute-start | bytes 1769480 | tf_op jit(solution)/shard_map/ppermute | solution.py:1135
  78.4 68.4 %collective-permute-start.8 = (bf16[2,384,384]{2,1,0:T(8,128)(2,1)}, bf16[2,384,384]{2,1,0:T(8,128)(2,1)}, u32[]{:S(2)}, u32[]{:S(2)}) collective-permute-start(bf16[2,384,384]{2,1,0:T(8,128)(2,1)} %get-tuple-element.110), channel_id=1, source_target_pairs={{0,4},{4,0},{8,12},{12,8},{16,20},{20,16},{24,28},{28,24},{1,5},{5... | collective-permute-start | bytes 1769480 | tf_op jit(solution)/shard_map/ppermute | solution.py:1135
  85.2 11.1 %collective-permute-start.3 = (bf16[544,384]{1,0:T(8,128)(2,1)S(1)}, bf16[544,384]{1,0:T(8,128)(2,1)S(1)}, u32[]{:S(2)}, u32[]{:S(2)}) collective-permute-start(bf16[544,384]{1,0:T(8,128)(2,1)S(1)} %get-tuple-element.77.after_ref), channel_id=1, source_target_pairs={{0,2},{2,0},{1,3},{3,1},{4,6},{6,4},{5,7},{7,5},{8,10},{10,8},{9,1... | collective-permute-start | bytes 1253384 | tf_op jit(solution)/shard_map/ppermute | solution.py:1135
  99.9 7.8 %collective-permute-start.5 = (bf16[544,384]{1,0:T(8,128)(2,1)S(1)}, bf16[544,384]{1,0:T(8,128)(2,1)S(1)}, u32[]{:S(2)}, u32[]{:S(2)}) collective-permute-start(bf16[544,384]{1,0:T(8,128)(2,1)S(1)} %get-tuple-element.83.refs_2_), channel_id=1, source_target_pairs={{0,1},{1,0},{2,3},{3,2},{4,5},{5,4},{6,7},{7,6},{8,9},{9,8},{10,11... | collective-permute-start | bytes 1253384 | tf_op jit(solution)/shard_map/ppermute | solution.py:1135
  100.0 70.0 %collective-permute-start.12 = (bf16[1088,384]{1,0:T(8,128)(2,1)}, bf16[1088,384]{1,0:T(8,128)(2,1)}, u32[]{:S(2)}, u32[]{:S(2)}) collective-permute-start(bf16[1088,384]{1,0:T(8,128)(2,1)} %get-tuple-element.80.after_ref.refs_1_), channel_id=1, source_target_pairs={{0,2},{2,0},{1,3},{3,1},{4,6},{6,4},{5,7},{7,5},{8,10},{10,8},{9,1... | collective-permute-start | bytes 2506760 | tf_op jit(solution)/shard_map/ppermute | solution.py:1135
  102.6 21.0 %collective-permute-start.7 = (bf16[2,384,384]{2,1,0:T(8,128)(2,1)}, bf16[2,384,384]{2,1,0:T(8,128)(2,1)}, u32[]{:S(2)}, u32[]{:S(2)}) collective-permute-start(bf16[2,384,384]{2,1,0:T(8,128)(2,1)} %add.35.after_ref.refs_0_), channel_id=1, source_target_pairs={{0,8},{4,12},{24,16},{28,20},{1,9},{5,13},{25,17},{29,21},{2,10},{... | collective-permute-start | bytes 1769480 | tf_op jit(solution)/shard_map/ppermute | solution.py:1168
  121.3 42.4 %collective-permute-start.10 = (bf16[2,384,384]{2,1,0:T(8,128)(2,1)}, bf16[2,384,384]{2,1,0:T(8,128)(2,1)}, u32[]{:S(2)}, u32[]{:S(2)}) collective-permute-start(bf16[2,384,384]{2,1,0:T(8,128)(2,1)} %add.36.after_ref.refs_0_), channel_id=1, source_target_pairs={{0,8},{4,12},{24,16},{28,20},{1,9},{5,13},{25,17},{29,21},{2,10},{... | collective-permute-start | bytes 1769480 | tf_op jit(solution)/shard_map/ppermute | solution.py:1168
  125.8 35.3 %collective-permute-start.9 = (bf16[2,384,384]{2,1,0:T(8,128)(2,1)}, bf16[2,384,384]{2,1,0:T(8,128)(2,1)}, u32[]{:S(2)}, u32[]{:S(2)}) collective-permute-start(bf16[2,384,384]{2,1,0:T(8,128)(2,1)} %add.37.after_ref.refs_0_), channel_id=1, source_target_pairs={{8,16},{12,20},{16,8},{20,12},{9,17},{13,21},{17,9},{21,13},{10,18... | collective-permute-start | bytes 1769480 | tf_op jit(solution)/shard_map/ppermute | solution.py:1170
  142.6 23.2 %collective-permute-start.11 = (bf16[1088,384]{1,0:T(8,128)(2,1)S(1)}, bf16[1088,384]{1,0:T(8,128)(2,1)S(1)}, u32[]{:S(2)}, u32[]{:S(2)}) collective-permute-start(bf16[1088,384]{1,0:T(8,128)(2,1)S(1)} %get-tuple-element.101.after_ref), channel_id=1, source_target_pairs={{0,1},{1,0},{2,3},{3,2},{4,5},{5,4},{6,7},{7,6},{8,9},{9,8},{10,11... | collective-permute-start | bytes 2506760 | tf_op jit(solution)/shard_map/ppermute | solution.py:1135
  148.1 28.1 %collective-permute-start.13 = (bf16[2,384,384]{2,1,0:T(8,128)(2,1)S(1)}, bf16[2,384,384]{2,1,0:T(8,128)(2,1)S(1)}, u32[]{:S(2)}, u32[]{:S(2)}) collective-permute-start(bf16[2,384,384]{2,1,0:T(8,128)(2,1)S(1)} %add.38.after_ref.refs_0_), channel_id=1, source_target_pairs={{0,8},{4,12},{24,16},{28,20},{1,9},{5,13},{25,17},{29,21},{2,10},{... | collective-permute-start | bytes 1769480 | tf_op jit(solution)/shard_map/ppermute | solution.py:1168
  156.1 43.7 %all-to-all-start = ((bf16[16,56,384]{2,1,0:T(8,128)(2,1)}), bf16[16,56,384]{2,1,0:T(8,128)(2,1)}, u32[]{:S(2)}, u32[]{:S(2)}) async-start(bf16[16,56,384]{2,1,0:T(8,128)(2,1)} %bitcast.12), calls=%async_computation | async-start | bytes 1376256 | tf_op jit(solution)/shard_map/all_to_all | solution.py:1256
  162.4 27.0 %collective-permute-start.15 = (bf16[2,384,384]{2,1,0:T(8,128)(2,1)S(1)}, bf16[2,384,384]{2,1,0:T(8,128)(2,1)S(1)}, u32[]{:S(2)}, u32[]{:S(2)}) collective-permute-start(bf16[2,384,384]{2,1,0:T(8,128)(2,1)S(1)} %add.39.after_ref.refs_1_), channel_id=1, source_target_pairs={{8,0},{12,4},{16,24},{20,28},{9,1},{13,5},{17,25},{21,29},{10,2},{... | collective-permute-start | bytes 1769480 | tf_op jit(solution)/shard_map/ppermute | solution.py:1171
  165.1 11.8 %collective-permute-start.14 = (bf16[2,384,384]{2,1,0:T(8,128)(2,1)S(1)}, bf16[2,384,384]{2,1,0:T(8,128)(2,1)S(1)}, u32[]{:S(2)}, u32[]{:S(2)}) collective-permute-start(bf16[2,384,384]{2,1,0:T(8,128)(2,1)S(1)} %add.40.after_ref.refs_0_), channel_id=1, source_target_pairs={{8,16},{12,20},{16,8},{20,12},{9,17},{13,21},{17,9},{21,13},{10,18... | collective-permute-start | bytes 1769480 | tf_op jit(solution)/shard_map/ppermute | solution.py:1170
  168.1 24.3 %collective-permute-start.16 = (bf16[544,384]{1,0:T(8,128)(2,1)S(1)}, bf16[544,384]{1,0:T(8,128)(2,1)S(1)}, u32[]{:S(2)}, u32[]{:S(2)}) collective-permute-start(bf16[544,384]{1,0:T(8,128)(2,1)S(1)} %get-tuple-element.112.after_ref), channel_id=1, source_target_pairs={{0,2},{2,0},{1,3},{3,1},{4,6},{6,4},{5,7},{7,5},{8,10},{10,8},{9,1... | collective-permute-start | bytes 1253384 | tf_op jit(solution)/shard_map/ppermute | solution.py:1135
  172.9 47.1 %collective-permute-start.19 = (bf16[1088,384]{1,0:T(8,128)(2,1)}, bf16[1088,384]{1,0:T(8,128)(2,1)}, u32[]{:S(2)}, u32[]{:S(2)}) collective-permute-start(bf16[1088,384]{1,0:T(8,128)(2,1)} %block_out.1.after_ref.refs_1_), channel_id=1, source_target_pairs={{0,1},{1,0},{2,3},{3,2},{4,5},{5,4},{6,7},{7,6},{8,9},{9,8},{10,11... | collective-permute-start | bytes 2506760 | tf_op jit(solution)/shard_map/ppermute | solution.py:1135
  176.3 22.1 %collective-permute-start.17 = (bf16[2,384,384]{2,1,0:T(8,128)(2,1)S(1)}, bf16[2,384,384]{2,1,0:T(8,128)(2,1)S(1)}, u32[]{:S(2)}, u32[]{:S(2)}) collective-permute-start(bf16[2,384,384]{2,1,0:T(8,128)(2,1)S(1)} %add.41.after_ref.refs_0_), channel_id=1, source_target_pairs={{8,16},{12,20},{16,8},{20,12},{9,17},{13,21},{17,9},{21,13},{10,18... | collective-permute-start | bytes 1769480 | tf_op jit(solution)/shard_map/ppermute | solution.py:1170
  177.2 39.5 %collective-permute-start.18 = (bf16[2,384,384]{2,1,0:T(8,128)(2,1)S(1)}, bf16[2,384,384]{2,1,0:T(8,128)(2,1)S(1)}, u32[]{:S(2)}, u32[]{:S(2)}) collective-permute-start(bf16[2,384,384]{2,1,0:T(8,128)(2,1)S(1)} %add.42.after_ref.refs_1_), channel_id=1, source_target_pairs={{8,0},{12,4},{16,24},{20,28},{9,1},{13,5},{17,25},{21,29},{10,2},{... | collective-permute-start | bytes 1769480 | tf_op jit(solution)/shard_map/ppermute | solution.py:1171
  190.8 46.8 %collective-permute-start.24 = (bf16[2,384,384]{2,1,0:T(8,128)(2,1)}, bf16[2,384,384]{2,1,0:T(8,128)(2,1)}, u32[]{:S(2)}, u32[]{:S(2)}) collective-permute-start(bf16[2,384,384]{2,1,0:T(8,128)(2,1)} %choose.3.after_ref.mine_ref), channel_id=1, source_target_pairs={{0,4},{4,0},{8,12},{12,8},{16,20},{20,16},{24,28},{28,24},{1,5},{5... | collective-permute-start | bytes 1769480 | tf_op jit(solution)/shard_map/ppermute | solution.py:1135
  195.3 27.3 %collective-permute-start.20 = (bf16[544,384]{1,0:T(8,128)(2,1)S(1)}, bf16[544,384]{1,0:T(8,128)(2,1)S(1)}, u32[]{:S(2)}, u32[]{:S(2)}) collective-permute-start(bf16[544,384]{1,0:T(8,128)(2,1)S(1)} %token_grad.1.after_ref.refs_1_), channel_id=1, source_target_pairs={{0,2},{2,0},{1,3},{3,1},{4,6},{6,4},{5,7},{7,5},{8,10},{10,8},{9,1... | collective-permute-start | bytes 1253384 | tf_op jit(solution)/shard_map/ppermute | solution.py:1135
  198.5 31.0 %collective-permute-start.21 = (bf16[2,384,384]{2,1,0:T(8,128)(2,1)S(1)}, bf16[2,384,384]{2,1,0:T(8,128)(2,1)S(1)}, u32[]{:S(2)}, u32[]{:S(2)}) collective-permute-start(bf16[2,384,384]{2,1,0:T(8,128)(2,1)S(1)} %add.43.after_ref.refs_1_), channel_id=1, source_target_pairs={{8,0},{12,4},{16,24},{20,28},{9,1},{13,5},{17,25},{21,29},{10,2},{... | collective-permute-start | bytes 1769480 | tf_op jit(solution)/shard_map/ppermute | solution.py:1171
  201.9 38.6 %all-to-all-start.1 = ((bf16[16,56,384]{2,1,0:T(8,128)(2,1)}), bf16[16,56,384]{2,1,0:T(8,128)(2,1)}, u32[]{:S(2)}, u32[]{:S(2)}) async-start(bf16[16,56,384]{2,1,0:T(8,128)(2,1)} %total.1.after_ref), calls=%async_computation.1 | async-start | bytes 1376256 | tf_op jit(solution)/shard_map/all_to_all | solution.py:1272
  218.1 22.4 %collective-permute-start.23 = (bf16[2,384,384]{2,1,0:T(8,128)(2,1)}, bf16[2,384,384]{2,1,0:T(8,128)(2,1)}, u32[]{:S(2)}, u32[]{:S(2)}) collective-permute-start(bf16[2,384,384]{2,1,0:T(8,128)(2,1)} %choose.4.after_ref.mine_ref), channel_id=1, source_target_pairs={{0,4},{4,0},{8,12},{12,8},{16,20},{20,16},{24,28},{28,24},{1,5},{5... | collective-permute-start | bytes 1769480 | tf_op jit(solution)/shard_map/ppermute | solution.py:1135
  223.2 10.2 %collective-permute-start.22 = (bf16[1088,384]{1,0:T(8,128)(2,1)S(1)}, bf16[1088,384]{1,0:T(8,128)(2,1)S(1)}, u32[]{:S(2)}, u32[]{:S(2)}) collective-permute-start(bf16[1088,384]{1,0:T(8,128)(2,1)S(1)} %weave.1.after_ref.refs_1_), channel_id=1, source_target_pairs={{0,1},{1,0},{2,3},{3,2},{4,5},{5,4},{6,7},{7,6},{8,9},{9,8},{10,11... | collective-permute-start | bytes 2506760 | tf_op jit(solution)/shard_map/ppermute | solution.py:1135
  230.9 21.1 %collective-permute-start.26 = (bf16[2,384,384]{2,1,0:T(8,128)(2,1)}, bf16[2,384,384]{2,1,0:T(8,128)(2,1)}, u32[]{:S(2)}, u32[]{:S(2)}) collective-permute-start(bf16[2,384,384]{2,1,0:T(8,128)(2,1)} %choose.5.after_ref.mine_ref), channel_id=1, source_target_pairs={{0,4},{4,0},{8,12},{12,8},{16,20},{20,16},{24,28},{28,24},{1,5},{5... | collective-permute-start | bytes 1769480 | tf_op jit(solution)/shard_map/ppermute | solution.py:1135
  240.4 2.9 %collective-permute-start.25 = (bf16[896,384]{1,0:T(8,128)(2,1)}, bf16[896,384]{1,0:T(8,128)(2,1)S(1)}, u32[]{:S(2)}, u32[]{:S(2)}) collective-permute-start(bf16[896,384]{1,0:T(8,128)(2,1)} %bitcast.13.refs_1_), channel_id=1, source_target_pairs={{0,1},{1,0},{2,3},{3,2},{4,5},{5,4},{6,7},{7,6},{8,9},{9,8},{10,11... | collective-permute-start | bytes 2064392 | tf_op jit(solution)/shard_map/ppermute | solution.py:1135
  (23 other events, 202.2 us)
Sparse Core Ops, SparseCore 0:
  80.5 89.8 all-reduce.3

commit v2 on v1

--- a/solution.py
+++ b/solution.py
@@ -1109,10 +1109,10 @@
         gqkv_ref[i] = part
         product = product + part * wqkv_ref[i].astype(F32)
     gproj_ref[...] = jnp.concatenate([low[3 * share : 4 * share], high[3 * share : 4 * share]], 0)
-    g1_ref[...] = jnp.sum(product.T, 0, keepdims=True) / gain1_ref[...]
+    g1_ref[...] = (jnp.sum(product.T, 0, keepdims=True) / gain1_ref[...])[0]
     small = low[4 * share : 4 * share + 16] + high[4 * share : 4 * share + 16]
     groute_ref[...] = small[0:8]
-    g2_ref[...] = small[8:9]
+    g2_ref[...] = small[8]
 
 
 def run_attn_end(where, mine, other, wqkv, gain1, after):
@@ -1120,8 +1120,8 @@
     outs = (
         sds((3, width, width), F32),
         sds((width, width), F32),
-        sds((1, width), F32),
-        sds((1, width), F32),
+        sds((width,), F32),
+        sds((width,), F32),
         sds((8, width), F32),
     )
     return call(
@@ -1248,53 +1248,55 @@
     last = ga_c, VMEM_SPEC
     last = first_step(1, last)
     last = line_step(0, 1, last)
+    last = first_step(2, last)
     hkeep, hsend, dqt, dkt, dvt = run_back_second(own, lengths, where, k, kt, v, *state, w3, last)
     hgot = swap(hsend, "lo", 1)
+    last = hsend, ANY_SPEC
+    last = line_step(0, 2, last)
+    last = line_step(1, 1, last)
+    last = line_step(2, 1, last)
     pay_rows = up(2 * width + 16, 8 * lax.axis_size(("wide", "hi")))
-    pay = run_weights(pay_rows, dqt, dkt, dvt, ga_c, hid_c, ho_c, hid, groute, gain2_part, (hsend, ANY_SPEC))
+    pay = run_weights(pay_rows, dqt, dkt, dvt, ga_c, hid_c, ho_c, hid, groute, gain2_part, last)
     share = pay_rows // lax.axis_size(("wide", "hi"))
     pay_got = lax.all_to_all(pay.reshape(-1, share, width), ("wide", "hi"), 0, 0)
-    last = first_step(2, (pay, ANY_SPEC))
-    last = line_step(0, 2, last)
-    last = line_step(1, 1, last)
+    last = pay, ANY_SPEC
     hk, hs = run_split(where, hkeep, hgot, last)
     hs_got = swap(hs, "hi", 1)
     out_own = run_out(mid, ex, ex_got, (hs, ANY_SPEC))
     out_oth = swap(out_own, "lo", 1)
-    last = line_step(2, 1, (out_own, ANY_SPEC))
-    last = line_step(1, 2, last)
+    last = line_step(1, 2, (out_own, ANY_SPEC))
     last = last_step(0, last)
+    last = line_step(2, 2, last)
     token_rows = run_tokens(where, hk, hs_got, gmid, tokens, gain1, last)
     token_got = swap(token_rows, "hi", 1)
-    last = line_step(2, 2, (token_rows, ANY_SPEC))
+    last = last_step(1, (token_rows, ANY_SPEC))
     pay_got = run_total(pay_got, last)
     last = pay_got, ANY_SPEC
     pay_got = lax.all_to_all(pay_got, ("wide", "hi"), 0, 0).reshape(pay.shape)
-    last = last_step(1, last)
     layer_out = run_join(where, out_own, out_oth, last)
     token_own = run_weave(where, token_rows, token_got, (layer_out, FAR_ANY))
     token_oth = swap(token_own, "lo", 1)
     last = last_step(2, (token_own, ANY_SPEC))
-    grad_tokens = run_join(where, token_own, token_oth, last)
-    before = run_summed_end(total_a, w_in.shape, w_out.shape, (grad_tokens, FAR_ANY))
+    before = run_summed_end(total_a, w_in.shape, w_out.shape, last)
     at = PARTS[0]
-    for i, size in enumerate(PARTS[1:]):
-        if i == len(PARTS) - 2:
-            pay_oth = swap(pay_got, "lo", 1)
-            grad_qkv, grad_proj, grad_norm1, grad_norm2, route_t = run_attn_end(
-                where, pay_got, pay_oth, wqkv, gain1, (before[0], FAR_ANY)
-            )
-        before = run_expert_end(at, where, sums[i], others[i], w_in.shape, w_out.shape, before)
-        at += size
-    grad_in, grad_out = before
+    before = run_expert_end(at, where, sums[0], others[0], w_in.shape, w_out.shape, before)
+    grad_tokens = run_join(where, token_own, token_oth, (before[0], FAR_ANY))
+    before = run_expert_end(at + PARTS[1], where, sums[1], others[1], w_in.shape, w_out.shape, before)
+    pay_oth = swap(pay_got, "lo", 1)
+    grad_qkv, grad_proj, grad_norm1, grad_norm2, route_t = run_attn_end(
+        where, pay_got, pay_oth, wqkv, gain1, (before[0], FAR_ANY)
+    )
+    grad_in, grad_out = run_expert_end(
+        at + PARTS[1] + PARTS[2], where, sums[2], others[2], w_in.shape, w_out.shape, before
+    )
 
     return (
         layer_out,
         grad_tokens,
         grad_qkv.transpose(1, 0, 2),
         grad_proj,
-        grad_norm1.reshape(width),
-        grad_norm2.reshape(width),
+        grad_norm1,
+        grad_norm2,
         route_t.T,
         grad_in,
         grad_out,

time: 263 us -> 254 us (0.966)
  starting transfers between devices: 62.1 us -> 51.4 us
  Pallas kernels: 143 us -> 151 us
  waiting for transfers between devices: 33.9 us -> 31.2 us
    all_to_all x1, starting transfers between devices: 14.8 us -> 4.46 us  [on_device(): pay_got = lax.all_to_all(pay_got, ('wide', 'hi'), 0, 0).reshape(pay.shape)]
    pallas_call x35, Pallas kernels: 143 us -> 151 us  [run_on(): return run(*placed)]
    ppermute x3, waiting for transfers between devices: 17.2 us -> 10.2 us  [wide_step(): return lax.ppermute(value, 'wide', [(b, a) for a, b in inward])]
    all_to_all x1, starting transfers between devices: 4.95 us -> 9.46 us  [on_device(): lax.all_to_all(pay.reshape(-1, share, width), ('wide', 'hi'), 0, 0)]
    ppermute x18, waiting for transfers between devices: 13.3 us -> 17.6 us  [swap(): return lax.ppermute(value, axis, [(i, i ^ mask) for i in range(size)])]
    ppermute x18, starting transfers between devices: 20.2 us -> 16 us  [swap(): return lax.ppermute(value, axis, [(i, i ^ mask) for i in range(size)])]
    all_to_all x1, waiting for transfers between devices: 0.01 us -> 3.31 us  [on_device(): pay_got = lax.all_to_all(pay_got, ('wide', 'hi'), 0, 0).reshape(pay.shape)]
    ppermute x3, waiting for transfers between devices: 3.26 us -> 0.01 us  [wide_step(): return lax.ppermute(value, 'wide', inward)]
  transfers between devices with their start and end apart: 30 -> 30, of which waited for: 7 -> 9; matrix products, arithmetic and copies ran while one was open for 1% -> 0% of each run, Pallas kernels for 32% -> 36%
where the time goes in v2:
time: 254 us; the launch traced here: 253 us
  Pallas kernels  151 us (59%)
  starting transfers between devices  51.4 us (20%)
  waiting for transfers between devices  31.2 us (12%)
  between operations  14.6 us (6%)
  local copies, waits for them, and re-layouts  5.19 us (2%)
    pallas_call x35, Pallas kernels, run_on(): return run(*placed)  151 us
    ppermute x18, waiting for transfers between devices, swap(): return lax.ppermute(value, axis, [(i, i ^ mask) for i in range(size)])  17.6 us
    ppermute x18, starting transfers between devices, swap(): return lax.ppermute(value, axis, [(i, i ^ mask) for i in range(size)])  16 us
    ppermute x3, starting transfers between devices, wide_step(): return lax.ppermute(value, 'wide', inward)  12.9 us
    ppermute x3, waiting for transfers between devices, wide_step(): return lax.ppermute(value, 'wide', [(b, a) for a, b in inward])  10.2 us
    all_to_all x1, starting transfers between devices, on_device(): lax.all_to_all(pay.reshape(-1, share, width), ('wide', 'hi'), 0, 0)  9.46 us
  transfers between devices with their start and end apart: 30, of which 9 were waited for; matrix products, arithmetic and copies ran while one was open for 0% of the time, Pallas kernels for 36%

profile of v2, /device:TPU:0, one launch (start us, length us, event | category | flops | bytes accessed | tf_op | source)
XLA Modules:
  0.0 253.3 jit_solution(8151994802526710675)
XLA Ops:
  10.2 29.1 %front.1 = (bf16[2560,384]{1,0:T(8,128)(2,1)}, bf16[2560,256]{1,0:T(8,128)(2,1)}, bf16[192,2560]{1,0:T(8,128)(2,1)}, bf16[2560,256]{1,0:T(8,128)(2,1)}, bf16[230...) custom-call(s32[1,8]{1,0:T(1,128)S(1)} %copy-done.10, ...), custom_call_target="tpu_custom_call" | custom-call | flops 330000007168 | bytes 10000 | tf_op jit(solution)/shard_map/front/pallas_call | solution.py:394
  41.7 8.2 %mid.1 = (f32[1088,384]{1,0:T(8,128)}, bf16[1216,768]{1,0:T(8,128)(2,1)S(1)}, bf16[1216,768]{1,0:T(8,128)(2,1)S(1)}) custom-call(s32[4]{0:T(128)S(1)} %pad_add_fusion.where_ref.refs_0_.refs_1_, bf16[1088,384]{1,0:T(8,128)(2,1)S(1)} %get-tuple-element.69.after_ref.keep_ref, bf16[1088,384]{1,0:T(8,128)(2,1)S(1)} %collective-permute-done.got_ref, ...), custom_call_target="tpu_custom_call" | custom-call | flops 89999998976 | bytes 10000 | tf_op jit(solution)/shard_map/mid/pallas_call | solution.py:394
  50.3 3.5 %collective-permute-done.1.oth_ref = bf16[1216,768]{1,0:T(8,128)(2,1)S(1)} collective-permute-done((bf16[1216,768]{1,0:T(8,128)(2,1)S(1)}, bf16[1216,768]{1,0:T(8,128)(2,1)S(1)}, u32[]{:S(2)}, u32[]{:S(2)}) %collective-permute-start.1) | collective-permute-done | bytes 1867808 | tf_op jit(solution)/shard_map/ppermute | solution.py:1135
  53.8 20.3 %experts.1 = (bf16[1216,768]{1,0:T(8,128)(2,1)S(1)}, bf16[1216,768]{1,0:T(8,128)(2,1)S(1)}, f32[384,128]{1,0:T(8,128)S(1)}, bf16[2,2,384,384]{3,2,1,0:T(8,128)(2...) custom-call(s32[32,128]{1,0:T(8,128)S(1)} %get-tuple-element.70.plan, ...), custom_call_target="tpu_custom_call" | custom-call | flops 219999993856 | bytes 10000 | tf_op jit(solution)/shard_map/experts/pallas_call | solution.py:394
  80.1 3.2 %unsort.1 = (bf16[544,384]{1,0:T(8,128)(2,1)S(1)}, bf16[544,384]{1,0:T(8,128)(2,1)S(1)}) custom-call(s32[4]{0:T(128)S(1)} %pad_add_fusion.where_ref.refs_0_.refs_1_, bf16[1216,768]{1,0:T(8,128)(2,1)S(1)} %copy-done.15, bf16[1216,768]{1,0:T(8,128)(2,1)} %collective-permute-done.2.got_ref.refs_1_, bf16[2,544,1280]{2,1,0:T(8,128)(2,1)S(1)} %unpick.1.unpick_ref), custom_call_target="tpu_custom_call" | custom-call | flops 40000000000 | bytes 10000 | tf_op jit(solution)/shard_map/unsort/pallas_call | solution.py:394
  83.4 2.9 %collective-permute-start.3 = (bf16[544,384]{1,0:T(8,128)(2,1)S(1)}, bf16[544,384]{1,0:T(8,128)(2,1)S(1)}, u32[]{:S(2)}, u32[]{:S(2)}) collective-permute-start(bf16[544,384]{1,0:T(8,128)(2,1)S(1)} %get-tuple-element.77.after_ref), channel_id=1, source_target_pairs={{0,2},{2,0},{1,3},{3,1},{4,6},{6,4},{5,7},{7,5},{8,10},{10,8},{9,1... | collective-permute-start | bytes 1253384 | tf_op jit(solution)/shard_map/ppermute | solution.py:1135
  86.3 3.2 %unsort_out.1.after_ref.refs_6_ = bf16[1088,384]{1,0:T(8,128)(2,1)S(1)} custom-call(bf16[544,384]{1,0:T(8,128)(2,1)S(1)} %get-tuple-element.77.after_ref, bf16[1216,768]{1,0:T(8,128)(2,1)S(1)} %copy-done.15, bf16[1216,768]{1,0:T(8,128)(2,1)} %collective-permute-done.2.got_ref.refs_1_, f32[8,1152]{1,0:T(8,128)S(1)} %get-tuple-element.72.pos_ref.refs_0_.refs_2_), custom_call_target="tpu_custom_call" | custom-call | flops 30000001024 | bytes 10000 | tf_op jit(solution)/shard_map/unsort_out/pallas_call | solution.py:394
  89.5 6.7 %collective-permute-done.3.refs_2_ = bf16[544,384]{1,0:T(8,128)(2,1)S(1)} collective-permute-done((bf16[544,384]{1,0:T(8,128)(2,1)S(1)}, bf16[544,384]{1,0:T(8,128)(2,1)S(1)}, u32[]{:S(2)}, u32[]{:S(2)}) %collective-permute-start.3) | collective-permute-done | bytes 417824 | tf_op jit(solution)/shard_map/ppermute | solution.py:1135
  96.2 3.6 %mid_back.1 = (f32[544,384]{1,0:T(8,128)}, bf16[544,384]{1,0:T(8,128)(2,1)S(1)}, f32[8,384]{1,0:T(8,128)S(1)}, bf16[1088,384]{1,0:T(8,128)(2,1)}) custom-call(bf16[1088,384]{1,0:T(8,128)(2,1)S(1)} %unsort_out.1.after_ref.refs_6_, s32[4]{0:T(128)S(1)} %pad_add_fusion.where_ref.refs_0_.refs_1_, bf16[544,384]{1,0:T(8,128)(2,1)S(1)} %get-tuple-element.78.refs_1_, ...), custom_call_target="tpu_custom_call" | custom-call | flops 40000000000 | bytes 10000 | tf_op jit(solution)/shard_map/mid_back/pallas_call | solution.py:394
  102.7 5.8 %collective-permute-start.7 = (bf16[2,384,384]{2,1,0:T(8,128)(2,1)}, bf16[2,384,384]{2,1,0:T(8,128)(2,1)}, u32[]{:S(2)}, u32[]{:S(2)}) collective-permute-start(bf16[2,384,384]{2,1,0:T(8,128)(2,1)} %add.33.after_ref.refs_0_), channel_id=1, source_target_pairs={{0,8},{4,12},{24,16},{28,20},{1,9},{5,13},{25,17},{29,21},{2,10},{... | collective-permute-start | bytes 1769480 | tf_op jit(solution)/shard_map/ppermute | solution.py:1168
  108.5 12.6 %back_first.1 = (bf16[1280,384]{1,0:T(8,128)(2,1)S(1)}, bf16[1280,384]{1,0:T(8,128)(2,1)S(1)}, bf16[1280,256]{1,0:T(8,128)(2,1)S(1)}, bf16[1280,256]{1,0:T(8,128...) custom-call(bf16[2,384,384]{2,1,0:T(8,128)(2,1)} %add.33.after_ref.r, ...), custom_call_target="tpu_custom_call" | custom-call | flops 140000002048 | bytes 10000 | tf_op jit(solution)/shard_map/back_first/pallas_call | solution.py:394
  121.1 2.4 add.34.after_ref.refs_0_
  123.5 2.3 collective-permute-start.10
  131.6 4.9 %collective-permute-start.11 = (bf16[2,384,384]{2,1,0:T(8,128)(2,1)}, bf16[2,384,384]{2,1,0:T(8,128)(2,1)}, u32[]{:S(2)}, u32[]{:S(2)}) collective-permute-start(bf16[2,384,384]{2,1,0:T(8,128)(2,1)} %add.36.after_ref.refs_0_), channel_id=1, source_target_pairs={{0,8},{4,12},{24,16},{28,20},{1,9},{5,13},{25,17},{29,21},{2,10},{... | collective-permute-start | bytes 1769480 | tf_op jit(solution)/shard_map/ppermute | solution.py:1168
  136.5 17.7 %back_second.1 = (bf16[1088,384]{1,0:T(8,128)(2,1)}, bf16[1088,384]{1,0:T(8,128)(2,1)S(1)}, bf16[192,1280]{1,0:T(8,128)(2,1)S(1)}, bf16[192,2560]{1,0:T(8,128)(2,1)S(1)}, bf16[192,2560]{1,0:T(8,128)(2,1)S(1)}) custom-call(bf16[2,384,384]{2,1,0:T(8,128)(2,1)} %add.36.after_ref.refs_0_, s32[1,8]{1,0:T(1,128)S(1)} %copy-done.11, ...), custom_call_target="tpu_custom_call" | custom-call | flops 140000002048 | bytes 10000 | tf_op jit(solution)/shard_map/back_second/pallas_call | solution.py:394
  157.0 2.2 add.38.after_ref.refs_0_
  163.7 4.1 %weights.1.after_ref = bf16[896,384]{1,0:T(8,128)(2,1)} custom-call(bf16[2,384,384]{2,1,0:T(8,128)(2,1)S(1)} %add.39.after_ref.refs_0_, bf16[192,1280]{1,0:T(8,128)(2,1)S(1)} %get-tuple-element.104.refs_0_, bf16[192,2560]{1,0:T(8,128)(2,1)S(1)} %get-tuple-element.105.refs_1_, bf16[192,2560]{1,0:T(8,128)(2,1)S(1)} %get-tuple-element.106.refs_2_, ...), custom_call_target="tpu_custom_call" | custom-call | flops 40000000000 | bytes 10000 | tf_op jit(solution)/shard_map/weights/pallas_call | solution.py:394
  167.8 9.5 %all-to-all-start = ((bf16[16,56,384]{2,1,0:T(8,128)(2,1)}), bf16[16,56,384]{2,1,0:T(8,128)(2,1)}, u32[]{:S(2)}, u32[]{:S(2)}) async-start(bf16[16,56,384]{2,1,0:T(8,128)(2,1)} %bitcast.12), calls=%async_computation | async-start | bytes 1376256 | tf_op jit(solution)/shard_map/all_to_all | solution.py:1261
  177.3 2.2 split.1
  191.6 3.1 %collective-permute-done.17.refs_2_ = bf16[544,384]{1,0:T(8,128)(2,1)S(1)} collective-permute-done((bf16[544,384]{1,0:T(8,128)(2,1)S(1)}, bf16[544,384]{1,0:T(8,128)(2,1)S(1)}, u32[]{:S(2)}, u32[]{:S(2)}) %collective-permute-start.17) | collective-permute-done | bytes 417824 | tf_op jit(solution)/shard_map/ppermute | solution.py:1135
  194.7 2.8 %token_grad.1.after_ref.refs_1_ = bf16[544,384]{1,0:T(8,128)(2,1)S(1)} custom-call(bf16[2,384,384]{2,1,0:T(8,128)(2,1)S(1)} %add.41.after_ref.refs_1_, s32[4]{0:T(128)S(1)} %pad_add_fusion.where_ref.refs_0_.refs_1_, bf16[544,384]{1,0:T(8,128)(2,1)} %get-tuple-element.113.refs_1_, bf16[544,384]{1,0:T(8,128)(2,1)S(1)} %collective-permute-done.17.refs_2_, ...), custom_call_target="tpu_custom_call" | custom-call | flops 30000001024 | bytes 10000 | tf_op jit(solution)/shard_map/token_grad/pallas_call | solution.py:394
  199.0 7.0 %collective-permute-done.18.refs_2_ = bf16[2,384,384]{2,1,0:T(8,128)(2,1)S(1)} collective-permute-done((bf16[2,384,384]{2,1,0:T(8,128)(2,1)S(1)}, bf16[2,384,384]{2,1,0:T(8,128)(2,1)S(1)}, u32[]{:S(2)}, u32[]{:S(2)}) %collective-permute-start.18) | collective-permute-done | bytes 589856 | tf_op jit(solution)/shard_map/ppermute | solution.py:1171
  207.5 2.7 %collective-permute-start.24 = (bf16[2,384,384]{2,1,0:T(8,128)(2,1)}, bf16[2,384,384]{2,1,0:T(8,128)(2,1)}, u32[]{:S(2)}, u32[]{:S(2)}) collective-permute-start(bf16[2,384,384]{2,1,0:T(8,128)(2,1)} %choose.4.after_ref.mine_ref), channel_id=1, source_target_pairs={{0,4},{4,0},{8,12},{12,8},{16,20},{20,16},{24,28},{28,24},{1,5},{5... | collective-permute-start | bytes 1769480 | tf_op jit(solution)/shard_map/ppermute | solution.py:1135
  212.2 4.5 %all-to-all-start.1 = ((bf16[16,56,384]{2,1,0:T(8,128)(2,1)}), bf16[16,56,384]{2,1,0:T(8,128)(2,1)}, u32[]{:S(2)}, u32[]{:S(2)}) async-start(bf16[16,56,384]{2,1,0:T(8,128)(2,1)} %total.1.after_ref), calls=%async_computation.1 | async-start | bytes 1376256 | tf_op jit(solution)/shard_map/all_to_all | solution.py:1275
  219.6 3.3 %collective-permute-done.22.refs_2_ = bf16[2,384,384]{2,1,0:T(8,128)(2,1)S(1)} collective-permute-done((bf16[2,384,384]{2,1,0:T(8,128)(2,1)S(1)}, bf16[2,384,384]{2,1,0:T(8,128)(2,1)S(1)}, u32[]{:S(2)}, u32[]{:S(2)}) %collective-permute-start.22) | collective-permute-done | bytes 589856 | tf_op jit(solution)/shard_map/ppermute | solution.py:1171
  224.3 2.5 summed_end.1
  226.8 2.8 %expert_end.3 = (f32[8,384,384]{2,1,0:T(8,128)}, f32[8,384,384]{2,1,0:T(8,128)}) custom-call(s32[4]{0:T(128)S(1)} %pad_add_fusion.where_ref.refs_0_.refs_1_, bf16[2,384,384]{2,1,0:T(8,128)(2,1)} %choose.3.after_ref.mine_ref, bf16[2,384,384]{2,1,0:T(8,128)(2,1)} %collective-permute-done.20.other_ref, ...), custom_call_target="tpu_custom_call", output_to_operand_aliasing={{0}: (3, {}), {1}: (4, {})} | custom-call | flops 30000001024 | bytes 10000 | tf_op jit(solution)/shard_map/expert_end/pallas_call | solution.py:394
  231.3 3.3 %all-to-all-done.1 = bf16[16,56,384]{2,1,0:T(8,128)(2,1)} async-done(((bf16[16,56,384]{2,1,0:T(8,128)(2,1)}), bf16[16,56,384]{2,1,0:T(8,128)(2,1)}, u32[]{:S(2)}, u32[]{:S(2)}) %all-to-all-start.1) | async-done | bytes 688160 | tf_op jit(solution)/shard_map/all_to_all | solution.py:1275
  234.7 2.8 %expert_end.4 = (f32[8,384,384]{2,1,0:T(8,128)}, f32[8,384,384]{2,1,0:T(8,128)}) custom-call(s32[4]{0:T(128)S(1)} %pad_add_fusion.where_ref.refs_0_.refs_1_, bf16[2,384,384]{2,1,0:T(8,128)(2,1)} %choose.4.after_ref.mine_ref, bf16[2,384,384]{2,1,0:T(8,128)(2,1)} %collective-permute-done.24.other_ref, ...), custom_call_target="tpu_custom_call", output_to_operand_aliasing={{0}: (3, {}), {1}: (4, {})} | custom-call | flops 30000001024 | bytes 10000 | tf_op jit(solution)/shard_map/expert_end/pallas_call | solution.py:394
  237.5 3.0 %attn_end.1 = (f32[3,384,384]{2,1,0:T(8,128)}, f32[384,384]{1,0:T(8,128)}, f32[384]{0:T(512)}, f32[384]{0:T(512)}, f32[8,384]{1,0:T(8,128)}) custom-call(f32[8,384,384]{2,1,0:T(8,128)} %get-tuple-element.120.after_ref.refs_0_, s32[4]{0:T(128)S(1)} %pad_add_fusion.where_ref.refs_0_.refs_1_, bf16[896,384]{1,0:T(8,128)(2,1)} %bitcast.13.refs_1_, ...), custom_call_target="tpu_custom_call" | custom-call | flops 40000000000 | bytes 10000 | tf_op jit(solution)/shard_map/attn_end/pallas_call | solution.py:394
  240.6 3.1 %collective-permute-done.26.other_ref = bf16[2,384,384]{2,1,0:T(8,128)(2,1)} collective-permute-done((bf16[2,384,384]{2,1,0:T(8,128)(2,1)}, bf16[2,384,384]{2,1,0:T(8,128)(2,1)}, u32[]{:S(2)}, u32[]{:S(2)}) %collective-permute-start.26) | collective-permute-done | bytes 589856 | tf_op jit(solution)/shard_map/ppermute | solution.py:1135
  243.7 2.7 %expert_end.5 = (f32[8,384,384]{2,1,0:T(8,128)}, f32[8,384,384]{2,1,0:T(8,128)}) custom-call(s32[4]{0:T(128)S(1)} %pad_add_fusion.where_ref.refs_0_.refs_1_, bf16[2,384,384]{2,1,0:T(8,128)(2,1)} %choose.5.after_ref.mine_ref, bf16[2,384,384]{2,1,0:T(8,128)(2,1)} %collective-permute-done.26.other_ref, ...), custom_call_target="tpu_custom_call", output_to_operand_aliasing={{0}: (3, {}), {1}: (4, {})} | custom-call | flops 30000001024 | bytes 10000 | tf_op jit(solution)/shard_map/expert_end/pallas_call | solution.py:394
  (124 shorter events, 50.8 us)
Async XLA Ops:
  7.2 217.1 %all-reduce.4.cloned.1.call-start = ((), (), s32[]{:S(2)}) async-start(), calls=%async_computation.2 | async-start | bytes 2359296 | tf_op jit(solution)/shard_map/psum | solution.py:1202
  7.9 31.3 %copy-start.3 = (f32[1,384]{1,0:T(1,128)}, f32[1,384]{1,0:T(1,128)S(1)}, u32[]{:S(2)}) copy-start(f32[1,384]{1,0:T(1,128)S(1)} %reshape.54.gain1_ref.refs_5_.refs_4_) | copy-start | bytes 4612
  9.4 29.9 %copy-start = (bf16[3,384,192]{2,1,0:T(8,128)(2,1)}, bf16[3,384,192]{2,1,0:T(8,128)(2,1)S(1)}, u32[]{:S(2)}) copy-start(bf16[3,384,192]{2,1,0:T(8,128)(2,1)S(1)} %dynamic-slice_bitcast_fusion.w3_ref.refs_12_) | copy-start | bytes 1327108
  39.3 2.4 collective-permute-start
  49.9 3.9 %collective-permute-start.1 = (bf16[1216,768]{1,0:T(8,128)(2,1)S(1)}, bf16[1216,768]{1,0:T(8,128)(2,1)S(1)}, u32[]{:S(2)}, u32[]{:S(2)}) collective-permute-start(bf16[1216,768]{1,0:T(8,128)(2,1)S(1)} %get-tuple-element.74), channel_id=1, source_target_pairs={{0,1},{1,0},{2,3},{3,2},{4,5},{5,4},{6,7},{7,6},{8,9},{9,8},{10,11... | collective-permute-start | bytes 5603336 | tf_op jit(solution)/shard_map/ppermute | solution.py:1135
  76.0 4.0 %collective-permute-start.2 = (bf16[1216,768]{1,0:T(8,128)(2,1)S(1)}, bf16[1216,768]{1,0:T(8,128)(2,1)}, u32[]{:S(2)}, u32[]{:S(2)}) collective-permute-start(bf16[1216,768]{1,0:T(8,128)(2,1)S(1)} %get-tuple-element.76.after_ref), channel_id=1, source_target_pairs={{0,1},{1,0},{2,3},{3,2},{4,5},{5,4},{6,7},{7,6},{8,9},{9,8},{10,11... | collective-permute-start | bytes 5603336 | tf_op jit(solution)/shard_map/ppermute | solution.py:1135
  76.4 25.4 %collective-permute-start.4 = (bf16[2,384,384]{2,1,0:T(8,128)(2,1)}, bf16[2,384,384]{2,1,0:T(8,128)(2,1)S(1)}, u32[]{:S(2)}, u32[]{:S(2)}) collective-permute-start(bf16[2,384,384]{2,1,0:T(8,128)(2,1)} %get-tuple-element.82), channel_id=1, source_target_pairs={{0,4},{4,0},{8,12},{12,8},{16,20},{20,16},{24,28},{28,24},{1,5},{5... | collective-permute-start | bytes 1769480 | tf_op jit(solution)/shard_map/ppermute | solution.py:1135
  76.6 44.5 %collective-permute-start.6 = (bf16[2,384,384]{2,1,0:T(8,128)(2,1)}, bf16[2,384,384]{2,1,0:T(8,128)(2,1)}, u32[]{:S(2)}, u32[]{:S(2)}) collective-permute-start(bf16[2,384,384]{2,1,0:T(8,128)(2,1)} %get-tuple-element.93), channel_id=1, source_target_pairs={{0,4},{4,0},{8,12},{12,8},{16,20},{20,16},{24,28},{28,24},{1,5},{5... | collective-permute-start | bytes 1769480 | tf_op jit(solution)/shard_map/ppermute | solution.py:1135
  78.4 51.1 %collective-permute-start.8 = (bf16[2,384,384]{2,1,0:T(8,128)(2,1)}, bf16[2,384,384]{2,1,0:T(8,128)(2,1)}, u32[]{:S(2)}, u32[]{:S(2)}) collective-permute-start(bf16[2,384,384]{2,1,0:T(8,128)(2,1)} %get-tuple-element.95), channel_id=1, source_target_pairs={{0,4},{4,0},{8,12},{12,8},{16,20},{20,16},{24,28},{28,24},{1,5},{5... | collective-permute-start | bytes 1769480 | tf_op jit(solution)/shard_map/ppermute | solution.py:1135
  83.4 12.9 %collective-permute-start.3 = (bf16[544,384]{1,0:T(8,128)(2,1)S(1)}, bf16[544,384]{1,0:T(8,128)(2,1)S(1)}, u32[]{:S(2)}, u32[]{:S(2)}) collective-permute-start(bf16[544,384]{1,0:T(8,128)(2,1)S(1)} %get-tuple-element.77.after_ref), channel_id=1, source_target_pairs={{0,2},{2,0},{1,3},{3,1},{4,6},{6,4},{5,7},{7,5},{8,10},{10,8},{9,1... | collective-permute-start | bytes 1253384 | tf_op jit(solution)/shard_map/ppermute | solution.py:1135
  99.8 8.6 %collective-permute-start.5 = (bf16[544,384]{1,0:T(8,128)(2,1)S(1)}, bf16[544,384]{1,0:T(8,128)(2,1)S(1)}, u32[]{:S(2)}, u32[]{:S(2)}) collective-permute-start(bf16[544,384]{1,0:T(8,128)(2,1)S(1)} %get-tuple-element.83.refs_2_), channel_id=1, source_target_pairs={{0,1},{1,0},{2,3},{3,2},{4,5},{5,4},{6,7},{7,6},{8,9},{9,8},{10,11... | collective-permute-start | bytes 1253384 | tf_op jit(solution)/shard_map/ppermute | solution.py:1135
  99.9 81.5 %collective-permute-start.13 = (bf16[1088,384]{1,0:T(8,128)(2,1)}, bf16[1088,384]{1,0:T(8,128)(2,1)}, u32[]{:S(2)}, u32[]{:S(2)}) collective-permute-start(bf16[1088,384]{1,0:T(8,128)(2,1)} %get-tuple-element.80.after_ref.refs_1_), channel_id=1, source_target_pairs={{0,2},{2,0},{1,3},{3,1},{4,6},{6,4},{5,7},{7,5},{8,10},{10,8},{9,1... | collective-permute-start | bytes 2506760 | tf_op jit(solution)/shard_map/ppermute | solution.py:1135
  102.7 23.1 %collective-permute-start.7 = (bf16[2,384,384]{2,1,0:T(8,128)(2,1)}, bf16[2,384,384]{2,1,0:T(8,128)(2,1)}, u32[]{:S(2)}, u32[]{:S(2)}) collective-permute-start(bf16[2,384,384]{2,1,0:T(8,128)(2,1)} %add.33.after_ref.refs_0_), channel_id=1, source_target_pairs={{0,8},{4,12},{24,16},{28,20},{1,9},{5,13},{25,17},{29,21},{2,10},{... | collective-permute-start | bytes 1769480 | tf_op jit(solution)/shard_map/ppermute | solution.py:1168
  123.5 33.4 %collective-permute-start.10 = (bf16[2,384,384]{2,1,0:T(8,128)(2,1)}, bf16[2,384,384]{2,1,0:T(8,128)(2,1)}, u32[]{:S(2)}, u32[]{:S(2)}) collective-permute-start(bf16[2,384,384]{2,1,0:T(8,128)(2,1)} %add.34.after_ref.refs_0_), channel_id=1, source_target_pairs={{0,8},{4,12},{24,16},{28,20},{1,9},{5,13},{25,17},{29,21},{2,10},{... | collective-permute-start | bytes 1769480 | tf_op jit(solution)/shard_map/ppermute | solution.py:1168
  128.0 26.3 %collective-permute-start.9 = (bf16[2,384,384]{2,1,0:T(8,128)(2,1)}, bf16[2,384,384]{2,1,0:T(8,128)(2,1)}, u32[]{:S(2)}, u32[]{:S(2)}) collective-permute-start(bf16[2,384,384]{2,1,0:T(8,128)(2,1)} %add.35.after_ref.refs_0_), channel_id=1, source_target_pairs={{8,16},{12,20},{16,8},{20,12},{9,17},{13,21},{17,9},{21,13},{10,18... | collective-permute-start | bytes 1769480 | tf_op jit(solution)/shard_map/ppermute | solution.py:1170
  131.6 29.3 %collective-permute-start.11 = (bf16[2,384,384]{2,1,0:T(8,128)(2,1)}, bf16[2,384,384]{2,1,0:T(8,128)(2,1)}, u32[]{:S(2)}, u32[]{:S(2)}) collective-permute-start(bf16[2,384,384]{2,1,0:T(8,128)(2,1)} %add.36.after_ref.refs_0_), channel_id=1, source_target_pairs={{0,8},{4,12},{24,16},{28,20},{1,9},{5,13},{25,17},{29,21},{2,10},{... | collective-permute-start | bytes 1769480 | tf_op jit(solution)/shard_map/ppermute | solution.py:1168
  154.2 23.1 %collective-permute-start.12 = (bf16[1088,384]{1,0:T(8,128)(2,1)S(1)}, bf16[1088,384]{1,0:T(8,128)(2,1)S(1)}, u32[]{:S(2)}, u32[]{:S(2)}) collective-permute-start(bf16[1088,384]{1,0:T(8,128)(2,1)S(1)} %get-tuple-element.103.after_ref), channel_id=1, source_target_pairs={{0,1},{1,0},{2,3},{3,2},{4,5},{5,4},{6,7},{7,6},{8,9},{9,8},{10,11... | collective-permute-start | bytes 2506760 | tf_op jit(solution)/shard_map/ppermute | solution.py:1135
  155.6 30.5 %collective-permute-start.15 = (bf16[2,384,384]{2,1,0:T(8,128)(2,1)S(1)}, bf16[2,384,384]{2,1,0:T(8,128)(2,1)S(1)}, u32[]{:S(2)}, u32[]{:S(2)}) collective-permute-start(bf16[2,384,384]{2,1,0:T(8,128)(2,1)S(1)} %add.37.after_ref.refs_1_), channel_id=1, source_target_pairs={{8,0},{12,4},{16,24},{20,28},{9,1},{13,5},{17,25},{21,29},{10,2},{... | collective-permute-start | bytes 1769480 | tf_op jit(solution)/shard_map/ppermute | solution.py:1171
  159.2 24.3 %collective-permute-start.14 = (bf16[2,384,384]{2,1,0:T(8,128)(2,1)}, bf16[2,384,384]{2,1,0:T(8,128)(2,1)}, u32[]{:S(2)}, u32[]{:S(2)}) collective-permute-start(bf16[2,384,384]{2,1,0:T(8,128)(2,1)} %add.38.after_ref.refs_0_), channel_id=1, source_target_pairs={{8,16},{12,20},{16,8},{20,12},{9,17},{13,21},{17,9},{21,13},{10,18... | collective-permute-start | bytes 1769480 | tf_op jit(solution)/shard_map/ppermute | solution.py:1170
  162.2 26.9 %collective-permute-start.16 = (bf16[2,384,384]{2,1,0:T(8,128)(2,1)S(1)}, bf16[2,384,384]{2,1,0:T(8,128)(2,1)}, u32[]{:S(2)}, u32[]{:S(2)}) collective-permute-start(bf16[2,384,384]{2,1,0:T(8,128)(2,1)S(1)} %add.39.after_ref.refs_0_), channel_id=1, source_target_pairs={{8,16},{12,20},{16,8},{20,12},{9,17},{13,21},{17,9},{21,13},{10,18... | collective-permute-start | bytes 1769480 | tf_op jit(solution)/shard_map/ppermute | solution.py:1170
  167.8 42.3 %all-to-all-start = ((bf16[16,56,384]{2,1,0:T(8,128)(2,1)}), bf16[16,56,384]{2,1,0:T(8,128)(2,1)}, u32[]{:S(2)}, u32[]{:S(2)}) async-start(bf16[16,56,384]{2,1,0:T(8,128)(2,1)} %bitcast.12), calls=%async_computation | async-start | bytes 1376256 | tf_op jit(solution)/shard_map/all_to_all | solution.py:1261
  179.5 15.1 %collective-permute-start.17 = (bf16[544,384]{1,0:T(8,128)(2,1)S(1)}, bf16[544,384]{1,0:T(8,128)(2,1)S(1)}, u32[]{:S(2)}, u32[]{:S(2)}) collective-permute-start(bf16[544,384]{1,0:T(8,128)(2,1)S(1)} %get-tuple-element.112.after_ref), channel_id=1, source_target_pairs={{0,2},{2,0},{1,3},{3,1},{4,6},{6,4},{5,7},{7,5},{8,10},{10,8},{9,1... | collective-permute-start | bytes 1253384 | tf_op jit(solution)/shard_map/ppermute | solution.py:1135
  183.4 33.3 %collective-permute-start.19 = (bf16[1088,384]{1,0:T(8,128)(2,1)S(1)}, bf16[1088,384]{1,0:T(8,128)(2,1)S(1)}, u32[]{:S(2)}, u32[]{:S(2)}) collective-permute-start(bf16[1088,384]{1,0:T(8,128)(2,1)S(1)} %block_out.1.after_ref.refs_1_), channel_id=1, source_target_pairs={{0,1},{1,0},{2,3},{3,2},{4,5},{5,4},{6,7},{7,6},{8,9},{9,8},{10,11... | collective-permute-start | bytes 2506760 | tf_op jit(solution)/shard_map/ppermute | solution.py:1135
  184.9 21.1 %collective-permute-start.18 = (bf16[2,384,384]{2,1,0:T(8,128)(2,1)S(1)}, bf16[2,384,384]{2,1,0:T(8,128)(2,1)S(1)}, u32[]{:S(2)}, u32[]{:S(2)}) collective-permute-start(bf16[2,384,384]{2,1,0:T(8,128)(2,1)S(1)} %add.40.after_ref.refs_1_), channel_id=1, source_target_pairs={{8,0},{12,4},{16,24},{20,28},{9,1},{13,5},{17,25},{21,29},{10,2},{... | collective-permute-start | bytes 1769480 | tf_op jit(solution)/shard_map/ppermute | solution.py:1171
  187.6 39.2 %collective-permute-start.20 = (bf16[2,384,384]{2,1,0:T(8,128)(2,1)}, bf16[2,384,384]{2,1,0:T(8,128)(2,1)}, u32[]{:S(2)}, u32[]{:S(2)}) collective-permute-start(bf16[2,384,384]{2,1,0:T(8,128)(2,1)} %choose.3.after_ref.mine_ref), channel_id=1, source_target_pairs={{0,4},{4,0},{8,12},{12,8},{16,20},{20,16},{24,28},{28,24},{1,5},{5... | collective-permute-start | bytes 1769480 | tf_op jit(solution)/shard_map/ppermute | solution.py:1135
  190.3 32.6 %collective-permute-start.22 = (bf16[2,384,384]{2,1,0:T(8,128)(2,1)S(1)}, bf16[2,384,384]{2,1,0:T(8,128)(2,1)S(1)}, u32[]{:S(2)}, u32[]{:S(2)}) collective-permute-start(bf16[2,384,384]{2,1,0:T(8,128)(2,1)S(1)} %add.41.after_ref.refs_1_), channel_id=1, source_target_pairs={{8,0},{12,4},{16,24},{20,28},{9,1},{13,5},{17,25},{21,29},{10,2},{... | collective-permute-start | bytes 1769480 | tf_op jit(solution)/shard_map/ppermute | solution.py:1171
  197.5 20.9 %collective-permute-start.21 = (bf16[544,384]{1,0:T(8,128)(2,1)S(1)}, bf16[544,384]{1,0:T(8,128)(2,1)}, u32[]{:S(2)}, u32[]{:S(2)}) collective-permute-start(bf16[544,384]{1,0:T(8,128)(2,1)S(1)} %token_grad.1.after_ref.refs_1_), channel_id=1, source_target_pairs={{0,2},{2,0},{1,3},{3,1},{4,6},{6,4},{5,7},{7,5},{8,10},{10,8},{9,1... | collective-permute-start | bytes 1253384 | tf_op jit(solution)/shard_map/ppermute | solution.py:1135
  207.5 27.2 %collective-permute-start.24 = (bf16[2,384,384]{2,1,0:T(8,128)(2,1)}, bf16[2,384,384]{2,1,0:T(8,128)(2,1)}, u32[]{:S(2)}, u32[]{:S(2)}) collective-permute-start(bf16[2,384,384]{2,1,0:T(8,128)(2,1)} %choose.4.after_ref.mine_ref), channel_id=1, source_target_pairs={{0,4},{4,0},{8,12},{12,8},{16,20},{20,16},{24,28},{28,24},{1,5},{5... | collective-permute-start | bytes 1769480 | tf_op jit(solution)/shard_map/ppermute | solution.py:1135
  212.2 22.4 %all-to-all-start.1 = ((bf16[16,56,384]{2,1,0:T(8,128)(2,1)}), bf16[16,56,384]{2,1,0:T(8,128)(2,1)}, u32[]{:S(2)}, u32[]{:S(2)}) async-start(bf16[16,56,384]{2,1,0:T(8,128)(2,1)} %total.1.after_ref), calls=%async_computation.1 | async-start | bytes 1376256 | tf_op jit(solution)/shard_map/all_to_all | solution.py:1275
  219.6 10.0 %collective-permute-start.23 = (bf16[1088,384]{1,0:T(8,128)(2,1)S(1)}, bf16[1088,384]{1,0:T(8,128)(2,1)S(1)}, u32[]{:S(2)}, u32[]{:S(2)}) collective-permute-start(bf16[1088,384]{1,0:T(8,128)(2,1)S(1)} %weave.1.after_ref.refs_1_), channel_id=1, source_target_pairs={{0,1},{1,0},{2,3},{3,2},{4,5},{5,4},{6,7},{7,6},{8,9},{9,8},{10,11... | collective-permute-start | bytes 2506760 | tf_op jit(solution)/shard_map/ppermute | solution.py:1135
  224.3 19.4 %collective-permute-start.26 = (bf16[2,384,384]{2,1,0:T(8,128)(2,1)}, bf16[2,384,384]{2,1,0:T(8,128)(2,1)}, u32[]{:S(2)}, u32[]{:S(2)}) collective-permute-start(bf16[2,384,384]{2,1,0:T(8,128)(2,1)} %choose.5.after_ref.mine_ref), channel_id=1, source_target_pairs={{0,4},{4,0},{8,12},{12,8},{16,20},{20,16},{24,28},{28,24},{1,5},{5... | collective-permute-start | bytes 1769480 | tf_op jit(solution)/shard_map/ppermute | solution.py:1135
  234.7 2.9 %collective-permute-start.25 = (bf16[896,384]{1,0:T(8,128)(2,1)}, bf16[896,384]{1,0:T(8,128)(2,1)S(1)}, u32[]{:S(2)}, u32[]{:S(2)}) collective-permute-start(bf16[896,384]{1,0:T(8,128)(2,1)} %bitcast.13.refs_1_), channel_id=1, source_target_pairs={{0,1},{1,0},{2,3},{3,2},{4,5},{5,4},{6,7},{7,6},{8,9},{9,8},{10,11... | collective-permute-start | bytes 2064392 | tf_op jit(solution)/shard_map/ppermute | solution.py:1135
  (23 other events, 160.4 us)
Sparse Core Ops, SparseCore 0:
  78.7 94.0 all-reduce.3

commit v3 on v2

--- a/solution.py
+++ b/solution.py
@@ -1260,12 +1260,12 @@
     share = pay_rows // lax.axis_size(("wide", "hi"))
     pay_got = lax.all_to_all(pay.reshape(-1, share, width), ("wide", "hi"), 0, 0)
     last = pay, ANY_SPEC
+    last = line_step(1, 2, last)
     hk, hs = run_split(where, hkeep, hgot, last)
     hs_got = swap(hs, "hi", 1)
     out_own = run_out(mid, ex, ex_got, (hs, ANY_SPEC))
     out_oth = swap(out_own, "lo", 1)
-    last = line_step(1, 2, (out_own, ANY_SPEC))
-    last = last_step(0, last)
+    last = last_step(0, (out_own, ANY_SPEC))
     last = line_step(2, 2, last)
     token_rows = run_tokens(where, hk, hs_got, gmid, tokens, gain1, last)
     token_got = swap(token_rows, "hi", 1)

time: 254 us -> 255 us (level); the launches traced: 253 us -> 251 us
  Pallas kernels: 151 us -> 145 us
  starting transfers between devices: 51.4 us -> 56 us
    pallas_call x35, Pallas kernels: 151 us -> 145 us  [run_on(): return run(*placed)]
    ppermute x18, starting transfers between devices: 16 us -> 19.1 us  [swap(): return lax.ppermute(value, axis, [(i, i ^ mask) for i in range(size)])]
    ppermute x3, waiting for transfers between devices: 10.2 us -> 7.65 us  [wide_step(): return lax.ppermute(value, 'wide', [(b, a) for a, b in inward])]
  transfers between devices with their start and end apart: 30 -> 30, of which waited for: 9 -> 9; matrix products, arithmetic and copies ran while one was open for 0% -> 0% of each run, Pallas kernels for 36% -> 35%
where the time goes in v3:
time: 255 us; the launch traced here: 251 us
  Pallas kernels  145 us (57%)
  starting transfers between devices  56 us (22%)
  waiting for transfers between devices  29.7 us (12%)
  between operations  14.6 us (6%)
  local copies, waits for them, and re-layouts  6.04 us (2%)
    pallas_call x35, Pallas kernels, run_on(): return run(*placed)  145 us
    ppermute x18, starting transfers between devices, swap(): return lax.ppermute(value, axis, [(i, i ^ mask) for i in range(size)])  19.1 us
    ppermute x18, waiting for transfers between devices, swap(): return lax.ppermute(value, axis, [(i, i ^ mask) for i in range(size)])  17.2 us
    ppermute x3, starting transfers between devices, wide_step(): return lax.ppermute(value, 'wide', inward)  11.7 us
    all_to_all x1, starting transfers between devices, on_device(): lax.all_to_all(pay.reshape(-1, share, width), ('wide', 'hi'), 0, 0)  9.88 us
    ppermute x3, waiting for transfers between devices, wide_step(): return lax.ppermute(value, 'wide', [(b, a) for a, b in inward])  7.65 us
    all_to_all x1, starting transfers between devices, on_device(): pay_got = lax.all_to_all(pay_got, ('wide', 'hi'), 0, 0).reshape(pay.shape)  6.7 us
  transfers between devices with their start and end apart: 30, of which 9 were waited for; matrix products, arithmetic and copies ran while one was open for 0% of the time, Pallas kernels for 35%

profile of v3, /device:TPU:0, one launch (start us, length us, event | category | flops | bytes accessed | tf_op | source)
XLA Modules:
  0.0 251.5 jit_solution(1591775512885589598)
XLA Ops:
  10.2 24.8 %front.1 = (bf16[2560,384]{1,0:T(8,128)(2,1)}, bf16[2560,256]{1,0:T(8,128)(2,1)}, bf16[192,2560]{1,0:T(8,128)(2,1)}, bf16[2560,256]{1,0:T(8,128)(2,1)}, bf16[230...) custom-call(s32[1,8]{1,0:T(1,128)S(1)} %copy-done.10, ...), custom_call_target="tpu_custom_call" | custom-call | flops 330000007168 | bytes 10000 | tf_op jit(solution)/shard_map/front/pallas_call | solution.py:394
  37.5 8.2 %mid.1 = (f32[1088,384]{1,0:T(8,128)}, bf16[1216,768]{1,0:T(8,128)(2,1)S(1)}, bf16[1216,768]{1,0:T(8,128)(2,1)S(1)}) custom-call(s32[4]{0:T(128)S(1)} %pad_add_fusion.where_ref.refs_0_.refs_1_, bf16[1088,384]{1,0:T(8,128)(2,1)S(1)} %get-tuple-element.69.after_ref.keep_ref, bf16[1088,384]{1,0:T(8,128)(2,1)S(1)} %collective-permute-done.got_ref, ...), custom_call_target="tpu_custom_call" | custom-call | flops 89999998976 | bytes 10000 | tf_op jit(solution)/shard_map/mid/pallas_call | solution.py:394
  46.1 3.5 %collective-permute-done.1.oth_ref = bf16[1216,768]{1,0:T(8,128)(2,1)S(1)} collective-permute-done((bf16[1216,768]{1,0:T(8,128)(2,1)S(1)}, bf16[1216,768]{1,0:T(8,128)(2,1)S(1)}, u32[]{:S(2)}, u32[]{:S(2)}) %collective-permute-start.1) | collective-permute-done | bytes 1867808 | tf_op jit(solution)/shard_map/ppermute | solution.py:1135
  49.5 20.3 %experts.1 = (bf16[1216,768]{1,0:T(8,128)(2,1)S(1)}, bf16[1216,768]{1,0:T(8,128)(2,1)S(1)}, f32[384,128]{1,0:T(8,128)S(1)}, bf16[2,2,384,384]{3,2,1,0:T(8,128)(2...) custom-call(s32[32,128]{1,0:T(8,128)S(1)} %get-tuple-element.70.plan, ...), custom_call_target="tpu_custom_call" | custom-call | flops 219999993856 | bytes 10000 | tf_op jit(solution)/shard_map/experts/pallas_call | solution.py:394
  72.1 7.5 %collective-permute-start.4 = (bf16[2,384,384]{2,1,0:T(8,128)(2,1)}, bf16[2,384,384]{2,1,0:T(8,128)(2,1)S(1)}, u32[]{:S(2)}, u32[]{:S(2)}) collective-permute-start(bf16[2,384,384]{2,1,0:T(8,128)(2,1)} %get-tuple-element.82), channel_id=1, source_target_pairs={{0,4},{4,0},{8,12},{12,8},{16,20},{20,16},{24,28},{28,24},{1,5},{5... | collective-permute-start | bytes 1769480 | tf_op jit(solution)/shard_map/ppermute | solution.py:1135
  83.2 3.2 %unsort.1 = (bf16[544,384]{1,0:T(8,128)(2,1)S(1)}, bf16[544,384]{1,0:T(8,128)(2,1)S(1)}) custom-call(s32[4]{0:T(128)S(1)} %pad_add_fusion.where_ref.refs_0_.refs_1_, bf16[1216,768]{1,0:T(8,128)(2,1)S(1)} %copy-done.15, bf16[1216,768]{1,0:T(8,128)(2,1)} %collective-permute-done.2.got_ref.refs_1_, bf16[2,544,1280]{2,1,0:T(8,128)(2,1)S(1)} %unpick.1.unpick_ref), custom_call_target="tpu_custom_call" | custom-call | flops 40000000000 | bytes 10000 | tf_op jit(solution)/shard_map/unsort/pallas_call | solution.py:394
  88.0 3.2 %unsort_out.1.after_ref.refs_6_ = bf16[1088,384]{1,0:T(8,128)(2,1)S(1)} custom-call(bf16[544,384]{1,0:T(8,128)(2,1)S(1)} %get-tuple-element.77.after_ref, bf16[1216,768]{1,0:T(8,128)(2,1)S(1)} %copy-done.15, bf16[1216,768]{1,0:T(8,128)(2,1)} %collective-permute-done.2.got_ref.refs_1_, f32[8,1152]{1,0:T(8,128)S(1)} %get-tuple-element.72.pos_ref.refs_0_.refs_2_), custom_call_target="tpu_custom_call" | custom-call | flops 30000001024 | bytes 10000 | tf_op jit(solution)/shard_map/unsort_out/pallas_call | solution.py:394
  91.2 6.3 %collective-permute-done.3.refs_2_ = bf16[544,384]{1,0:T(8,128)(2,1)S(1)} collective-permute-done((bf16[544,384]{1,0:T(8,128)(2,1)S(1)}, bf16[544,384]{1,0:T(8,128)(2,1)S(1)}, u32[]{:S(2)}, u32[]{:S(2)}) %collective-permute-start.3) | collective-permute-done | bytes 417824 | tf_op jit(solution)/shard_map/ppermute | solution.py:1135
  97.5 3.6 %mid_back.1 = (f32[544,384]{1,0:T(8,128)}, bf16[544,384]{1,0:T(8,128)(2,1)S(1)}, f32[8,384]{1,0:T(8,128)S(1)}, bf16[1088,384]{1,0:T(8,128)(2,1)}) custom-call(bf16[1088,384]{1,0:T(8,128)(2,1)S(1)} %unsort_out.1.after_ref.refs_6_, s32[4]{0:T(128)S(1)} %pad_add_fusion.where_ref.refs_0_.refs_1_, bf16[544,384]{1,0:T(8,128)(2,1)S(1)} %get-tuple-element.78.refs_1_, ...), custom_call_target="tpu_custom_call" | custom-call | flops 40000000000 | bytes 10000 | tf_op jit(solution)/shard_map/mid_back/pallas_call | solution.py:394
  103.8 4.0 %collective-permute-start.7 = (bf16[2,384,384]{2,1,0:T(8,128)(2,1)}, bf16[2,384,384]{2,1,0:T(8,128)(2,1)}, u32[]{:S(2)}, u32[]{:S(2)}) collective-permute-start(bf16[2,384,384]{2,1,0:T(8,128)(2,1)} %add.33.after_ref.refs_0_), channel_id=1, source_target_pairs={{0,8},{4,12},{24,16},{28,20},{1,9},{5,13},{25,17},{29,21},{2,10},{... | collective-permute-start | bytes 1769480 | tf_op jit(solution)/shard_map/ppermute | solution.py:1168
  107.8 12.6 %back_first.1 = (bf16[1280,384]{1,0:T(8,128)(2,1)S(1)}, bf16[1280,384]{1,0:T(8,128)(2,1)S(1)}, bf16[1280,256]{1,0:T(8,128)(2,1)S(1)}, bf16[1280,256]{1,0:T(8,128...) custom-call(bf16[2,384,384]{2,1,0:T(8,128)(2,1)} %add.33.after_ref.r, ...), custom_call_target="tpu_custom_call" | custom-call | flops 140000002048 | bytes 10000 | tf_op jit(solution)/shard_map/back_first/pallas_call | solution.py:394
  120.4 2.4 add.34.after_ref.refs_0_
  122.8 3.0 %collective-permute-start.10 = (bf16[2,384,384]{2,1,0:T(8,128)(2,1)}, bf16[2,384,384]{2,1,0:T(8,128)(2,1)}, u32[]{:S(2)}, u32[]{:S(2)}) collective-permute-start(bf16[2,384,384]{2,1,0:T(8,128)(2,1)} %add.34.after_ref.refs_0_), channel_id=1, source_target_pairs={{0,8},{4,12},{24,16},{28,20},{1,9},{5,13},{25,17},{29,21},{2,10},{... | collective-permute-start | bytes 1769480 | tf_op jit(solution)/shard_map/ppermute | solution.py:1168
  125.9 2.2 add.35.after_ref.refs_0_
  129.6 2.1 add.36.after_ref.refs_0_
  131.6 4.7 %collective-permute-start.11 = (bf16[2,384,384]{2,1,0:T(8,128)(2,1)}, bf16[2,384,384]{2,1,0:T(8,128)(2,1)}, u32[]{:S(2)}, u32[]{:S(2)}) collective-permute-start(bf16[2,384,384]{2,1,0:T(8,128)(2,1)} %add.36.after_ref.refs_0_), channel_id=1, source_target_pairs={{0,8},{4,12},{24,16},{28,20},{1,9},{5,13},{25,17},{29,21},{2,10},{... | collective-permute-start | bytes 1769480 | tf_op jit(solution)/shard_map/ppermute | solution.py:1168
  136.3 16.1 %back_second.1 = (bf16[1088,384]{1,0:T(8,128)(2,1)}, bf16[1088,384]{1,0:T(8,128)(2,1)S(1)}, bf16[192,1280]{1,0:T(8,128)(2,1)S(1)}, bf16[192,2560]{1,0:T(8,128)(2,1)S(1)}, bf16[192,2560]{1,0:T(8,128)(2,1)S(1)}) custom-call(bf16[2,384,384]{2,1,0:T(8,128)(2,1)} %add.36.after_ref.refs_0_, s32[1,8]{1,0:T(1,128)S(1)} %copy-done.11, ...), custom_call_target="tpu_custom_call" | custom-call | flops 140000002048 | bytes 10000 | tf_op jit(solution)/shard_map/back_second/pallas_call | solution.py:394
  155.3 2.2 add.38.after_ref.refs_0_
  162.1 4.1 %weights.1.after_ref = bf16[896,384]{1,0:T(8,128)(2,1)} custom-call(bf16[2,384,384]{2,1,0:T(8,128)(2,1)S(1)} %add.39.after_ref.refs_0_, bf16[192,1280]{1,0:T(8,128)(2,1)S(1)} %get-tuple-element.104.refs_0_, bf16[192,2560]{1,0:T(8,128)(2,1)S(1)} %get-tuple-element.105.refs_1_, bf16[192,2560]{1,0:T(8,128)(2,1)S(1)} %get-tuple-element.106.refs_2_, ...), custom_call_target="tpu_custom_call" | custom-call | flops 40000000000 | bytes 10000 | tf_op jit(solution)/shard_map/weights/pallas_call | solution.py:394
  166.2 9.9 %all-to-all-start = ((bf16[16,56,384]{2,1,0:T(8,128)(2,1)}), bf16[16,56,384]{2,1,0:T(8,128)(2,1)}, u32[]{:S(2)}, u32[]{:S(2)}) async-start(bf16[16,56,384]{2,1,0:T(8,128)(2,1)} %bitcast.12), calls=%async_computation | async-start | bytes 1376256 | tf_op jit(solution)/shard_map/all_to_all | solution.py:1261
  178.8 2.2 split.1
  190.4 5.2 %collective-permute-done.17.refs_2_ = bf16[544,384]{1,0:T(8,128)(2,1)S(1)} collective-permute-done((bf16[544,384]{1,0:T(8,128)(2,1)S(1)}, bf16[544,384]{1,0:T(8,128)(2,1)S(1)}, u32[]{:S(2)}, u32[]{:S(2)}) %collective-permute-start.17) | collective-permute-done | bytes 417824 | tf_op jit(solution)/shard_map/ppermute | solution.py:1135
  195.6 2.8 %token_grad.1.after_ref.refs_1_ = bf16[544,384]{1,0:T(8,128)(2,1)S(1)} custom-call(bf16[2,384,384]{2,1,0:T(8,128)(2,1)S(1)} %add.41.after_ref.refs_1_, s32[4]{0:T(128)S(1)} %pad_add_fusion.where_ref.refs_0_.refs_1_, bf16[544,384]{1,0:T(8,128)(2,1)} %get-tuple-element.113.refs_1_, bf16[544,384]{1,0:T(8,128)(2,1)S(1)} %collective-permute-done.17.refs_2_, ...), custom_call_target="tpu_custom_call" | custom-call | flops 30000001024 | bytes 10000 | tf_op jit(solution)/shard_map/token_grad/pallas_call | solution.py:394
  200.1 5.2 %collective-permute-done.18.refs_2_ = bf16[2,384,384]{2,1,0:T(8,128)(2,1)S(1)} collective-permute-done((bf16[2,384,384]{2,1,0:T(8,128)(2,1)S(1)}, bf16[2,384,384]{2,1,0:T(8,128)(2,1)S(1)}, u32[]{:S(2)}, u32[]{:S(2)}) %collective-permute-start.18) | collective-permute-done | bytes 589856 | tf_op jit(solution)/shard_map/ppermute | solution.py:1171
  209.4 6.7 %all-to-all-start.1 = ((bf16[16,56,384]{2,1,0:T(8,128)(2,1)}), bf16[16,56,384]{2,1,0:T(8,128)(2,1)}, u32[]{:S(2)}, u32[]{:S(2)}) async-start(bf16[16,56,384]{2,1,0:T(8,128)(2,1)} %total.1.after_ref), calls=%async_computation.1 | async-start | bytes 1376256 | tf_op jit(solution)/shard_map/all_to_all | solution.py:1275
  219.1 2.5 collective-permute-done.22.refs_2_
  223.0 2.5 %summed_end.1 = (f32[8,384,384]{2,1,0:T(8,128)}, f32[8,384,384]{2,1,0:T(8,128)}) custom-call(bf16[2,384,384]{2,1,0:T(8,128)(2,1)} %choose.5.after_ref.mine_ref, bf16[2,2,384,384]{3,2,1,0:T(8,128)(2,1)} %all-reduce.4.cloned.1.call-done.refs_0_), custom_call_target="tpu_custom_call" | custom-call | flops 40000000000 | bytes 10000 | tf_op jit(solution)/shard_map/summed_end/pallas_call | solution.py:394
  225.5 2.8 %expert_end.3 = (f32[8,384,384]{2,1,0:T(8,128)}, f32[8,384,384]{2,1,0:T(8,128)}) custom-call(s32[4]{0:T(128)S(1)} %pad_add_fusion.where_ref.refs_0_.refs_1_, bf16[2,384,384]{2,1,0:T(8,128)(2,1)} %choose.3.after_ref.mine_ref, bf16[2,384,384]{2,1,0:T(8,128)(2,1)} %collective-permute-done.20.other_ref, ...), custom_call_target="tpu_custom_call", output_to_operand_aliasing={{0}: (3, {}), {1}: (4, {})} | custom-call | flops 30000001024 | bytes 10000 | tf_op jit(solution)/shard_map/expert_end/pallas_call | solution.py:394
  230.0 4.2 %all-to-all-done.1 = bf16[16,56,384]{2,1,0:T(8,128)(2,1)} async-done(((bf16[16,56,384]{2,1,0:T(8,128)(2,1)}), bf16[16,56,384]{2,1,0:T(8,128)(2,1)}, u32[]{:S(2)}, u32[]{:S(2)}) %all-to-all-start.1) | async-done | bytes 688160 | tf_op jit(solution)/shard_map/all_to_all | solution.py:1275
  234.2 2.8 %expert_end.4 = (f32[8,384,384]{2,1,0:T(8,128)}, f32[8,384,384]{2,1,0:T(8,128)}) custom-call(s32[4]{0:T(128)S(1)} %pad_add_fusion.where_ref.refs_0_.refs_1_, bf16[2,384,384]{2,1,0:T(8,128)(2,1)} %choose.4.after_ref.mine_ref, bf16[2,384,384]{2,1,0:T(8,128)(2,1)} %collective-permute-done.24.other_ref, ...), custom_call_target="tpu_custom_call", output_to_operand_aliasing={{0}: (3, {}), {1}: (4, {})} | custom-call | flops 30000001024 | bytes 10000 | tf_op jit(solution)/shard_map/expert_end/pallas_call | solution.py:394
  237.1 3.0 %attn_end.1 = (f32[3,384,384]{2,1,0:T(8,128)}, f32[384,384]{1,0:T(8,128)}, f32[384]{0:T(512)}, f32[384]{0:T(512)}, f32[8,384]{1,0:T(8,128)}) custom-call(f32[8,384,384]{2,1,0:T(8,128)} %get-tuple-element.120.after_ref.refs_0_, s32[4]{0:T(128)S(1)} %pad_add_fusion.where_ref.refs_0_.refs_1_, bf16[896,384]{1,0:T(8,128)(2,1)} %bitcast.13.refs_1_, ...), custom_call_target="tpu_custom_call" | custom-call | flops 40000000000 | bytes 10000 | tf_op jit(solution)/shard_map/attn_end/pallas_call | solution.py:394
  241.9 2.7 %expert_end.5 = (f32[8,384,384]{2,1,0:T(8,128)}, f32[8,384,384]{2,1,0:T(8,128)}) custom-call(s32[4]{0:T(128)S(1)} %pad_add_fusion.where_ref.refs_0_.refs_1_, bf16[2,384,384]{2,1,0:T(8,128)(2,1)} %choose.5.after_ref.mine_ref, bf16[2,384,384]{2,1,0:T(8,128)(2,1)} %collective-permute-done.26.other_ref, ...), custom_call_target="tpu_custom_call", output_to_operand_aliasing={{0}: (3, {}), {1}: (4, {})} | custom-call | flops 30000001024 | bytes 10000 | tf_op jit(solution)/shard_map/expert_end/pallas_call | solution.py:394
  (124 shorter events, 50.3 us)
Async XLA Ops:
  7.2 215.8 %all-reduce.4.cloned.1.call-start = ((), (), s32[]{:S(2)}) async-start(), calls=%async_computation.2 | async-start | bytes 2359296 | tf_op jit(solution)/shard_map/psum | solution.py:1202
  7.9 27.1 %copy-start.3 = (f32[1,384]{1,0:T(1,128)}, f32[1,384]{1,0:T(1,128)S(1)}, u32[]{:S(2)}) copy-start(f32[1,384]{1,0:T(1,128)S(1)} %reshape.54.gain1_ref.refs_5_.refs_4_) | copy-start | bytes 4612
  9.4 25.7 %copy-start = (bf16[3,384,192]{2,1,0:T(8,128)(2,1)}, bf16[3,384,192]{2,1,0:T(8,128)(2,1)S(1)}, u32[]{:S(2)}) copy-start(bf16[3,384,192]{2,1,0:T(8,128)(2,1)S(1)} %dynamic-slice_bitcast_fusion.w3_ref.refs_12_) | copy-start | bytes 1327108
  35.0 2.4 collective-permute-start
  45.7 3.9 %collective-permute-start.1 = (bf16[1216,768]{1,0:T(8,128)(2,1)S(1)}, bf16[1216,768]{1,0:T(8,128)(2,1)S(1)}, u32[]{:S(2)}, u32[]{:S(2)}) collective-permute-start(bf16[1216,768]{1,0:T(8,128)(2,1)S(1)} %get-tuple-element.74), channel_id=1, source_target_pairs={{0,1},{1,0},{2,3},{3,2},{4,5},{5,4},{6,7},{7,6},{8,9},{9,8},{10,11... | collective-permute-start | bytes 5603336 | tf_op jit(solution)/shard_map/ppermute | solution.py:1135
  71.8 10.4 %collective-permute-start.2 = (bf16[1216,768]{1,0:T(8,128)(2,1)S(1)}, bf16[1216,768]{1,0:T(8,128)(2,1)}, u32[]{:S(2)}, u32[]{:S(2)}) collective-permute-start(bf16[1216,768]{1,0:T(8,128)(2,1)S(1)} %get-tuple-element.76.after_ref), channel_id=1, source_target_pairs={{0,1},{1,0},{2,3},{3,2},{4,5},{5,4},{6,7},{7,6},{8,9},{9,8},{10,11... | collective-permute-start | bytes 5603336 | tf_op jit(solution)/shard_map/ppermute | solution.py:1135
  72.1 30.7 %collective-permute-start.4 = (bf16[2,384,384]{2,1,0:T(8,128)(2,1)}, bf16[2,384,384]{2,1,0:T(8,128)(2,1)S(1)}, u32[]{:S(2)}, u32[]{:S(2)}) collective-permute-start(bf16[2,384,384]{2,1,0:T(8,128)(2,1)} %get-tuple-element.82), channel_id=1, source_target_pairs={{0,4},{4,0},{8,12},{12,8},{16,20},{20,16},{24,28},{28,24},{1,5},{5... | collective-permute-start | bytes 1769480 | tf_op jit(solution)/shard_map/ppermute | solution.py:1135
  79.6 40.8 %collective-permute-start.6 = (bf16[2,384,384]{2,1,0:T(8,128)(2,1)}, bf16[2,384,384]{2,1,0:T(8,128)(2,1)}, u32[]{:S(2)}, u32[]{:S(2)}) collective-permute-start(bf16[2,384,384]{2,1,0:T(8,128)(2,1)} %get-tuple-element.93), channel_id=1, source_target_pairs={{0,4},{4,0},{8,12},{12,8},{16,20},{20,16},{24,28},{28,24},{1,5},{5... | collective-permute-start | bytes 1769480 | tf_op jit(solution)/shard_map/ppermute | solution.py:1135
  79.6 49.9 %collective-permute-start.8 = (bf16[2,384,384]{2,1,0:T(8,128)(2,1)}, bf16[2,384,384]{2,1,0:T(8,128)(2,1)}, u32[]{:S(2)}, u32[]{:S(2)}) collective-permute-start(bf16[2,384,384]{2,1,0:T(8,128)(2,1)} %get-tuple-element.95), channel_id=1, source_target_pairs={{0,4},{4,0},{8,12},{12,8},{16,20},{20,16},{24,28},{28,24},{1,5},{5... | collective-permute-start | bytes 1769480 | tf_op jit(solution)/shard_map/ppermute | solution.py:1135
  86.4 11.1 %collective-permute-start.3 = (bf16[544,384]{1,0:T(8,128)(2,1)S(1)}, bf16[544,384]{1,0:T(8,128)(2,1)S(1)}, u32[]{:S(2)}, u32[]{:S(2)}) collective-permute-start(bf16[544,384]{1,0:T(8,128)(2,1)S(1)} %get-tuple-element.77.after_ref), channel_id=1, source_target_pairs={{0,2},{2,0},{1,3},{3,1},{4,6},{6,4},{5,7},{7,5},{8,10},{10,8},{9,1... | collective-permute-start | bytes 1253384 | tf_op jit(solution)/shard_map/ppermute | solution.py:1135
  101.1 6.6 %collective-permute-start.5 = (bf16[544,384]{1,0:T(8,128)(2,1)S(1)}, bf16[544,384]{1,0:T(8,128)(2,1)S(1)}, u32[]{:S(2)}, u32[]{:S(2)}) collective-permute-start(bf16[544,384]{1,0:T(8,128)(2,1)S(1)} %get-tuple-element.83.refs_2_), channel_id=1, source_target_pairs={{0,1},{1,0},{2,3},{3,2},{4,5},{5,4},{6,7},{7,6},{8,9},{9,8},{10,11... | collective-permute-start | bytes 1253384 | tf_op jit(solution)/shard_map/ppermute | solution.py:1135
  101.2 81.7 %collective-permute-start.14 = (bf16[1088,384]{1,0:T(8,128)(2,1)}, bf16[1088,384]{1,0:T(8,128)(2,1)}, u32[]{:S(2)}, u32[]{:S(2)}) collective-permute-start(bf16[1088,384]{1,0:T(8,128)(2,1)} %get-tuple-element.80.after_ref.refs_1_), channel_id=1, source_target_pairs={{0,2},{2,0},{1,3},{3,1},{4,6},{6,4},{5,7},{7,5},{8,10},{10,8},{9,1... | collective-permute-start | bytes 2506760 | tf_op jit(solution)/shard_map/ppermute | solution.py:1135
  103.8 22.1 %collective-permute-start.7 = (bf16[2,384,384]{2,1,0:T(8,128)(2,1)}, bf16[2,384,384]{2,1,0:T(8,128)(2,1)}, u32[]{:S(2)}, u32[]{:S(2)}) collective-permute-start(bf16[2,384,384]{2,1,0:T(8,128)(2,1)} %add.33.after_ref.refs_0_), channel_id=1, source_target_pairs={{0,8},{4,12},{24,16},{28,20},{1,9},{5,13},{25,17},{29,21},{2,10},{... | collective-permute-start | bytes 1769480 | tf_op jit(solution)/shard_map/ppermute | solution.py:1168
  122.8 32.5 %collective-permute-start.10 = (bf16[2,384,384]{2,1,0:T(8,128)(2,1)}, bf16[2,384,384]{2,1,0:T(8,128)(2,1)}, u32[]{:S(2)}, u32[]{:S(2)}) collective-permute-start(bf16[2,384,384]{2,1,0:T(8,128)(2,1)} %add.34.after_ref.refs_0_), channel_id=1, source_target_pairs={{0,8},{4,12},{24,16},{28,20},{1,9},{5,13},{25,17},{29,21},{2,10},{... | collective-permute-start | bytes 1769480 | tf_op jit(solution)/shard_map/ppermute | solution.py:1168
  128.1 24.5 %collective-permute-start.9 = (bf16[2,384,384]{2,1,0:T(8,128)(2,1)}, bf16[2,384,384]{2,1,0:T(8,128)(2,1)}, u32[]{:S(2)}, u32[]{:S(2)}) collective-permute-start(bf16[2,384,384]{2,1,0:T(8,128)(2,1)} %add.35.after_ref.refs_0_), channel_id=1, source_target_pairs={{8,16},{12,20},{16,8},{20,12},{9,17},{13,21},{17,9},{21,13},{10,18... | collective-permute-start | bytes 1769480 | tf_op jit(solution)/shard_map/ppermute | solution.py:1170
  131.6 27.5 %collective-permute-start.11 = (bf16[2,384,384]{2,1,0:T(8,128)(2,1)}, bf16[2,384,384]{2,1,0:T(8,128)(2,1)}, u32[]{:S(2)}, u32[]{:S(2)}) collective-permute-start(bf16[2,384,384]{2,1,0:T(8,128)(2,1)} %add.36.after_ref.refs_0_), channel_id=1, source_target_pairs={{0,8},{4,12},{24,16},{28,20},{1,9},{5,13},{25,17},{29,21},{2,10},{... | collective-permute-start | bytes 1769480 | tf_op jit(solution)/shard_map/ppermute | solution.py:1168
  152.5 26.3 %collective-permute-start.13 = (bf16[1088,384]{1,0:T(8,128)(2,1)S(1)}, bf16[1088,384]{1,0:T(8,128)(2,1)S(1)}, u32[]{:S(2)}, u32[]{:S(2)}) collective-permute-start(bf16[1088,384]{1,0:T(8,128)(2,1)S(1)} %get-tuple-element.103.after_ref), channel_id=1, source_target_pairs={{0,1},{1,0},{2,3},{3,2},{4,5},{5,4},{6,7},{7,6},{8,9},{9,8},{10,11... | collective-permute-start | bytes 2506760 | tf_op jit(solution)/shard_map/ppermute | solution.py:1135
  154.0 31.0 %collective-permute-start.15 = (bf16[2,384,384]{2,1,0:T(8,128)(2,1)S(1)}, bf16[2,384,384]{2,1,0:T(8,128)(2,1)S(1)}, u32[]{:S(2)}, u32[]{:S(2)}) collective-permute-start(bf16[2,384,384]{2,1,0:T(8,128)(2,1)S(1)} %add.37.after_ref.refs_1_), channel_id=1, source_target_pairs={{8,0},{12,4},{16,24},{20,28},{9,1},{13,5},{17,25},{21,29},{10,2},{... | collective-permute-start | bytes 1769480 | tf_op jit(solution)/shard_map/ppermute | solution.py:1171
  157.5 18.5 %collective-permute-start.12 = (bf16[2,384,384]{2,1,0:T(8,128)(2,1)}, bf16[2,384,384]{2,1,0:T(8,128)(2,1)}, u32[]{:S(2)}, u32[]{:S(2)}) collective-permute-start(bf16[2,384,384]{2,1,0:T(8,128)(2,1)} %add.38.after_ref.refs_0_), channel_id=1, source_target_pairs={{8,16},{12,20},{16,8},{20,12},{9,17},{13,21},{17,9},{21,13},{10,18... | collective-permute-start | bytes 1769480 | tf_op jit(solution)/shard_map/ppermute | solution.py:1170
  160.6 27.3 %collective-permute-start.16 = (bf16[2,384,384]{2,1,0:T(8,128)(2,1)S(1)}, bf16[2,384,384]{2,1,0:T(8,128)(2,1)}, u32[]{:S(2)}, u32[]{:S(2)}) collective-permute-start(bf16[2,384,384]{2,1,0:T(8,128)(2,1)S(1)} %add.39.after_ref.refs_0_), channel_id=1, source_target_pairs={{8,16},{12,20},{16,8},{20,12},{9,17},{13,21},{17,9},{21,13},{10,18... | collective-permute-start | bytes 1769480 | tf_op jit(solution)/shard_map/ppermute | solution.py:1170
  166.2 41.2 %all-to-all-start = ((bf16[16,56,384]{2,1,0:T(8,128)(2,1)}), bf16[16,56,384]{2,1,0:T(8,128)(2,1)}, u32[]{:S(2)}, u32[]{:S(2)}) async-start(bf16[16,56,384]{2,1,0:T(8,128)(2,1)} %bitcast.12), calls=%async_computation | async-start | bytes 1376256 | tf_op jit(solution)/shard_map/all_to_all | solution.py:1261
  177.5 27.7 %collective-permute-start.18 = (bf16[2,384,384]{2,1,0:T(8,128)(2,1)S(1)}, bf16[2,384,384]{2,1,0:T(8,128)(2,1)S(1)}, u32[]{:S(2)}, u32[]{:S(2)}) collective-permute-start(bf16[2,384,384]{2,1,0:T(8,128)(2,1)S(1)} %add.40.after_ref.refs_1_), channel_id=1, source_target_pairs={{8,0},{12,4},{16,24},{20,28},{9,1},{13,5},{17,25},{21,29},{10,2},{... | collective-permute-start | bytes 1769480 | tf_op jit(solution)/shard_map/ppermute | solution.py:1171
  181.0 14.6 %collective-permute-start.17 = (bf16[544,384]{1,0:T(8,128)(2,1)S(1)}, bf16[544,384]{1,0:T(8,128)(2,1)S(1)}, u32[]{:S(2)}, u32[]{:S(2)}) collective-permute-start(bf16[544,384]{1,0:T(8,128)(2,1)S(1)} %get-tuple-element.112.after_ref), channel_id=1, source_target_pairs={{0,2},{2,0},{1,3},{3,1},{4,6},{6,4},{5,7},{7,5},{8,10},{10,8},{9,1... | collective-permute-start | bytes 1253384 | tf_op jit(solution)/shard_map/ppermute | solution.py:1135
  184.9 31.2 %collective-permute-start.19 = (bf16[1088,384]{1,0:T(8,128)(2,1)S(1)}, bf16[1088,384]{1,0:T(8,128)(2,1)S(1)}, u32[]{:S(2)}, u32[]{:S(2)}) collective-permute-start(bf16[1088,384]{1,0:T(8,128)(2,1)S(1)} %block_out.1.after_ref.refs_1_), channel_id=1, source_target_pairs={{0,1},{1,0},{2,3},{3,2},{4,5},{5,4},{6,7},{7,6},{8,9},{9,8},{10,11... | collective-permute-start | bytes 2506760 | tf_op jit(solution)/shard_map/ppermute | solution.py:1135
  186.4 39.1 %collective-permute-start.20 = (bf16[2,384,384]{2,1,0:T(8,128)(2,1)}, bf16[2,384,384]{2,1,0:T(8,128)(2,1)}, u32[]{:S(2)}, u32[]{:S(2)}) collective-permute-start(bf16[2,384,384]{2,1,0:T(8,128)(2,1)} %choose.3.after_ref.mine_ref), channel_id=1, source_target_pairs={{0,4},{4,0},{8,12},{12,8},{16,20},{20,16},{24,28},{28,24},{1,5},{5... | collective-permute-start | bytes 1769480 | tf_op jit(solution)/shard_map/ppermute | solution.py:1135
  189.1 32.5 %collective-permute-start.22 = (bf16[2,384,384]{2,1,0:T(8,128)(2,1)S(1)}, bf16[2,384,384]{2,1,0:T(8,128)(2,1)S(1)}, u32[]{:S(2)}, u32[]{:S(2)}) collective-permute-start(bf16[2,384,384]{2,1,0:T(8,128)(2,1)S(1)} %add.41.after_ref.refs_1_), channel_id=1, source_target_pairs={{8,0},{12,4},{16,24},{20,28},{9,1},{13,5},{17,25},{21,29},{10,2},{... | collective-permute-start | bytes 1769480 | tf_op jit(solution)/shard_map/ppermute | solution.py:1171
  198.4 19.5 %collective-permute-start.21 = (bf16[544,384]{1,0:T(8,128)(2,1)S(1)}, bf16[544,384]{1,0:T(8,128)(2,1)}, u32[]{:S(2)}, u32[]{:S(2)}) collective-permute-start(bf16[544,384]{1,0:T(8,128)(2,1)S(1)} %token_grad.1.after_ref.refs_1_), channel_id=1, source_target_pairs={{0,2},{2,0},{1,3},{3,1},{4,6},{6,4},{5,7},{7,5},{8,10},{10,8},{9,1... | collective-permute-start | bytes 1253384 | tf_op jit(solution)/shard_map/ppermute | solution.py:1135
  206.7 27.5 %collective-permute-start.24 = (bf16[2,384,384]{2,1,0:T(8,128)(2,1)}, bf16[2,384,384]{2,1,0:T(8,128)(2,1)}, u32[]{:S(2)}, u32[]{:S(2)}) collective-permute-start(bf16[2,384,384]{2,1,0:T(8,128)(2,1)} %choose.4.after_ref.mine_ref), channel_id=1, source_target_pairs={{0,4},{4,0},{8,12},{12,8},{16,20},{20,16},{24,28},{28,24},{1,5},{5... | collective-permute-start | bytes 1769480 | tf_op jit(solution)/shard_map/ppermute | solution.py:1135
  209.4 24.8 %all-to-all-start.1 = ((bf16[16,56,384]{2,1,0:T(8,128)(2,1)}), bf16[16,56,384]{2,1,0:T(8,128)(2,1)}, u32[]{:S(2)}, u32[]{:S(2)}) async-start(bf16[16,56,384]{2,1,0:T(8,128)(2,1)} %total.1.after_ref), calls=%async_computation.1 | async-start | bytes 1376256 | tf_op jit(solution)/shard_map/all_to_all | solution.py:1275
  219.0 9.3 %collective-permute-start.23 = (bf16[1088,384]{1,0:T(8,128)(2,1)S(1)}, bf16[1088,384]{1,0:T(8,128)(2,1)S(1)}, u32[]{:S(2)}, u32[]{:S(2)}) collective-permute-start(bf16[1088,384]{1,0:T(8,128)(2,1)S(1)} %weave.1.after_ref.refs_1_), channel_id=1, source_target_pairs={{0,1},{1,0},{2,3},{3,2},{4,5},{5,4},{6,7},{7,6},{8,9},{9,8},{10,11... | collective-permute-start | bytes 2506760 | tf_op jit(solution)/shard_map/ppermute | solution.py:1135
  223.0 18.9 %collective-permute-start.26 = (bf16[2,384,384]{2,1,0:T(8,128)(2,1)}, bf16[2,384,384]{2,1,0:T(8,128)(2,1)}, u32[]{:S(2)}, u32[]{:S(2)}) collective-permute-start(bf16[2,384,384]{2,1,0:T(8,128)(2,1)} %choose.5.after_ref.mine_ref), channel_id=1, source_target_pairs={{0,4},{4,0},{8,12},{12,8},{16,20},{20,16},{24,28},{28,24},{1,5},{5... | collective-permute-start | bytes 1769480 | tf_op jit(solution)/shard_map/ppermute | solution.py:1135
  234.2 2.9 %collective-permute-start.25 = (bf16[896,384]{1,0:T(8,128)(2,1)}, bf16[896,384]{1,0:T(8,128)(2,1)S(1)}, u32[]{:S(2)}, u32[]{:S(2)}) collective-permute-start(bf16[896,384]{1,0:T(8,128)(2,1)} %bitcast.13.refs_1_), channel_id=1, source_target_pairs={{0,1},{1,0},{2,3},{3,2},{4,5},{5,4},{6,7},{7,6},{8,9},{9,8},{10,11... | collective-permute-start | bytes 2064392 | tf_op jit(solution)/shard_map/ppermute | solution.py:1135
  (23 other events, 149.2 us)
Sparse Core Ops, SparseCore 0:
  81.8 90.1 all-reduce.3
